TPU v7x, 256 devices: a whole 4x4x8 slice. The times are simulated.
256 devices in a mesh: filt: 16 (over z_hi, x, core), slab: 16 (over y, z_lo).
Axes of the slice: x: 4, y: 4, z: 8 (z_hi: 2, z_lo: 4; z = z_hi * 4 + z_lo), core: 2. Of those that a mesh axis runs over, the one named last changes fastest.
Arguments:
- inputs: bfloat16 [1024, 16, 1024], P('filt', 'slab'), may hold values from -6 to 6
- weights: bfloat16 [1024, 27, 1024], P('filt', None, 'slab'), may hold values from -0.0390625 to 0.0390625
- bias: bfloat16 [1024], P('filt'), may hold values from -3 to 3
- cotangent: bfloat16 [1024, 16, 1024], P('filt', 'slab'), may hold values from -6 to 6
Outputs:
- activated: bfloat16 [1024, 16, 1024], P('filt', 'slab')
- input_grad: bfloat16 [1024, 16, 1024], P('filt', 'slab')
All inputs are finite; a program needn't handle non-finite values.
Results may differ from a plain program's by a relative error of at most 0.019.
Values may be sent and summed in bfloat16 or wider, within the bound.
No kernel may reach another device: no remote copies, remote signals or barrier semaphores. Data moves between devices by JAX's collectives and lax.ppermute only.
A program may use at most 256 MiB of HBM per device.

v0:
```python
import jax
import jax.numpy as jnp
from jax import lax
from jax.sharding import PartitionSpec as P

HH = 32
WW = 32


tap_shifts = [(a - 1, b - 1, c - 1) for a in range(3) for b in range(3) for c in range(3)]


def with_halo(x, sides, width):
    for axis, dim in sides:
        count, length = (lax.axis_size(axis), x.shape[dim])
        up = [(i, (i + 1) % count) for i in range(count - 1)]
        down = [(j, i) for i, j in up]
        last = lax.slice_in_dim(x, length - width, length, axis=dim)
        leading = lax.slice_in_dim(x, 0, width, axis=dim)
        before = lax.ppermute(last, axis, up)
        after = lax.ppermute(leading, axis, down)
        x = jnp.concatenate([before, x, after], axis=dim)
    return x


def padded_volume(block):
    volume = block.reshape(block.shape[0], block.shape[1], HH, WW)
    return jnp.pad(volume, ((0, 0), (0, 0), (1, 1), (1, 1)))


def tap_block(padded, step_depth, step_row, step_col, planes):
    window = padded[
        :,
        1 + step_depth : 1 + step_depth + planes,
        1 + step_row : 1 + step_row + HH,
        1 + step_col : 1 + step_col + WW,
    ]
    return window.reshape(padded.shape[0], planes * HH * WW)


def stacked_taps(padded, factor, planes):
    blocks = []
    for shift_set in tap_shifts:
        blocks.append(
            tap_block(
                padded, factor * shift_set[0], factor * shift_set[1], factor * shift_set[2], planes
            )
        )
    return jnp.concatenate(blocks, axis=0)


def silu_slope(value):
    sig = jax.nn.sigmoid(value)
    return sig * (1.0 + value * (1.0 - sig))


def local(inputs, weights, bias, cotangent):
    planes = inputs.shape[1]
    filters = weights.shape[0]
    full_weights = lax.all_gather(weights, "slab", axis=2, tiled=True)
    extended = with_halo(inputs, (("slab", 1),), 1)
    portion = lax.all_gather(extended, "filt", axis=0, tiled=True)
    count = portion.shape[0]
    weight_part = full_weights
    matrix = weight_part.reshape(filters, len(tap_shifts) * count)
    stacked = stacked_taps(padded_volume(portion), 1, planes)
    preact = jnp.dot(matrix, stacked, preferred_element_type=jnp.float32)
    preact = preact + bias.astype(jnp.float32)[:, None]
    activated = jax.nn.silu(preact).astype(jnp.bfloat16).reshape(cotangent.shape)
    grad_pre = (cotangent.reshape(preact.shape).astype(jnp.float32) * silu_slope(preact)).astype(
        jnp.bfloat16
    )
    grad_extended = with_halo(grad_pre.reshape(cotangent.shape), (("slab", 1),), 1)
    stacked_grad = stacked_taps(padded_volume(grad_extended), -1, planes)
    amount = lax.axis_size("filt") * inputs.shape[0]
    weight_part = full_weights
    matrix = jnp.transpose(weight_part, (2, 1, 0)).reshape(amount, len(tap_shifts) * filters)
    total = jnp.dot(matrix, stacked_grad, preferred_element_type=jnp.float32)
    input_grad = lax.psum_scatter(
        total.reshape(amount, planes, HH * WW).astype(jnp.bfloat16),
        "filt",
        scatter_dimension=0,
        tiled=True,
    )
    return (activated, input_grad)


def solution(mesh):
    return jax.shard_map(
        local,
        mesh=mesh,
        in_specs=(
            P("filt", "slab", None),
            P("filt", None, "slab"),
            P("filt"),
            P("filt", "slab", None),
        ),
        out_specs=(P("filt", "slab", None), P("filt", "slab", None)),
        check_vma=False,
    )
```

profile of v0, /device:TPU:8, one launch (start us, length us, event | category | flops | bytes accessed | tf_op | source)
XLA Modules:
  0.0 623.4 jit_solution(13348431824785942233)
XLA Ops:
  7.2 2.5 copy.71
  9.8 3.8 collective-permute-start
  13.6 4.7 collective-permute-start.1
  20.0 2.8 collective-permute-done.1
  25.3 173.1 %all-gather.5.cloned.1.call-done = bf16[64,27,1024]{0,1,2:T(8,128)(2,1)} async-done(((bf16[64,27,64]{0,1,2:T(8,128)(2,1)}), bf16[64,27,1024]{0,1,2:T(8,128)(2,1)}) %all-gather.5.cloned.1.call-update) | async-done | bytes 3538960 | tf_op jit(solution)/shard_map/all_gather | solution.py:60
  198.4 12.0 %copy.72 = bf16[64,27,1024]{2,1,0:T(8,128)(2,1)} copy(bf16[64,27,1024]{0,1,2:T(8,128)(2,1)} %all-gather.5.cloned.1.call-done) | data formatting | bytes 7077888 | tf_op jit(solution)/shard_map/all_gather | solution.py:60
  210.4 4.4 copy.106
  214.9 79.3 %all-gather.3.cloned.1.call-done = bf16[1024,3,1024]{2,0,1:T(8,128)(2,1)} async-done(((bf16[64,3,1024]{2,0,1:T(8,128)(2,1)}), bf16[1024,3,1024]{2,0,1:T(8,128)(2,1)}) %all-gather.3.cloned.1.call-update) | async-done | bytes 6291472 | tf_op jit(solution)/shard_map/all_gather | solution.py:62
  294.2 8.6 %copy.70 = bf16[1024,3,1024]{0,2,1:T(8,128)(2,1)} copy(bf16[1024,3,1024]{2,0,1:T(8,128)(2,1)} %all-gather.3.cloned.1.call-done) | data formatting | bytes 12582912 | tf_op jit(solution)/shard_map/all_gather | solution.py:62
  302.8 29.1 %pad_slice_fusion = (bf16[1024,1,32,32]{0,3,2,1:T(8,128)(2,1)}, bf16[1024,1,32,32]{0,3,2,1:T(8,128)(2,1)}, bf16[1024,1,32,32]{0,3,2,1:T(8,128)(2,1)}, bf16[1024,...) fusion(bf16[1024,3,32,32]{0,3,2,1:T(8,128)(2,1)} %bitcast.86), kind=kLoop, calls=%fused_computation | loop fusion | bytes 46137344 | tf_op jit(solution)/shard_map/slice | solution.py:32
  331.9 6.9 %pad_slice_fusion.1 = (bf16[1024,1,32,32]{0,3,2,1:T(8,128)(2,1)S(1)}, bf16[1024,1,32,32]{0,3,2,1:T(8,128)(2,1)}, bf16[1024,1,32,32]{0,3,2,1:T(8,128)(2,1)S(1)}, ...) fusion(bf16[1024,3,32,32]{0,3,2,1:T(8,128)(2,1)S(1)} %bitcast.87), kind=kLoop, calls=%fused_computation.1 | loop fusion | bytes 29360128 | tf_op jit(solution)/shard_map/slice | solution.py:32
  338.8 3.3 constant_dynamic-update-slice_fusion.26
  382.7 25.4 %fusion.7 = (bf16[64,1024]{1,0:T(8,128)(2,1)}, bf16[64,1,1024]{2,0,1:T(8,128)(2,1)}) fusion(bf16[64,1,1024]{2,0,1:T(8,128)(2,1)S(1)} %copy-done.24, f32[64]{0:T(128)S(1)} %convert_element_type.28, bf16[27648,1024]{0,1:T(8,128)(2,1)} %constant_dynamic-update-slice_fusion, bf16[64,27648]{1,0:T(8,128)(2,1)S(1)} %bitcast.89), kind=kOutput, calls=%fused_computation.41 | convolution fusion | flops 3624730624 | bytes 60555520 | tf_op jit(solution)/shard_map/dot_general | solution.py:67
  408.1 2.5 collective-permute-start.2
  410.7 6.0 collective-permute-start.3
  416.7 10.0 %copy.100 = bf16[64,27,1024]{2,0,1:T(8,128)(2,1)S(1)} copy(bf16[64,27,1024]{0,1,2:T(8,128)(2,1)} %all-gather.5.cloned.1.call-done) | data formatting | bytes 7077888 | tf_op jit(solution)/shard_map/all_gather | solution.py:60
  426.7 1.7 copy.74
  428.4 1.8 copy.73
  430.2 1.8 copy.75
  434.7 2.5 fusion.9
  492.0 1.8 copy.95
  521.0 7.3 %convert_bitcast_fusion = bf16[1024,1024]{0,1:T(8,128)(2,1)} fusion(bf16[1728,1024]{1,0:T(8,128)(2,1)} %constant_dynamic-update-slice_fusion.27, bf16[1024,1728]{0,1:T(8,128)(2,1)S(1)} %bitcast.117), kind=kOutput, calls=%fused_computation.28 | convolution fusion | flops 3624927232 | bytes 9175040 | tf_op jit(solution)/shard_map/dot_general | solution.py:78
  528.3 4.0 copy.104
  532.3 82.7 %reduce-scatter.4.cloned.1.call-done = bf16[64,1024]{1,0:T(8,128)(2,1)} async-done(((bf16[1024,1024]{1,0:T(8,128)(2,1)}), bf16[64,1024]{1,0:T(8,128)(2,1)}) %reduce-scatter.4.cloned.1.call-update) | async-done | bytes 131088
  (141 shorter events, 131.5 us)
Async XLA Ops:
  7.2 191.2 %all-gather.5.cloned.1.call-start = ((), (), s32[]{:S(2)}) async-start(), calls=%async_computation.2 | async-start | bytes 8912896 | tf_op jit(solution)/shard_map/all_gather | solution.py:60
  9.8 284.5 %all-gather.3.cloned.1.call-start = ((), (), s32[]{:S(2)}) async-start(), calls=%async_computation.1 | async-start | bytes 6684672 | tf_op jit(solution)/shard_map/all_gather | solution.py:62
  9.8 10.2 %collective-permute-start = (bf16[64,1,1024]{2,0,1:T(8,128)(2,1)}, bf16[64,1,1024]{2,0,1:T(8,128)(2,1)S(1)}, u32[]{:S(2)}, u32[]{:S(2)}) collective-permute-start(bf16[64,1,1024]{2,0,1:T(8,128)(2,1)} %param.4), channel_id=1, source_target_pairs={{0,1},{1,2},{2,3},{3,4},{4,5},{5,6},{6,7},{7,8},{8,9},{9,10},{10,1... | collective-permute-start | bytes 393224 | tf_op jit(solution)/shard_map/ppermute | solution.py:20
  13.6 9.2 %collective-permute-start.1 = (bf16[64,1,1024]{2,0,1:T(8,128)(2,1)}, bf16[64,1,1024]{2,0,1:T(8,128)(2,1)S(1)}, u32[]{:S(2)}, u32[]{:S(2)}) collective-permute-start(bf16[64,1,1024]{2,0,1:T(8,128)(2,1)} %param.4), channel_id=1, source_target_pairs={{1,0},{2,1},{3,2},{4,3},{5,4},{6,5},{7,6},{8,7},{9,8},{10,9},{11,1... | collective-permute-start | bytes 393224 | tf_op jit(solution)/shard_map/ppermute | solution.py:21
  24.6 590.4 %reduce-scatter.4.cloned.1.call-start = ((), (), s32[]{:S(2)}) async-start(), calls=%async_computation.3 | async-start | bytes 2228224
  302.8 29.1 %copy-start = (bf16[1024,3,1024]{0,2,1:T(8,128)(2,1)S(1)}, bf16[1024,3,1024]{0,2,1:T(8,128)(2,1)}, u32[]{:S(2)}) copy-start(bf16[1024,3,1024]{0,2,1:T(8,128)(2,1)} %copy.70) | copy-start | bytes 18874372
  338.8 3.3 copy-start.23
  338.8 4.8 copy-start.22
  345.2 3.2 copy-start.20
  346.7 3.1 copy-start.19
  351.4 3.1 copy-start.16
  352.9 3.1 copy-start.15
  354.5 3.1 copy-start.14
  357.6 3.1 copy-start.3
  359.2 3.2 copy-start.12
  360.7 3.2 copy-start.11
  362.3 3.2 copy-start.10
  367.0 3.1 copy-start.7
  368.6 3.2 copy-start.6
  370.2 3.2 copy-start.2
  371.7 3.2 copy-start.1
  378.1 3.1 copy-start.5
  408.1 20.3 %collective-permute-start.2 = (bf16[64,1,1024]{2,0,1:T(8,128)(2,1)}, bf16[64,1,1024]{2,0,1:T(8,128)(2,1)}, u32[]{:S(2)}, u32[]{:S(2)}) collective-permute-start(bf16[64,1,1024]{2,0,1:T(8,128)(2,1)} %bitcast.31), channel_id=1, source_target_pairs={{0,1},{1,2},{2,3},{3,4},{4,5},{5,6},{6,7},{7,8},{8,9},{9,10},{10,1... | collective-permute-start | bytes 393224 | tf_op jit(solution)/shard_map/ppermute | solution.py:20
  410.7 19.5 %collective-permute-start.3 = (bf16[64,1,1024]{2,0,1:T(8,128)(2,1)}, bf16[64,1,1024]{2,0,1:T(8,128)(2,1)}, u32[]{:S(2)}, u32[]{:S(2)}) collective-permute-start(bf16[64,1,1024]{2,0,1:T(8,128)(2,1)} %bitcast.31), channel_id=1, source_target_pairs={{1,0},{2,1},{3,2},{4,3},{5,4},{6,5},{7,6},{8,7},{9,8},{10,9},{11,1... | collective-permute-start | bytes 393224 | tf_op jit(solution)/shard_map/ppermute | solution.py:21
  (8 other events, 24.6 us)
Sparse Core Ops, SparseCore 0:
  9.9 188.4 all-gather.4
  201.2 93.0 all-gather.2
  532.4 82.5 reduce-scatter.3
where the time goes:
time: 626 us; the launch traced here: 623 us
  waiting for transfers between devices  340 us (54%)
  local copies, waits for them, and re-layouts  216 us (35%)
  matrix products  32.7 us (5%)
  starting transfers between devices  17.2 us (3%)
  between operations  13.9 us (2%)
    all_gather x1, waiting for transfers between devices, local(): full_weights = lax.all_gather(weights, 'slab', axis=2, tiled=True)  173 us
    unnamed x107, local copies, waits for them, and re-layouts  95.8 us
    unnamed x4, waiting for transfers between devices  82.8 us
    all_gather x1, waiting for transfers between devices, local(): portion = lax.all_gather(extended, 'filt', axis=0, tiled=True)  79.3 us
    reshape x24, local copies, waits for them, and re-layouts, tap_block(): return window.reshape(padded.shape[0], planes * HH * WW)  41.5 us
    slice x4, local copies, waits for them, and re-layouts, tap_block(): padded[:, 1 + step_depth:1 + step_depth + planes, 1 + step_row:1 + step_r...  39.7 us
    dot_general x1, matrix products, local(): preact = jnp.dot(matrix, stacked, preferred_element_type=jnp.float32)  25.4 us
    all_gather x2, local copies, waits for them, and re-layouts, local(): full_weights = lax.all_gather(weights, 'slab', axis=2, tiled=True)  22 us
  transfers between devices with their start and end apart: 7, of which 5 were waited for; matrix products, arithmetic and copies ran while one was open for 5% of the time, Pallas kernels for 0%

commit v1 on v0

v1 whole, which is shorter than its diff:
```python
import functools

import jax
import jax.numpy as jnp
from jax import lax
from jax.experimental import pallas as pl
from jax.experimental.pallas import tpu as pltpu
from jax.sharding import PartitionSpec as P

HH = 32
WW = 32
CELLS = HH * WW
TAPS = 27
SLOTS = 28
BLOCK = 64
COLS = SLOTS * BLOCK
HALF = COLS // 2
BLOCKS = 16
CHANNELS = BLOCKS * BLOCK

ZH, XN, CN = 2, 4, 2
YN, ZN = 4, 4

BF16 = jnp.bfloat16
F32 = jnp.float32
LIMIT = pltpu.CompilerParams(vmem_limit_bytes=48 * 1024 * 1024)


def filt_index(zh, x, c):
    return (zh * XN + x) * CN + c


FILT = [(zh, x, c) for zh in range(ZH) for x in range(XN) for c in range(CN)]
SLAB = [(y, z) for y in range(YN) for z in range(ZN)]
TO_CORE = [(filt_index(*d), filt_index(d[0], d[1], 1 - d[2])) for d in FILT]
TO_ZHI = [(filt_index(*d), filt_index(1 - d[0], d[1], d[2])) for d in FILT]


def to_x(k):
    return [(filt_index(*d), filt_index(d[0], (d[1] + k) % XN, d[2])) for d in FILT]


def to_y(k):
    return [(y * ZN + z, ((y + k) % YN) * ZN + z) for y, z in SLAB]


def to_z(k):
    return [(y * ZN + z, y * ZN + (z + k) % ZN) for y, z in SLAB]


UP = [(i, i + 1) for i in range(YN * ZN - 1)]
DOWN = [(i + 1, i) for i in range(YN * ZN - 1)]

VMEM = pl.BlockSpec(memory_space=pltpu.VMEM)
ANY = pl.BlockSpec(memory_space=pl.ANY)


def transpose_kernel(w_ref, out_ref):
    rows = TAPS * BLOCK
    for start in range(0, rows, 128):
        size = min(128, rows - start)
        part = w_ref[start : start + size, :].astype(F32)
        if size < 128:
            part = jnp.concatenate([part, jnp.zeros((128 - size, BLOCK), F32)], axis=0)
        out_ref[:, start : start + 128] = part.T.astype(BF16)


def filt_position():
    mine = lax.axis_index("filt")
    return mine // (XN * CN), (mine // CN) % XN, mine % CN


def slab_position():
    mine = lax.axis_index("slab")
    return mine // ZN, mine % ZN


def weight_copies(refs, scratch, sem, place):
    y, z = slab_position()
    copies = []
    for step_y in range(YN):
        for step_z in range(ZN):
            block = ((y + YN - step_y) % YN) * ZN + (z + ZN - step_z) % ZN
            row = pl.multiple_of(place(block) * BLOCK, BLOCK)
            for half in range(2):
                copies.append(
                    pltpu.make_async_copy(
                        refs[2 * step_y + half].at[pl.ds(step_z * BLOCK, BLOCK), :],
                        scratch.at[pl.ds(row, BLOCK), pl.ds(half * HALF, HALF)],
                        sem.at[len(copies)],
                    )
                )
    return copies


def forward_kernel(*refs):
    x_refs, w_refs = refs[:8], refs[8:16]
    own_ref, down_ref, up_ref = refs[16:19]
    x_scr, w_scr, y_scr, x_sem, w_sem = refs[19:]
    zh, x, c = filt_position()
    copies = []
    for step in range(XN):
        for other in range(CN):
            for far in range(ZH):
                core = c if other == 0 else 1 - c
                high = zh if far == 0 else 1 - zh
                block = filt_index(high, (x + XN - step) % XN, core)
                row = pl.multiple_of(block * BLOCK, BLOCK)
                copies.append(
                    pltpu.make_async_copy(
                        x_refs[2 * step + other].at[pl.ds(far * BLOCK, BLOCK), :],
                        x_scr.at[pl.ds(row, BLOCK), :],
                        x_sem.at[len(copies)],
                    )
                )
    copies += weight_copies(w_refs, w_scr, w_sem, lambda block: block)
    for copy in copies:
        copy.start()
    for copy in copies:
        copy.wait()
    for half in range(2):
        y_scr[half * HALF : (half + 1) * HALF, :] = lax.dot_general(
            w_scr[:, half * HALF : (half + 1) * HALF],
            x_scr[...],
            (((0,), (0,)), ((), ())),
            preferred_element_type=F32,
        )
    cell = lax.broadcasted_iota(jnp.int32, (8, CELLS), 1)
    column = cell % WW
    row_ok = {0: cell >= WW, 2: cell < CELLS - WW}
    col_ok = {0: column >= 1, 2: column < WW - 1}

    def body(part, carry):
        base = pl.multiple_of(part * 8, 8)
        for a, out in ((0, up_ref), (1, own_ref), (2, down_ref)):
            total = None
            for col in range(3):
                lane = None
                for row in range(3):
                    tap = 9 * a + 3 * row + col
                    value = y_scr[pl.ds(tap * BLOCK + base, 8), :]
                    if row != 1:
                        value = pltpu.roll(value, ((1 - row) * WW) % CELLS, 1)
                        value = jnp.where(row_ok[row], value, 0.0)
                    lane = value if lane is None else lane + value
                if col != 1:
                    lane = pltpu.roll(lane, (1 - col) % CELLS, 1)
                    lane = jnp.where(col_ok[col], lane, 0.0)
                total = lane if total is None else total + lane
            out[pl.ds(base, 8), :] = total.astype(out.dtype)
        return carry

    lax.fori_loop(0, BLOCK // 8, body, 0)


def pointwise_kernel(own_ref, below_ref, above_ref, bias_ref, cot_ref, act_ref, grad_ref):
    preact = (
        own_ref[...]
        + below_ref[...].astype(F32)
        + above_ref[...].astype(F32)
        + bias_ref[...].astype(F32)
    )
    sig = jax.nn.sigmoid(preact)
    act_ref[...] = (preact * sig).astype(BF16)
    slope = sig * (1.0 + preact * (1.0 - sig))
    grad_ref[...] = (cot_ref[...].astype(F32) * slope).astype(BF16)


def backward_kernel(*refs):
    grad_refs, w_refs = refs[:3], refs[3:11]
    mine_ref, other_ref = refs[11:13]
    w_scr, g_scr, w_sem = refs[13:]
    zh, x, c = filt_position()

    def place(block):
        high, at, core = block // (XN * CN), (block // CN) % XN, block % CN
        return ((core + c) % CN * XN + (at + XN - x) % XN) * ZH + (high + zh) % ZH

    copies = weight_copies(w_refs, w_scr, w_sem, place)
    for copy in copies:
        copy.start()
    cell = lax.broadcasted_iota(jnp.int32, (16, CELLS), 1)
    column = cell % WW
    row_ok = {2: cell >= WW, 0: cell < CELLS - WW}
    col_ok = {2: column >= 1, 0: column < WW - 1}

    def body(part, carry):
        base = pl.multiple_of(part * 16, 16)
        for a, grad in enumerate(grad_refs):
            plane = grad[pl.ds(base, 16), :].astype(F32)
            for col in range(3):
                lane = plane
                if col != 1:
                    lane = pltpu.roll(lane, (col - 1) % CELLS, 1)
                    lane = jnp.where(col_ok[col], lane, 0.0)
                for row in range(3):
                    value = lane
                    if row != 1:
                        value = pltpu.roll(value, ((row - 1) * WW) % CELLS, 1)
                        value = jnp.where(row_ok[row], value, 0.0)
                    tap = 9 * a + 3 * row + col
                    g_scr[pl.ds(tap * BLOCK + base, 16), :] = value.astype(BF16)
        return carry

    lax.fori_loop(0, BLOCK // 16, body, 0)
    g_scr[TAPS * BLOCK :, :] = jnp.zeros((COLS - TAPS * BLOCK, CELLS), BF16)
    for copy in copies:
        copy.wait()
    half = CHANNELS // 2
    for at, out in ((half, other_ref), (0, mine_ref)):
        out[...] = jnp.dot(
            w_scr[at : at + half, :], g_scr[...], preferred_element_type=F32
        ).astype(BF16)


def shape(rows, columns, dtype=BF16):
    return jax.ShapeDtypeStruct((rows, columns), dtype)


def gather_weights(weights):
    taps_first = jnp.transpose(weights, (1, 0, 2)).reshape(TAPS * BLOCK, BLOCK)
    own = pl.pallas_call(
        transpose_kernel,
        out_shape=shape(BLOCK, COLS),
        in_specs=[VMEM],
        out_specs=VMEM,
        compiler_params=LIMIT,
        name="weights_transpose",
    )(taps_first)
    blocks = [own] + [lax.ppermute(own, "slab", to_z(k)) for k in range(1, ZN)]
    left = jnp.concatenate([block[:, :HALF] for block in blocks], axis=0)
    right = jnp.concatenate([block[:, HALF:] for block in blocks], axis=0)
    left_1 = lax.ppermute(left, "slab", to_y(1))
    right_3 = lax.ppermute(right, "slab", to_y(-1))
    left_3 = lax.ppermute(left, "slab", to_y(-1))
    right_1 = lax.ppermute(right, "slab", to_y(1))
    left_2 = lax.ppermute(left_1, "slab", to_y(1))
    right_2 = lax.ppermute(right_3, "slab", to_y(-1))
    return [left, right, left_1, right_1, left_2, right_2, left_3, right_3]


def gather_inputs(inputs):
    far = lax.ppermute(inputs, "filt", TO_ZHI)
    pair = jnp.concatenate([inputs, far], axis=0)
    pieces = [pair] + [lax.ppermute(pair, "filt", to_x(k)) for k in (1, 2, -1)]
    out = []
    for piece in pieces:
        out += [piece, lax.ppermute(piece, "filt", TO_CORE)]
    return out


def local(inputs, weights, bias, cotangent):
    pieces = gather_inputs(inputs.reshape(BLOCK, CELLS))
    parts = gather_weights(weights)
    own, down, up = pl.pallas_call(
        forward_kernel,
        out_shape=(shape(BLOCK, CELLS, F32), shape(BLOCK, CELLS), shape(BLOCK, CELLS)),
        in_specs=[ANY] * 16,
        out_specs=(VMEM,) * 3,
        scratch_shapes=[
            pltpu.VMEM((CHANNELS, CELLS), BF16),
            pltpu.VMEM((CHANNELS, COLS), BF16),
            pltpu.VMEM((COLS, CELLS), F32),
            pltpu.SemaphoreType.DMA((16,)),
            pltpu.SemaphoreType.DMA((32,)),
        ],
        compiler_params=LIMIT,
        cost_estimate=pl.CostEstimate(
            flops=2 * COLS * CHANNELS * CELLS, bytes_accessed=6 * 2**20, transcendentals=0
        ),
        name="conv_forward",
    )(*pieces, *parts)
    below = lax.ppermute(up, "slab", UP)
    above = lax.ppermute(down, "slab", DOWN)
    activated, grad = pl.pallas_call(
        pointwise_kernel,
        out_shape=(shape(BLOCK, CELLS), shape(BLOCK, CELLS)),
        in_specs=[VMEM] * 5,
        out_specs=(VMEM,) * 2,
        compiler_params=LIMIT,
        name="silu_and_slope",
    )(own, below, above, bias.reshape(BLOCK, 1), cotangent.reshape(BLOCK, CELLS))
    grad_below = lax.ppermute(grad, "slab", UP)
    grad_above = lax.ppermute(grad, "slab", DOWN)
    mine, other = pl.pallas_call(
        backward_kernel,
        out_shape=(shape(CHANNELS // 2, CELLS), shape(CHANNELS // 2, CELLS)),
        in_specs=[VMEM] * 3 + [ANY] * 8,
        out_specs=(VMEM,) * 2,
        scratch_shapes=[
            pltpu.VMEM((CHANNELS, COLS), BF16),
            pltpu.VMEM((COLS, CELLS), BF16),
            pltpu.SemaphoreType.DMA((32,)),
        ],
        compiler_params=LIMIT,
        cost_estimate=pl.CostEstimate(
            flops=2 * COLS * CHANNELS * CELLS, bytes_accessed=6 * 2**20, transcendentals=0
        ),
        name="conv_backward",
    )(grad_above, grad, grad_below, *parts)
    received = lax.ppermute(other, "filt", TO_CORE)
    sums = []
    for k in range(XN):
        rows = slice(k * 2 * BLOCK, (k + 1) * 2 * BLOCK)
        sums.append((mine[rows].astype(F32) + received[rows].astype(F32)).astype(BF16))
    total = sums[0].astype(F32)
    for k in (1, 2, 3):
        total = total + lax.ppermute(sums[k], "filt", to_x(k)).astype(F32)
    far = lax.ppermute(total[BLOCK:].astype(BF16), "filt", TO_ZHI)
    input_grad = (total[:BLOCK] + far.astype(F32)).astype(BF16)
    return activated.reshape(cotangent.shape), input_grad.reshape(inputs.shape)


def solution(mesh):
    return jax.shard_map(
        local,
        mesh=mesh,
        in_specs=(
            P("filt", "slab", None),
            P("filt", None, "slab"),
            P("filt"),
            P("filt", "slab", None),
        ),
        out_specs=(P("filt", "slab", None), P("filt", "slab", None)),
        check_vma=False,
    )
```

time: 626 us -> 158 us (0.25)
  waiting for transfers between devices: 340 us -> 78 us
  local copies, waits for them, and re-layouts: 216 us -> 3.93 us
  starting transfers between devices: 17.2 us -> 50.5 us
  matrix products: 32.7 us -> 0 us
  Pallas kernels: 0 us -> 21.6 us
  between operations: 13.9 us -> 0.84 us
    all_gather x2 -> x0, waiting for transfers between devices: 252 us -> none  [the longest x1 173 us: local(): full_weights = lax.all_gather(weights, 'slab', axis=2, tiled=True)]
    unnamed x107 -> x18, local copies, waits for them, and re-layouts: 95.8 us -> 3.07 us
    unnamed x4 -> x0, waiting for transfers between devices: 82.8 us -> none
    ppermute x4 -> x26, waiting for transfers between devices: 4.49 us -> 78 us  [the longest x1 17.6 us: gather_inputs(): far = lax.ppermute(inputs, 'filt', TO_ZHI)]
    reshape x24 -> x1, local copies, waits for them, and re-layouts: 41.5 us -> 0.76 us  [local(): bias.reshape(BLOCK, 1)]
    slice x4 -> x5, local copies, waits for them, and re-layouts: 39.7 us -> 0.09 us  [the longest x4 0.08 us: gather_weights(): right = jnp.concatenate([block[:, HALF:] for block in blocks], axis=0)]
    ppermute x4 -> x26, starting transfers between devices: 17.1 us -> 50.5 us  [the longest x1 6.62 us: local(): above = lax.ppermute(down, 'slab', DOWN)]
    dot_general x2 -> x0, matrix products: 32.7 us -> none  [the longest x1 25.4 us: local(): preact = jnp.dot(matrix, stacked, preferred_element_type=jnp.float32)]
  transfers between devices with their start and end apart: 7 -> 26, of which waited for: 5 -> 17; matrix products, arithmetic and copies ran while one was open for 5% -> 1% of each run, Pallas kernels for 0% -> 0%
where the time goes in v1:
time: 158 us; the launch traced here: 156 us
  waiting for transfers between devices  78 us (49%)
  starting transfers between devices  50.5 us (32%)
  Pallas kernels  21.6 us (14%)
  local copies, waits for them, and re-layouts  3.93 us (2%)
    ppermute x1, waiting for transfers between devices, gather_inputs(): far = lax.ppermute(inputs, 'filt', TO_ZHI)  17.6 us
    ppermute x3, waiting for transfers between devices, local(): total = total + lax.ppermute(sums[k], 'filt', to_x(k)).astype(F32)  14.1 us
    pallas_call x1, Pallas kernels, local(): pl.pallas_call(forward_kernel, out_shape=(shape(BLOCK, CELLS, F32), shape...  13.2 us
    ppermute x3, waiting for transfers between devices, gather_inputs(): pieces = [pair] + [lax.ppermute(pair, 'filt', to_x(k)) for k in (1, 2, -1)]  9.87 us
    pallas_call x1, Pallas kernels, local(): pl.pallas_call(backward_kernel, out_shape=(shape(CHANNELS // 2, CELLS), s...  7.41 us
    ppermute x1, waiting for transfers between devices, local(): grad_below = lax.ppermute(grad, 'slab', UP)  7.05 us
    ppermute x1, waiting for transfers between devices, gather_weights(): right_1 = lax.ppermute(right, 'slab', to_y(1))  6.84 us
    ppermute x1, starting transfers between devices, local(): above = lax.ppermute(down, 'slab', DOWN)  6.62 us
  transfers between devices with their start and end apart: 26, of which 17 were waited for; matrix products, arithmetic and copies ran while one was open for 1% of the time, Pallas kernels for 0%

profile of v1, /device:TPU:8, one launch (start us, length us, event | category | flops | bytes accessed | tf_op | source)
XLA Modules:
  0.0 156.2 jit_solution(13059365175859082598)
XLA Ops:
  1.8 4.7 %collective-permute-start.10 = (bf16[64,1792]{1,0:T(8,128)(2,1)S(1)}, bf16[64,1792]{1,0:T(8,128)(2,1)S(1)}, u32[]{:S(2)}, u32[]{:S(2)}) collective-permute-start(bf16[64,1792]{1,0:T(8,128)(2,1)S(1)} %weights_transpose.1), channel_id=1, source_target_pairs={{0,3},{1,0},{2,1},{3,2},{4,7},{5,4},{6,5},{7,6},{8,11},{9,8},{10,9... | collective-permute-start | bytes 688136 | tf_op jit(solution)/shard_map/ppermute | solution.py:230
  7.2 5.4 %collective-permute-start = (bf16[64,1024]{1,0:T(8,128)(2,1)S(1)}, bf16[64,1024]{1,0:T(8,128)(2,1)S(1)}, u32[]{:S(2)}, u32[]{:S(2)}) collective-permute-start(bf16[64,1024]{1,0:T(8,128)(2,1)S(1)} %bitcast.11), channel_id=1, source_target_pairs={{0,128},{16,144},{32,160},{48,176},{64,192},{80,208},{96,224},{112... | collective-permute-start | bytes 393224 | tf_op jit(solution)/shard_map/ppermute | solution.py:243
  12.6 17.6 %collective-permute-done = bf16[64,1024]{1,0:T(8,128)(2,1)S(1)} collective-permute-done((bf16[64,1024]{1,0:T(8,128)(2,1)S(1)}, bf16[64,1024]{1,0:T(8,128)(2,1)S(1)}, u32[]{:S(2)}, u32[]{:S(2)}) %collective-permute-start) | collective-permute-done | bytes 131104 | tf_op jit(solution)/shard_map/ppermute | solution.py:243
  32.1 1.7 %collective-permute-start.11 = (bf16[256,896]{1,0:T(8,128)(2,1)S(1)}, bf16[256,896]{1,0:T(8,128)(2,1)S(1)}, u32[]{:S(2)}, u32[]{:S(2)}) collective-permute-start(bf16[256,896]{1,0:T(8,128)(2,1)S(1)} %pad_maximum_fusion.refs_8_.refs_3_), channel_id=1, source_target_pairs={{0,4},{1,5},{2,6},{3,7},{4,8},{5,9},{6,10},{7,11},{8,12},{9,13},{1... | collective-permute-start | bytes 1376264 | tf_op jit(solution)/shard_map/ppermute | solution.py:233
  34.4 2.7 %collective-permute-start.4 = (bf16[128,1024]{1,0:T(8,128)(2,1)S(1)}, bf16[128,1024]{1,0:T(8,128)(2,1)S(1)}, u32[]{:S(2)}, u32[]{:S(2)}) collective-permute-start(bf16[128,1024]{1,0:T(8,128)(2,1)S(1)} %pad_maximum_fusion.2.refs_0_), channel_id=1, source_target_pairs={{0,64},{16,80},{32,96},{48,112},{64,0},{80,16},{96,32},{112,48},{1... | collective-permute-start | bytes 786440 | tf_op jit(solution)/shard_map/ppermute | solution.py:245
  38.5 1.8 %collective-permute-done.2.refs_2_ = bf16[128,1024]{1,0:T(8,128)(2,1)S(1)} collective-permute-done((bf16[128,1024]{1,0:T(8,128)(2,1)S(1)}, bf16[128,1024]{1,0:T(8,128)(2,1)S(1)}, u32[]{:S(2)}, u32[]{:S(2)}) %collective-permute-start.2) | collective-permute-done | bytes 262176 | tf_op jit(solution)/shard_map/ppermute | solution.py:245
  40.3 6.6 %collective-permute-done.4.refs_4_ = bf16[128,1024]{1,0:T(8,128)(2,1)S(1)} collective-permute-done((bf16[128,1024]{1,0:T(8,128)(2,1)S(1)}, bf16[128,1024]{1,0:T(8,128)(2,1)S(1)}, u32[]{:S(2)}, u32[]{:S(2)}) %collective-permute-start.4) | collective-permute-done | bytes 262176 | tf_op jit(solution)/shard_map/ppermute | solution.py:245
  50.4 1.6 %collective-permute-start.13 = (bf16[256,896]{1,0:T(8,128)(2,1)S(1)}, bf16[256,896]{1,0:T(8,128)(2,1)S(1)}, u32[]{:S(2)}, u32[]{:S(2)}) collective-permute-start(bf16[256,896]{1,0:T(8,128)(2,1)S(1)} %collective-permute-done.11.refs_10_.refs_5_), channel_id=1, source_target_pairs={{0,4},{1,5},{2,6},{3,7},{4,8},{5,9},{6,10},{7,11},{8,12},{9,13},{1... | collective-permute-start | bytes 1376264 | tf_op jit(solution)/shard_map/ppermute | solution.py:237
  55.0 6.8 %collective-permute-done.12.refs_11_.refs_6_ = bf16[256,896]{1,0:T(8,128)(2,1)S(1)} collective-permute-done((bf16[256,896]{1,0:T(8,128)(2,1)S(1)}, bf16[256,896]{1,0:T(8,128)(2,1)S(1)}, u32[]{:S(2)}, u32[]{:S(2)}) %collective-permute-start.12) | collective-permute-done | bytes 458784 | tf_op jit(solution)/shard_map/ppermute | solution.py:236
  61.9 1.6 %collective-permute-done.16.refs_14_.refs_9_ = bf16[256,896]{1,0:T(8,128)(2,1)S(1)} collective-permute-done((bf16[256,896]{1,0:T(8,128)(2,1)S(1)}, bf16[256,896]{1,0:T(8,128)(2,1)S(1)}, u32[]{:S(2)}, u32[]{:S(2)}) %collective-permute-start.16) | collective-permute-done | bytes 458784 | tf_op jit(solution)/shard_map/ppermute | solution.py:235
  63.4 6.3 %collective-permute-done.13.refs_12_.refs_7_ = bf16[256,896]{1,0:T(8,128)(2,1)S(1)} collective-permute-done((bf16[256,896]{1,0:T(8,128)(2,1)S(1)}, bf16[256,896]{1,0:T(8,128)(2,1)S(1)}, u32[]{:S(2)}, u32[]{:S(2)}) %collective-permute-start.13) | collective-permute-done | bytes 458784 | tf_op jit(solution)/shard_map/ppermute | solution.py:237
  71.0 13.2 %conv_forward.1 = (f32[64,1024]{1,0:T(8,128)S(1)}, bf16[64,1024]{1,0:T(8,128)(2,1)S(1)}, bf16[64,1024]{1,0:T(8,128)(2,1)}) custom-call(bf16[128,1024]{1,0:T(8,128)(2,1)S(1)} %pad_maximum_fusion.2.refs_0_, bf16[128,1024]{1,0:T(8,128)(2,1)S(1)} %collective-permute-done.1.refs_1_, bf16[128,1024]{1,0:T(8,128)(2,1)S(1)} %collective-permute-done.2.refs_2_, ...), custom_call_target="tpu_custom_call" | custom-call | flops 3758096384 | bytes 6291456 | tf_op jit(solution)/shard_map/conv_forward/pallas_call | solution.py:255
  84.2 2.1 %collective-permute-start.17 = (bf16[64,1024]{1,0:T(8,128)(2,1)}, bf16[64,1024]{1,0:T(8,128)(2,1)S(1)}, u32[]{:S(2)}, u32[]{:S(2)}) collective-permute-start(bf16[64,1024]{1,0:T(8,128)(2,1)} %get-tuple-element.10), channel_id=1, source_target_pairs={{0,1},{1,2},{2,3},{3,4},{4,5},{5,6},{6,7},{7,8},{8,9},{9,10},{10,1... | collective-permute-start | bytes 393224 | tf_op jit(solution)/shard_map/ppermute | solution.py:273
  86.3 6.6 %collective-permute-start.18 = (bf16[64,1024]{1,0:T(8,128)(2,1)S(1)}, bf16[64,1024]{1,0:T(8,128)(2,1)S(1)}, u32[]{:S(2)}, u32[]{:S(2)}) collective-permute-start(bf16[64,1024]{1,0:T(8,128)(2,1)S(1)} %get-tuple-element.11), channel_id=1, source_target_pairs={{1,0},{2,1},{3,2},{4,3},{5,4},{6,5},{7,6},{8,7},{9,8},{10,9},{11,1... | collective-permute-start | bytes 393224 | tf_op jit(solution)/shard_map/ppermute | solution.py:274
  96.9 6.4 %collective-permute-start.19 = (bf16[64,1024]{1,0:T(8,128)(2,1)S(1)}, bf16[64,1024]{1,0:T(8,128)(2,1)S(1)}, u32[]{:S(2)}, u32[]{:S(2)}) collective-permute-start(bf16[64,1024]{1,0:T(8,128)(2,1)S(1)} %get-tuple-element.13.refs_1_), channel_id=1, source_target_pairs={{1,0},{2,1},{3,2},{4,3},{5,4},{6,5},{7,6},{8,7},{9,8},{10,9},{11,1... | collective-permute-start | bytes 393224 | tf_op jit(solution)/shard_map/ppermute | solution.py:284
  103.3 1.9 %collective-permute-start.20 = (bf16[64,1024]{1,0:T(8,128)(2,1)S(1)}, bf16[64,1024]{1,0:T(8,128)(2,1)S(1)}, u32[]{:S(2)}, u32[]{:S(2)}) collective-permute-start(bf16[64,1024]{1,0:T(8,128)(2,1)S(1)} %get-tuple-element.13.refs_1_), channel_id=1, source_target_pairs={{0,1},{1,2},{2,3},{3,4},{4,5},{5,6},{6,7},{7,8},{8,9},{9,10},{10,1... | collective-permute-start | bytes 393224 | tf_op jit(solution)/shard_map/ppermute | solution.py:283
  105.8 7.1 %collective-permute-done.20.refs_2_ = bf16[64,1024]{1,0:T(8,128)(2,1)S(1)} collective-permute-done((bf16[64,1024]{1,0:T(8,128)(2,1)S(1)}, bf16[64,1024]{1,0:T(8,128)(2,1)S(1)}, u32[]{:S(2)}, u32[]{:S(2)}) %collective-permute-start.20) | collective-permute-done | bytes 131104 | tf_op jit(solution)/shard_map/ppermute | solution.py:283
  114.9 7.4 %conv_backward.1 = (bf16[512,1024]{1,0:T(8,128)(2,1)S(1)}, bf16[512,1024]{1,0:T(8,128)(2,1)S(1)}) custom-call(bf16[64,1024]{1,0:T(8,128)(2,1)S(1)} %collective-permute-done.19.refs_0_, bf16[64,1024]{1,0:T(8,128)(2,1)S(1)} %get-tuple-element.13.refs_1_, bf16[64,1024]{1,0:T(8,128)(2,1)S(1)} %collective-permute-done.20.refs_2_, ...), custom_call_target="tpu_custom_call" | custom-call | flops 3758096384 | bytes 6291456 | tf_op jit(solution)/shard_map/conv_backward/pallas_call | solution.py:285
  122.4 2.6 %collective-permute-done.21 = bf16[512,1024]{1,0:T(8,128)(2,1)S(1)} collective-permute-done((bf16[512,1024]{1,0:T(8,128)(2,1)S(1)}, bf16[512,1024]{1,0:T(8,128)(2,1)S(1)}, u32[]{:S(2)}, u32[]{:S(2)}) %collective-permute-start.21) | collective-permute-done | bytes 1048608 | tf_op jit(solution)/shard_map/ppermute | solution.py:301
  125.3 3.7 %collective-permute-start.24 = (bf16[128,1024]{1,0:T(8,128)(2,1)S(1)}, bf16[128,1024]{1,0:T(8,128)(2,1)S(1)}, u32[]{:S(2)}, u32[]{:S(2)}) collective-permute-start(bf16[128,1024]{1,0:T(8,128)(2,1)S(1)} %get-tuple-element.17), channel_id=1, source_target_pairs={{0,96},{16,112},{32,0},{48,16},{64,32},{80,48},{96,64},{112,80},{1... | collective-permute-start | bytes 786440 | tf_op jit(solution)/shard_map/ppermute | solution.py:308
  130.0 10.5 %collective-permute-done.24 = bf16[128,1024]{1,0:T(8,128)(2,1)S(1)} collective-permute-done((bf16[128,1024]{1,0:T(8,128)(2,1)S(1)}, bf16[128,1024]{1,0:T(8,128)(2,1)S(1)}, u32[]{:S(2)}, u32[]{:S(2)}) %collective-permute-start.24) | collective-permute-done | bytes 262176 | tf_op jit(solution)/shard_map/ppermute | solution.py:308
  140.5 3.5 %collective-permute-done.22 = bf16[128,1024]{1,0:T(8,128)(2,1)S(1)} collective-permute-done((bf16[128,1024]{1,0:T(8,128)(2,1)S(1)}, bf16[128,1024]{1,0:T(8,128)(2,1)S(1)}, u32[]{:S(2)}, u32[]{:S(2)}) %collective-permute-start.22) | collective-permute-done | bytes 262176 | tf_op jit(solution)/shard_map/ppermute | solution.py:308
  144.3 5.0 %collective-permute-start.25 = (bf16[64,1024]{1,0:T(8,128)(2,1)S(1)}, bf16[64,1024]{1,0:T(8,128)(2,1)S(1)}, u32[]{:S(2)}, u32[]{:S(2)}) collective-permute-start(bf16[64,1024]{1,0:T(8,128)(2,1)S(1)} %slice.101), channel_id=1, source_target_pairs={{0,128},{16,144},{32,160},{48,176},{64,192},{80,208},{96,224},{112... | collective-permute-start | bytes 393224 | tf_op jit(solution)/shard_map/ppermute | solution.py:309
  149.3 6.2 %collective-permute-done.25 = bf16[64,1024]{1,0:T(8,128)(2,1)S(1)} collective-permute-done((bf16[64,1024]{1,0:T(8,128)(2,1)S(1)}, bf16[64,1024]{1,0:T(8,128)(2,1)S(1)}, u32[]{:S(2)}, u32[]{:S(2)}) %collective-permute-start.25) | collective-permute-done | bytes 131104 | tf_op jit(solution)/shard_map/ppermute | solution.py:309
  (62 shorter events, 22.3 us)
Async XLA Ops:
  1.8 30.1 %collective-permute-start.10 = (bf16[64,1792]{1,0:T(8,128)(2,1)S(1)}, bf16[64,1792]{1,0:T(8,128)(2,1)S(1)}, u32[]{:S(2)}, u32[]{:S(2)}) collective-permute-start(bf16[64,1792]{1,0:T(8,128)(2,1)S(1)} %weights_transpose.1), channel_id=1, source_target_pairs={{0,3},{1,0},{2,1},{3,2},{4,7},{5,4},{6,5},{7,6},{8,11},{9,8},{10,9... | collective-permute-start | bytes 688136 | tf_op jit(solution)/shard_map/ppermute | solution.py:230
  6.5 25.5 %collective-permute-start.9 = (bf16[64,1792]{1,0:T(8,128)(2,1)S(1)}, bf16[64,1792]{1,0:T(8,128)(2,1)S(1)}, u32[]{:S(2)}, u32[]{:S(2)}) collective-permute-start(bf16[64,1792]{1,0:T(8,128)(2,1)S(1)} %weights_transpose.1), channel_id=1, source_target_pairs={{0,2},{1,3},{2,0},{3,1},{4,6},{5,7},{6,4},{7,5},{8,10},{9,11},{10,... | collective-permute-start | bytes 688136 | tf_op jit(solution)/shard_map/ppermute | solution.py:230
  6.5 25.5 %collective-permute-start.8 = (bf16[64,1792]{1,0:T(8,128)(2,1)S(1)}, bf16[64,1792]{1,0:T(8,128)(2,1)S(1)}, u32[]{:S(2)}, u32[]{:S(2)}) collective-permute-start(bf16[64,1792]{1,0:T(8,128)(2,1)S(1)} %weights_transpose.1), channel_id=1, source_target_pairs={{0,1},{1,2},{2,3},{3,0},{4,5},{5,6},{6,7},{7,4},{8,9},{9,10},{10,1... | collective-permute-start | bytes 688136 | tf_op jit(solution)/shard_map/ppermute | solution.py:230
  7.2 23.1 %collective-permute-start = (bf16[64,1024]{1,0:T(8,128)(2,1)S(1)}, bf16[64,1024]{1,0:T(8,128)(2,1)S(1)}, u32[]{:S(2)}, u32[]{:S(2)}) collective-permute-start(bf16[64,1024]{1,0:T(8,128)(2,1)S(1)} %bitcast.11), channel_id=1, source_target_pairs={{0,128},{16,144},{32,160},{48,176},{64,192},{80,208},{96,224},{112... | collective-permute-start | bytes 393224 | tf_op jit(solution)/shard_map/ppermute | solution.py:243
  30.3 6.8 %collective-permute-start.1 = (bf16[128,1024]{1,0:T(8,128)(2,1)S(1)}, bf16[128,1024]{1,0:T(8,128)(2,1)S(1)}, u32[]{:S(2)}, u32[]{:S(2)}) collective-permute-start(bf16[128,1024]{1,0:T(8,128)(2,1)S(1)} %pad_maximum_fusion.2.refs_0_), channel_id=1, source_target_pairs={{0,16},{16,0},{32,48},{48,32},{64,80},{80,64},{96,112},{112,96},{1... | collective-permute-start | bytes 786440 | tf_op jit(solution)/shard_map/ppermute | solution.py:248
  30.4 9.9 %collective-permute-start.2 = (bf16[128,1024]{1,0:T(8,128)(2,1)S(1)}, bf16[128,1024]{1,0:T(8,128)(2,1)S(1)}, u32[]{:S(2)}, u32[]{:S(2)}) collective-permute-start(bf16[128,1024]{1,0:T(8,128)(2,1)S(1)} %pad_maximum_fusion.2.refs_0_), channel_id=1, source_target_pairs={{0,32},{16,48},{32,64},{48,80},{64,96},{80,112},{96,0},{112,16},{1... | collective-permute-start | bytes 786440 | tf_op jit(solution)/shard_map/ppermute | solution.py:245
  32.1 18.3 %collective-permute-start.11 = (bf16[256,896]{1,0:T(8,128)(2,1)S(1)}, bf16[256,896]{1,0:T(8,128)(2,1)S(1)}, u32[]{:S(2)}, u32[]{:S(2)}) collective-permute-start(bf16[256,896]{1,0:T(8,128)(2,1)S(1)} %pad_maximum_fusion.refs_8_.refs_3_), channel_id=1, source_target_pairs={{0,4},{1,5},{2,6},{3,7},{4,8},{5,9},{6,10},{7,11},{8,12},{9,13},{1... | collective-permute-start | bytes 1376264 | tf_op jit(solution)/shard_map/ppermute | solution.py:233
  33.8 18.2 %collective-permute-start.14 = (bf16[256,896]{1,0:T(8,128)(2,1)S(1)}, bf16[256,896]{1,0:T(8,128)(2,1)S(1)}, u32[]{:S(2)}, u32[]{:S(2)}) collective-permute-start(bf16[256,896]{1,0:T(8,128)(2,1)S(1)} %pad_maximum_fusion.1.refs_9_.refs_4_), channel_id=1, source_target_pairs={{0,12},{1,13},{2,14},{3,15},{4,0},{5,1},{6,2},{7,3},{8,4},{9,5},{1... | collective-permute-start | bytes 1376264 | tf_op jit(solution)/shard_map/ppermute | solution.py:234
  34.4 12.6 %collective-permute-start.4 = (bf16[128,1024]{1,0:T(8,128)(2,1)S(1)}, bf16[128,1024]{1,0:T(8,128)(2,1)S(1)}, u32[]{:S(2)}, u32[]{:S(2)}) collective-permute-start(bf16[128,1024]{1,0:T(8,128)(2,1)S(1)} %pad_maximum_fusion.2.refs_0_), channel_id=1, source_target_pairs={{0,64},{16,80},{32,96},{48,112},{64,0},{80,16},{96,32},{112,48},{1... | collective-permute-start | bytes 786440 | tf_op jit(solution)/shard_map/ppermute | solution.py:245
  37.1 11.3 %collective-permute-start.6 = (bf16[128,1024]{1,0:T(8,128)(2,1)S(1)}, bf16[128,1024]{1,0:T(8,128)(2,1)S(1)}, u32[]{:S(2)}, u32[]{:S(2)}) collective-permute-start(bf16[128,1024]{1,0:T(8,128)(2,1)S(1)} %pad_maximum_fusion.2.refs_0_), channel_id=1, source_target_pairs={{0,96},{16,112},{32,0},{48,16},{64,32},{80,48},{96,64},{112,80},{1... | collective-permute-start | bytes 786440 | tf_op jit(solution)/shard_map/ppermute | solution.py:245
  40.3 9.6 %collective-permute-start.3 = (bf16[128,1024]{1,0:T(8,128)(2,1)S(1)}, bf16[128,1024]{1,0:T(8,128)(2,1)S(1)}, u32[]{:S(2)}, u32[]{:S(2)}) collective-permute-start(bf16[128,1024]{1,0:T(8,128)(2,1)S(1)} %collective-permute-done.2.refs_2_), channel_id=1, source_target_pairs={{0,16},{16,0},{32,48},{48,32},{64,80},{80,64},{96,112},{112,96},{1... | collective-permute-start | bytes 786440 | tf_op jit(solution)/shard_map/ppermute | solution.py:248
  46.9 6.5 %collective-permute-start.5 = (bf16[128,1024]{1,0:T(8,128)(2,1)S(1)}, bf16[128,1024]{1,0:T(8,128)(2,1)S(1)}, u32[]{:S(2)}, u32[]{:S(2)}) collective-permute-start(bf16[128,1024]{1,0:T(8,128)(2,1)S(1)} %collective-permute-done.4.refs_4_), channel_id=1, source_target_pairs={{0,16},{16,0},{32,48},{48,32},{64,80},{80,64},{96,112},{112,96},{1... | collective-permute-start | bytes 786440 | tf_op jit(solution)/shard_map/ppermute | solution.py:248
  48.4 13.5 %collective-permute-start.12 = (bf16[256,896]{1,0:T(8,128)(2,1)S(1)}, bf16[256,896]{1,0:T(8,128)(2,1)S(1)}, u32[]{:S(2)}, u32[]{:S(2)}) collective-permute-start(bf16[256,896]{1,0:T(8,128)(2,1)S(1)} %pad_maximum_fusion.1.refs_9_.refs_4_), channel_id=1, source_target_pairs={{0,4},{1,5},{2,6},{3,7},{4,8},{5,9},{6,10},{7,11},{8,12},{9,13},{1... | collective-permute-start | bytes 1376264 | tf_op jit(solution)/shard_map/ppermute | solution.py:236
  50.0 13.5 %collective-permute-start.16 = (bf16[256,896]{1,0:T(8,128)(2,1)S(1)}, bf16[256,896]{1,0:T(8,128)(2,1)S(1)}, u32[]{:S(2)}, u32[]{:S(2)}) collective-permute-start(bf16[256,896]{1,0:T(8,128)(2,1)S(1)} %pad_maximum_fusion.refs_8_.refs_3_), channel_id=1, source_target_pairs={{0,12},{1,13},{2,14},{3,15},{4,0},{5,1},{6,2},{7,3},{8,4},{9,5},{1... | collective-permute-start | bytes 1376264 | tf_op jit(solution)/shard_map/ppermute | solution.py:235
  50.4 19.3 %collective-permute-start.13 = (bf16[256,896]{1,0:T(8,128)(2,1)S(1)}, bf16[256,896]{1,0:T(8,128)(2,1)S(1)}, u32[]{:S(2)}, u32[]{:S(2)}) collective-permute-start(bf16[256,896]{1,0:T(8,128)(2,1)S(1)} %collective-permute-done.11.refs_10_.refs_5_), channel_id=1, source_target_pairs={{0,4},{1,5},{2,6},{3,7},{4,8},{5,9},{6,10},{7,11},{8,12},{9,13},{1... | collective-permute-start | bytes 1376264 | tf_op jit(solution)/shard_map/ppermute | solution.py:237
  52.0 19.0 %collective-permute-start.15 = (bf16[256,896]{1,0:T(8,128)(2,1)S(1)}, bf16[256,896]{1,0:T(8,128)(2,1)S(1)}, u32[]{:S(2)}, u32[]{:S(2)}) collective-permute-start(bf16[256,896]{1,0:T(8,128)(2,1)S(1)} %collective-permute-done.14.refs_15_.refs_10_), channel_id=1, source_target_pairs={{0,12},{1,13},{2,14},{3,15},{4,0},{5,1},{6,2},{7,3},{8,4},{9,5},{1... | collective-permute-start | bytes 1376264 | tf_op jit(solution)/shard_map/ppermute | solution.py:238
  84.2 11.0 %collective-permute-start.17 = (bf16[64,1024]{1,0:T(8,128)(2,1)}, bf16[64,1024]{1,0:T(8,128)(2,1)S(1)}, u32[]{:S(2)}, u32[]{:S(2)}) collective-permute-start(bf16[64,1024]{1,0:T(8,128)(2,1)} %get-tuple-element.10), channel_id=1, source_target_pairs={{0,1},{1,2},{2,3},{3,4},{4,5},{5,6},{6,7},{7,8},{8,9},{9,10},{10,1... | collective-permute-start | bytes 393224 | tf_op jit(solution)/shard_map/ppermute | solution.py:273
  86.3 9.8 %collective-permute-start.18 = (bf16[64,1024]{1,0:T(8,128)(2,1)S(1)}, bf16[64,1024]{1,0:T(8,128)(2,1)S(1)}, u32[]{:S(2)}, u32[]{:S(2)}) collective-permute-start(bf16[64,1024]{1,0:T(8,128)(2,1)S(1)} %get-tuple-element.11), channel_id=1, source_target_pairs={{1,0},{2,1},{3,2},{4,3},{5,4},{6,5},{7,6},{8,7},{9,8},{10,9},{11,1... | collective-permute-start | bytes 393224 | tf_op jit(solution)/shard_map/ppermute | solution.py:274
  96.9 8.9 %collective-permute-start.19 = (bf16[64,1024]{1,0:T(8,128)(2,1)S(1)}, bf16[64,1024]{1,0:T(8,128)(2,1)S(1)}, u32[]{:S(2)}, u32[]{:S(2)}) collective-permute-start(bf16[64,1024]{1,0:T(8,128)(2,1)S(1)} %get-tuple-element.13.refs_1_), channel_id=1, source_target_pairs={{1,0},{2,1},{3,2},{4,3},{5,4},{6,5},{7,6},{8,7},{9,8},{10,9},{11,1... | collective-permute-start | bytes 393224 | tf_op jit(solution)/shard_map/ppermute | solution.py:284
  103.3 9.6 %collective-permute-start.20 = (bf16[64,1024]{1,0:T(8,128)(2,1)S(1)}, bf16[64,1024]{1,0:T(8,128)(2,1)S(1)}, u32[]{:S(2)}, u32[]{:S(2)}) collective-permute-start(bf16[64,1024]{1,0:T(8,128)(2,1)S(1)} %get-tuple-element.13.refs_1_), channel_id=1, source_target_pairs={{0,1},{1,2},{2,3},{3,4},{4,5},{5,6},{6,7},{7,8},{8,9},{9,10},{10,1... | collective-permute-start | bytes 393224 | tf_op jit(solution)/shard_map/ppermute | solution.py:283
  125.3 15.2 %collective-permute-start.24 = (bf16[128,1024]{1,0:T(8,128)(2,1)S(1)}, bf16[128,1024]{1,0:T(8,128)(2,1)S(1)}, u32[]{:S(2)}, u32[]{:S(2)}) collective-permute-start(bf16[128,1024]{1,0:T(8,128)(2,1)S(1)} %get-tuple-element.17), channel_id=1, source_target_pairs={{0,96},{16,112},{32,0},{48,16},{64,32},{80,48},{96,64},{112,80},{1... | collective-permute-start | bytes 786440 | tf_op jit(solution)/shard_map/ppermute | solution.py:308
  129.0 11.5 %collective-permute-start.23 = (bf16[128,1024]{1,0:T(8,128)(2,1)S(1)}, bf16[128,1024]{1,0:T(8,128)(2,1)S(1)}, u32[]{:S(2)}, u32[]{:S(2)}) collective-permute-start(bf16[128,1024]{1,0:T(8,128)(2,1)S(1)} %get-tuple-element.18), channel_id=1, source_target_pairs={{0,64},{16,80},{32,96},{48,112},{64,0},{80,16},{96,32},{112,48},{1... | collective-permute-start | bytes 786440 | tf_op jit(solution)/shard_map/ppermute | solution.py:308
  129.4 14.6 %collective-permute-start.22 = (bf16[128,1024]{1,0:T(8,128)(2,1)S(1)}, bf16[128,1024]{1,0:T(8,128)(2,1)S(1)}, u32[]{:S(2)}, u32[]{:S(2)}) collective-permute-start(bf16[128,1024]{1,0:T(8,128)(2,1)S(1)} %get-tuple-element.16), channel_id=1, source_target_pairs={{0,32},{16,48},{32,64},{48,80},{64,96},{80,112},{96,0},{112,16},{1... | collective-permute-start | bytes 786440 | tf_op jit(solution)/shard_map/ppermute | solution.py:308
  144.3 11.2 %collective-permute-start.25 = (bf16[64,1024]{1,0:T(8,128)(2,1)S(1)}, bf16[64,1024]{1,0:T(8,128)(2,1)S(1)}, u32[]{:S(2)}, u32[]{:S(2)}) collective-permute-start(bf16[64,1024]{1,0:T(8,128)(2,1)S(1)} %slice.101), channel_id=1, source_target_pairs={{0,128},{16,144},{32,160},{48,176},{64,192},{80,208},{96,224},{112... | collective-permute-start | bytes 393224 | tf_op jit(solution)/shard_map/ppermute | solution.py:309
  (11 other events, 150.5 us)

commit v2 on v1

v2 whole, which is shorter than its diff:
```python
import functools

import jax
import jax.numpy as jnp
from jax import lax
from jax.experimental import pallas as pl
from jax.experimental.pallas import tpu as pltpu
from jax.sharding import PartitionSpec as P

HH = 32
WW = 32
CELLS = HH * WW
TAPS = 27
SLOT_TAPS = [*range(9, 18), None, *range(0, 9), *range(18, 27)]
SLOTS = 28
BLOCK = 64
COLS = SLOTS * BLOCK
SAME = 10 * BLOCK
HALF = BLOCK // 2
GROUPS = [(0, 1, 2, 3)]
BLOCKS = 16
CHANNELS = BLOCKS * BLOCK

ZH, XN, CN = 2, 4, 2
YN, ZN = 4, 4

BF16 = jnp.bfloat16
F32 = jnp.float32
LIMIT = pltpu.CompilerParams(vmem_limit_bytes=24 * 1024 * 1024)


def filt_index(zh, x, c):
    return (zh * XN + x) * CN + c


FILT = [(zh, x, c) for zh in range(ZH) for x in range(XN) for c in range(CN)]
SLAB = [(y, z) for y in range(YN) for z in range(ZN)]
TO_CORE = [(filt_index(*d), filt_index(d[0], d[1], 1 - d[2])) for d in FILT]
TO_ZHI = [(filt_index(*d), filt_index(1 - d[0], d[1], d[2])) for d in FILT]


def to_x(k):
    return [(filt_index(*d), filt_index(d[0], (d[1] + k) % XN, d[2])) for d in FILT]


def to_y(k):
    return [(y * ZN + z, ((y + k) % YN) * ZN + z) for y, z in SLAB]


def to_z(k):
    return [(y * ZN + z, y * ZN + (z + k) % ZN) for y, z in SLAB]


UP = [(i, i + 1) for i in range(YN * ZN - 1)]
DOWN = [(i + 1, i) for i in range(YN * ZN - 1)]

VMEM = pl.BlockSpec(memory_space=pltpu.VMEM)
ANY = pl.BlockSpec(memory_space=pl.ANY)
HBM = pl.BlockSpec(memory_space=pltpu.HBM)


def transpose_kernel(w_ref, out_ref):
    for pair in range(0, SLOTS, 2):
        parts = []
        for slot in (pair, pair + 1):
            tap = SLOT_TAPS[slot]
            if tap is None:
                parts.append(jnp.zeros((BLOCK, BLOCK), F32))
            else:
                parts.append(w_ref[tap * BLOCK : (tap + 1) * BLOCK, :].astype(F32))
        turned = jnp.concatenate(parts, axis=0).T
        out_ref[:, pair * BLOCK : (pair + 2) * BLOCK] = turned.astype(BF16)


def filt_position():
    mine = lax.axis_index("filt")
    return mine // (XN * CN), (mine // CN) % XN, mine % CN


def slab_position():
    mine = lax.axis_index("slab")
    return mine // ZN, mine % ZN


def rows_of(block):
    return pl.ds(pl.multiple_of(block * BLOCK, BLOCK), BLOCK)


def weight_copies(pieces, w_scr, sem):
    y, z = slab_position()
    copies = []

    def add(ref, start, row, size):
        place = pl.ds(pl.multiple_of(row, HALF), size)
        copies.append(
            pltpu.make_async_copy(
                ref.at[pl.ds(start, size), :], w_scr.at[place, :], sem.at[len(copies)]
            )
        )

    for at, group in enumerate(GROUPS):
        refs = pieces[5 * at : 5 * at + 5]
        middle = len(group) * HALF
        for step_y in range(YN):
            for index, step_z in enumerate(group):
                block = ((y + YN - step_y) % YN) * ZN + (z + ZN - step_z) % ZN
                row, start = block * BLOCK, index * BLOCK
                if step_y != 2:
                    add(refs[{0: 0, 1: 1, 3: 4}[step_y]], start, row, BLOCK)
                elif start + BLOCK <= middle:
                    add(refs[2], start, row, BLOCK)
                elif start >= middle:
                    add(refs[3], start - middle, row, BLOCK)
                else:
                    add(refs[2], start, row, HALF)
                    add(refs[3], 0, row + HALF, HALF)
    return copies


def input_copies(pieces, x_scr, sem):
    zh, x, c = filt_position()
    copies = []
    for other in range(CN):
        for step in range(XN):
            for far in range(ZH):
                core = c if other == 0 else 1 - c
                high = zh if far == 0 else 1 - zh
                block = filt_index(high, (x + XN - step) % XN, core)
                copies.append(
                    pltpu.make_async_copy(
                        pieces[other].at[pl.ds((step * ZH + far) * BLOCK, BLOCK), :],
                        x_scr.at[rows_of(block), :],
                        sem.at[len(copies)],
                    )
                )
    return copies


def start_all(copies):
    for copy in copies:
        copy.start()


def wait_all(copies):
    for copy in copies:
        copy.wait()


def shifted_sum(y_scr, first, base):
    cell = lax.broadcasted_iota(jnp.int32, (8, CELLS), 1)
    column = cell % WW
    row_ok = {0: cell >= WW, 2: cell < CELLS - WW}
    col_ok = {0: column >= 1, 2: column < WW - 1}
    total = None
    for col in range(3):
        lane = None
        for row in range(3):
            value = y_scr[pl.ds((first + 3 * row + col) * BLOCK + base, 8), :]
            if row != 1:
                value = pltpu.roll(value, ((1 - row) * WW) % CELLS, 1)
                value = jnp.where(row_ok[row], value, 0.0)
            lane = value if lane is None else lane + value
        if col != 1:
            lane = pltpu.roll(lane, (1 - col) % CELLS, 1)
            lane = jnp.where(col_ok[col], lane, 0.0)
        total = lane if total is None else total + lane
    return total


def convolve(planes, w, x, out_refs, y_scr):
    y_scr[...] = lax.dot_general(w, x, (((0,), (0,)), ((), ())), preferred_element_type=F32)

    def body(part, carry):
        base = pl.multiple_of(part * 8, 8)
        for first, out in zip(planes, out_refs):
            out[pl.ds(base, 8), :] = shifted_sum(y_scr, first, base).astype(out.dtype)
        return carry

    lax.fori_loop(0, BLOCK // 8, body, 0)


def forward_beside_kernel(*refs):
    count = 2 + 5 * len(GROUPS)
    x_pieces, w_pieces = refs[:2], refs[2:count]
    matrix_ref, up_ref, down_ref = refs[count + 1 : count + 4]
    x_scr, w_scr, y_scr, x_sem, w_sem, out_sem = refs[count + 4 :]
    copies = input_copies(x_pieces, x_scr, x_sem) + weight_copies(w_pieces, w_scr, w_sem)
    start_all(copies)
    wait_all(copies)
    keep = pltpu.make_async_copy(w_scr, matrix_ref, out_sem)
    keep.start()
    convolve((0, 9), w_scr[:, SAME:], x_scr[...], (up_ref, down_ref), y_scr)
    keep.wait()


def ready_kernel(*refs):
    refs[-1][...] = jnp.zeros((8, 128), BF16)


def forward_same_kernel(*refs):
    x_pieces, matrix_ref, own_ref = refs[:2], refs[2], refs[3]
    x_scr, w_scr, y_scr, x_sem, w_sem = refs[4:]
    copies = input_copies(x_pieces, x_scr, x_sem)
    copies.append(pltpu.make_async_copy(matrix_ref.at[:, pl.ds(0, SAME)], w_scr, w_sem))
    start_all(copies)
    wait_all(copies)
    convolve((0,), w_scr[...], x_scr[...], (own_ref,), y_scr)


def pointwise_kernel(own_ref, below_ref, above_ref, bias_ref, cot_ref, act_ref, grad_ref):
    preact = (
        own_ref[...]
        + below_ref[...].astype(F32)
        + above_ref[...].astype(F32)
        + bias_ref[...].astype(F32)
    )
    sig = jax.nn.sigmoid(preact)
    act_ref[...] = (preact * sig).astype(BF16)
    slope = sig * (1.0 + preact * (1.0 - sig))
    grad_ref[...] = (cot_ref[...].astype(F32) * slope).astype(BF16)


def stack_taps(grad_refs, g_scr):
    cell = lax.broadcasted_iota(jnp.int32, (16, CELLS), 1)
    column = cell % WW
    row_ok = {2: cell >= WW, 0: cell < CELLS - WW}
    col_ok = {2: column >= 1, 0: column < WW - 1}

    def body(part, carry):
        base = pl.multiple_of(part * 16, 16)
        for at, grad in enumerate(grad_refs):
            plane = grad[pl.ds(base, 16), :].astype(F32)
            for col in range(3):
                lane = plane
                if col != 1:
                    lane = pltpu.roll(lane, (col - 1) % CELLS, 1)
                    lane = jnp.where(col_ok[col], lane, 0.0)
                for row in range(3):
                    value = lane
                    if row != 1:
                        value = pltpu.roll(value, ((row - 1) * WW) % CELLS, 1)
                        value = jnp.where(row_ok[row], value, 0.0)
                    slot = 9 * at + 3 * row + col
                    g_scr[pl.ds(slot * BLOCK + base, 16), :] = value.astype(BF16)
        return carry

    lax.fori_loop(0, BLOCK // 16, body, 0)


def backward_same_kernel(grad_ref, matrix_ref, out_ref, w_scr, g_scr, sem):
    copy = pltpu.make_async_copy(matrix_ref.at[:, pl.ds(0, SAME)], w_scr, sem)
    copy.start()
    stack_taps([grad_ref], g_scr)
    g_scr[9 * BLOCK :, :] = jnp.zeros((BLOCK, CELLS), BF16)
    copy.wait()
    half = CHANNELS // 2
    for start in (0, half):
        out_ref[start : start + half, :] = jnp.dot(
            w_scr[start : start + half, :], g_scr[...], preferred_element_type=F32
        )


def backward_beside_kernel(far, *refs):
    above_ref, below_ref, same_ref, matrix_ref, out_ref, w_scr, g_scr, sem = refs
    zh, x, c = filt_position()
    size = CHANNELS // 2
    first = pl.multiple_of(((zh + far) % ZH) * size, size)
    copy = pltpu.make_async_copy(
        matrix_ref.at[pl.ds(first, size), pl.ds(SAME, COLS - SAME)], w_scr, sem
    )
    copy.start()
    stack_taps([above_ref, below_ref], g_scr)
    copy.wait()
    total = same_ref[pl.ds(first, size), :] + jnp.dot(
        w_scr[...], g_scr[...], preferred_element_type=F32
    )
    total = total.astype(BF16)
    for at in range(size // BLOCK):
        along, core = at // CN, at % CN
        place = (core + c) % CN * XN + (along + XN - x) % XN
        out_ref[rows_of(place), :] = total[at * BLOCK : (at + 1) * BLOCK, :]


def shape(rows, columns, dtype=BF16):
    return jax.ShapeDtypeStruct((rows, columns), dtype)


def call(kernel, name, outs, scratch, columns, operands, in_any=(), in_hbm=(), out_hbm=(), limit=None):
    cost = None
    if columns:
        cost = pl.CostEstimate(
            flops=2 * columns * CHANNELS * CELLS, bytes_accessed=2**20, transcendentals=0
        )
    return pl.pallas_call(
        kernel,
        out_shape=outs,
        in_specs=[
            ANY if at in in_any else HBM if at in in_hbm else VMEM for at in range(len(operands))
        ],
        out_specs=tuple(HBM if at in out_hbm else VMEM for at in range(len(outs))),
        scratch_shapes=scratch,
        compiler_params=pltpu.CompilerParams(vmem_limit_bytes=(limit or 24) * 2**20),
        cost_estimate=cost,
        name=name,
    )(*operands)


def gather_weights(weights):
    taps_first = jnp.transpose(weights, (1, 0, 2)).reshape(TAPS * BLOCK, BLOCK)
    (own,) = call(
        transpose_kernel, "weights_transpose", (shape(BLOCK, COLS),), [], 0, [taps_first]
    )
    blocks = [own] + [lax.ppermute(own, "slab", to_z(k)) for k in range(1, ZN)]
    pieces = []
    for group in GROUPS:
        line = jnp.concatenate([blocks[k] for k in group], axis=0)
        half = line.shape[0] // 2
        before = lax.ppermute(line, "slab", to_y(1))
        after = lax.ppermute(line, "slab", to_y(-1))
        first = lax.ppermute(before[:half], "slab", to_y(1))
        second = lax.ppermute(after[half:], "slab", to_y(-1))
        pieces += [line, before, first, second, after]
    return pieces


def gather_inputs(inputs, w_pieces):
    far = lax.ppermute(lax.optimization_barrier((inputs, w_pieces[0]))[0], "filt", TO_ZHI)
    pair = jnp.concatenate([inputs, far], axis=0)
    row = jnp.concatenate(
        [pair] + [lax.ppermute(pair, "filt", to_x(k)) for k in range(1, XN)], axis=0
    )
    return [row, lax.ppermute(row, "filt", TO_CORE)]


def sum_over_row(part):
    size = part.shape[0] // 2
    received = lax.ppermute(part[size:], "filt", TO_CORE)
    sums = []
    for k in range(XN):
        rows = slice(k * BLOCK, (k + 1) * BLOCK)
        sums.append((part[rows].astype(F32) + received[rows].astype(F32)).astype(BF16))
    arrived = [lax.ppermute(sums[k], "filt", to_x(k)) for k in range(1, XN)]
    result = sums[0].astype(F32)
    for piece in arrived:
        result = result + piece.astype(F32)
    return result


def local(inputs, weights, bias, cotangent):
    w_pieces = gather_weights(weights)
    x_pieces = gather_inputs(inputs.reshape(BLOCK, CELLS), w_pieces)
    (ready,) = call(
        ready_kernel, "weights_ready", (shape(8, 128),), [], 7168, w_pieces[2:4], in_any=range(2)
    )
    x_scratch = pltpu.VMEM((CHANNELS, CELLS), BF16)
    matrix, up, down = call(
        forward_beside_kernel,
        "forward_beside",
        (shape(CHANNELS, COLS), shape(BLOCK, CELLS), shape(BLOCK, CELLS)),
        [
            x_scratch,
            pltpu.VMEM((CHANNELS, COLS), BF16),
            pltpu.VMEM((COLS - SAME, CELLS), F32),
            pltpu.SemaphoreType.DMA((BLOCKS,)),
            pltpu.SemaphoreType.DMA((2 * BLOCKS,)),
            pltpu.SemaphoreType.DMA,
        ],
        COLS - SAME,
        x_pieces + w_pieces + [ready],
        in_any=range(3 + len(w_pieces)),
        out_hbm=(0,),
        limit=56,
    )
    below = lax.ppermute(up, "slab", UP)
    above = lax.ppermute(down, "slab", DOWN)
    (own,) = call(
        forward_same_kernel,
        "forward_same",
        (shape(BLOCK, CELLS, F32),),
        [
            x_scratch,
            pltpu.VMEM((CHANNELS, SAME), BF16),
            pltpu.VMEM((SAME, CELLS), F32),
            pltpu.SemaphoreType.DMA((BLOCKS,)),
            pltpu.SemaphoreType.DMA,
        ],
        SAME,
        x_pieces + [matrix],
        in_any=range(2),
        in_hbm=(2,),
        limit=55,
    )
    activated, grad = call(
        pointwise_kernel,
        "silu_and_slope",
        (shape(BLOCK, CELLS), shape(BLOCK, CELLS)),
        [],
        0,
        [own, below, above, bias.reshape(BLOCK, 1), cotangent.reshape(BLOCK, CELLS)],
    )
    grad_below = lax.ppermute(grad, "slab", UP)
    grad_above = lax.ppermute(grad, "slab", DOWN)
    (same,) = call(
        backward_same_kernel,
        "backward_same",
        (shape(CHANNELS, CELLS, F32),),
        [
            pltpu.VMEM((CHANNELS, SAME), BF16),
            pltpu.VMEM((SAME, CELLS), BF16),
            pltpu.SemaphoreType.DMA,
        ],
        SAME,
        [grad, matrix],
        in_hbm=(1,),
    )
    sums = []
    for far, name in ((1, "backward_far"), (0, "backward_near")):
        (part,) = call(
            functools.partial(backward_beside_kernel, far),
            name,
            (shape(CHANNELS // 2, CELLS),),
            [
                pltpu.VMEM((CHANNELS // 2, COLS - SAME), BF16),
                pltpu.VMEM((COLS - SAME, CELLS), BF16),
                pltpu.SemaphoreType.DMA,
            ],
            (COLS - SAME) // 2,
            [grad_above, grad_below, same, matrix],
            in_hbm=(3,),
        )
        sums.append(sum_over_row(part))
    arrived = lax.ppermute(sums[0].astype(BF16), "filt", TO_ZHI)
    input_grad = (sums[1] + arrived.astype(F32)).astype(BF16)
    return activated.reshape(cotangent.shape), input_grad.reshape(inputs.shape)


def solution(mesh):
    return jax.shard_map(
        local,
        mesh=mesh,
        in_specs=(
            P("filt", "slab", None),
            P("filt", None, "slab"),
            P("filt"),
            P("filt", "slab", None),
        ),
        out_specs=(P("filt", "slab", None), P("filt", "slab", None)),
        check_vma=False,
    )
```

time: 158 us -> 130 us (0.82)
  waiting for transfers between devices: 78 us -> 43.7 us
  starting transfers between devices: 50.5 us -> 54.6 us
  Pallas kernels: 21.6 us -> 24.3 us
    ppermute x19 -> x18, waiting for transfers between devices: 68 us -> 25.4 us  [the longest x1 7.85 us: gather_weights(): second = lax.ppermute(after[half:], 'slab', to_y(-1))]
    ppermute x3, waiting for transfers between devices: 0.01 us -> 18.3 us  [gather_weights(): blocks = [own] + [lax.ppermute(own, 'slab', to_z(k)) for k in range(1, ZN)]]
    ppermute x1, waiting for transfers between devices: 7.05 us -> 0.01 us  [local(): grad_below = lax.ppermute(grad, 'slab', UP)]
    ppermute x19 -> x18, starting transfers between devices: 28.2 us -> 32 us  [the longest x6 8.95 us: sum_over_row(): arrived = [lax.ppermute(sums[k], 'filt', to_x(k)) for k in range(1, XN)]]
    pallas_call x4 -> x8, Pallas kernels: 21.6 us -> 24.3 us  [call(): pl.pallas_call(kernel, out_shape=outs, in_specs=[ANY if at in in_any else...]
    unnamed x18 -> x32, local copies, waits for them, and re-layouts: 3.07 us -> 4.36 us
  transfers between devices with their start and end apart: 26 -> 25, of which waited for: 17 -> 10; matrix products, arithmetic and copies ran while one was open for 1% -> 1% of each run, Pallas kernels for 0% -> 9%
where the time goes in v2:
time: 130 us; the launch traced here: 129 us
  starting transfers between devices  54.6 us (42%)
  waiting for transfers between devices  43.7 us (34%)
  Pallas kernels  24.3 us (19%)
  local copies, waits for them, and re-layouts  4.62 us (4%)
    pallas_call x8, Pallas kernels, call(): pl.pallas_call(kernel, out_shape=outs, in_specs=[ANY if at in in_any else...  24.3 us
    ppermute x3, waiting for transfers between devices, gather_weights(): blocks = [own] + [lax.ppermute(own, 'slab', to_z(k)) for k in range(1, ZN)]  18.3 us
    ppermute x6, starting transfers between devices, sum_over_row(): arrived = [lax.ppermute(sums[k], 'filt', to_x(k)) for k in range(1, XN)]  8.95 us
    ppermute x1, waiting for transfers between devices, gather_weights(): second = lax.ppermute(after[half:], 'slab', to_y(-1))  7.85 us
    ppermute x1, starting transfers between devices, local(): grad_above = lax.ppermute(grad, 'slab', DOWN)  6.62 us
    ppermute x3, starting transfers between devices, gather_inputs(): lax.ppermute(pair, 'filt', to_x(k))  6.42 us
    ppermute x1, starting transfers between devices, gather_inputs(): lax.ppermute(lax.optimization_barrier((inputs, w_pieces[0]))[0], 'filt',...  6.11 us
    ppermute x1, starting transfers between devices, local(): arrived = lax.ppermute(sums[0].astype(BF16), 'filt', TO_ZHI)  5.79 us
  transfers between devices with their start and end apart: 25, of which 10 were waited for; matrix products, arithmetic and copies ran while one was open for 1% of the time, Pallas kernels for 9%

profile of v2, /device:TPU:8, one launch (start us, length us, event | category | flops | bytes accessed | tf_op | source)
XLA Modules:
  0.0 129.4 jit_solution(3705975876829435038)
XLA Ops:
  1.8 4.7 %collective-permute-start.2 = (bf16[64,1792]{1,0:T(8,128)(2,1)S(1)}, bf16[64,1792]{1,0:T(8,128)(2,1)S(1)}, u32[]{:S(2)}, u32[]{:S(2)}) collective-permute-start(bf16[64,1792]{1,0:T(8,128)(2,1)S(1)} %weights_transpose.1), channel_id=1, source_target_pairs={{0,3},{1,0},{2,1},{3,2},{4,7},{5,4},{6,5},{7,6},{8,11},{9,8},{10,9... | collective-permute-start | bytes 688136 | tf_op jit(solution)/shard_map/ppermute | solution.py:313
  7.2 5.4 %collective-permute-done.2 = bf16[64,1792]{1,0:T(8,128)(2,1)S(1)} collective-permute-done((bf16[64,1792]{1,0:T(8,128)(2,1)S(1)}, bf16[64,1792]{1,0:T(8,128)(2,1)S(1)}, u32[]{:S(2)}, u32[]{:S(2)}) %collective-permute-start.2) | collective-permute-done | bytes 229408 | tf_op jit(solution)/shard_map/ppermute | solution.py:313
  12.6 12.9 %collective-permute-done.1 = bf16[64,1792]{1,0:T(8,128)(2,1)S(1)} collective-permute-done((bf16[64,1792]{1,0:T(8,128)(2,1)S(1)}, bf16[64,1792]{1,0:T(8,128)(2,1)S(1)}, u32[]{:S(2)}, u32[]{:S(2)}) %collective-permute-start.1) | collective-permute-done | bytes 229408 | tf_op jit(solution)/shard_map/ppermute | solution.py:313
  27.7 6.1 %collective-permute-start.3 = (bf16[64,1024]{1,0:T(8,128)(2,1)S(1)}, bf16[64,1024]{1,0:T(8,128)(2,1)S(1)}, u32[]{:S(2)}, u32[]{:S(2)}) collective-permute-start(bf16[64,1024]{1,0:T(8,128)(2,1)S(1)} %bitcast.12), channel_id=1, source_target_pairs={{0,128},{16,144},{32,160},{48,176},{64,192},{80,208},{96,224},{112... | collective-permute-start | bytes 393224 | tf_op jit(solution)/shard_map/ppermute | solution.py:327
  33.8 4.3 %collective-permute-done.3 = bf16[64,1024]{1,0:T(8,128)(2,1)S(1)} collective-permute-done((bf16[64,1024]{1,0:T(8,128)(2,1)S(1)}, bf16[64,1024]{1,0:T(8,128)(2,1)S(1)}, u32[]{:S(2)}, u32[]{:S(2)}) %collective-permute-start.3) | collective-permute-done | bytes 131104 | tf_op jit(solution)/shard_map/ppermute | solution.py:327
  38.2 3.1 %collective-permute-start.5 = (bf16[128,1024]{1,0:T(8,128)(2,1)S(1)}, bf16[128,1024]{1,0:T(8,128)(2,1)S(1)}, u32[]{:S(2)}, u32[]{:S(2)}) collective-permute-start(bf16[128,1024]{1,0:T(8,128)(2,1)S(1)} %pad_maximum_fusion.1), channel_id=1, source_target_pairs={{0,64},{16,80},{32,96},{48,112},{64,0},{80,16},{96,32},{112,48},{1... | collective-permute-start | bytes 786440 | tf_op jit(solution)/shard_map/ppermute | solution.py:330
  41.9 2.7 %collective-permute-start.6 = (bf16[128,1024]{1,0:T(8,128)(2,1)S(1)}, bf16[128,1024]{1,0:T(8,128)(2,1)S(1)}, u32[]{:S(2)}, u32[]{:S(2)}) collective-permute-start(bf16[128,1024]{1,0:T(8,128)(2,1)S(1)} %pad_maximum_fusion.1), channel_id=1, source_target_pairs={{0,96},{16,112},{32,0},{48,16},{64,32},{80,48},{96,64},{112,80},{1... | collective-permute-start | bytes 786440 | tf_op jit(solution)/shard_map/ppermute | solution.py:330
  44.6 2.5 %collective-permute-done.10.refs_6_ = bf16[256,1792]{1,0:T(8,128)(2,1)S(1)} collective-permute-done((bf16[256,1792]{1,0:T(8,128)(2,1)S(1)}, bf16[256,1792]{1,0:T(8,128)(2,1)S(1)}, u32[]{:S(2)}, u32[]{:S(2)}) %collective-permute-start.10) | collective-permute-done | bytes 917536 | tf_op jit(solution)/shard_map/ppermute | solution.py:319
  50.0 7.8 %collective-permute-done.11.refs_1_.refs_5_ = bf16[128,1792]{1,0:T(8,128)(2,1)S(1)} collective-permute-done((bf16[128,1792]{1,0:T(8,128)(2,1)S(1)}, bf16[128,1792]{1,0:T(8,128)(2,1)S(1)}, u32[]{:S(2)}, u32[]{:S(2)}) %collective-permute-start.11) | collective-permute-done | bytes 458784 | tf_op jit(solution)/shard_map/ppermute | solution.py:321
  57.9 2.8 %collective-permute-done.9.refs_0_.refs_4_ = bf16[128,1792]{1,0:T(8,128)(2,1)S(1)} collective-permute-done((bf16[128,1792]{1,0:T(8,128)(2,1)S(1)}, bf16[128,1792]{1,0:T(8,128)(2,1)S(1)}, u32[]{:S(2)}, u32[]{:S(2)}) %collective-permute-start.9) | collective-permute-done | bytes 458784 | tf_op jit(solution)/shard_map/ppermute | solution.py:320
  63.0 8.5 %forward_beside.1 = (bf16[1024,1792]{1,0:T(8,128)(2,1)}, bf16[64,1024]{1,0:T(8,128)(2,1)}, bf16[64,1024]{1,0:T(8,128)(2,1)}) custom-call(bf16[512,1024]{1,0:T(8,128)(2,1)} %copy-done.7, bf16[512,1024]{1,0:T(8,128)(2,1)} %copy-done.8, bf16[256,1792]{1,0:T(8,128)(2,1)} %copy-done.9, bf16[256,1792]{1,0:T(8,128)(2,1)} %copy-done.12, ...), custom_call_target="tpu_custom_call" | custom-call | flops 2415919104 | bytes 1048576 | tf_op jit(solution)/shard_map/forward_beside/pallas_call | solution.py:294
  71.5 3.3 %collective-permute-start.12 = (bf16[64,1024]{1,0:T(8,128)(2,1)}, bf16[64,1024]{1,0:T(8,128)(2,1)S(1)}, u32[]{:S(2)}, u32[]{:S(2)}) collective-permute-start(bf16[64,1024]{1,0:T(8,128)(2,1)} %get-tuple-element.10), channel_id=1, source_target_pairs={{0,1},{1,2},{2,3},{3,4},{4,5},{5,6},{6,7},{7,8},{8,9},{9,10},{10,1... | collective-permute-start | bytes 393224 | tf_op jit(solution)/shard_map/ppermute | solution.py:374
  74.8 5.4 %collective-permute-start.13 = (bf16[64,1024]{1,0:T(8,128)(2,1)}, bf16[64,1024]{1,0:T(8,128)(2,1)S(1)}, u32[]{:S(2)}, u32[]{:S(2)}) collective-permute-start(bf16[64,1024]{1,0:T(8,128)(2,1)} %get-tuple-element.11), channel_id=1, source_target_pairs={{1,0},{2,1},{3,2},{4,3},{5,4},{6,5},{7,6},{8,7},{9,8},{10,9},{11,1... | collective-permute-start | bytes 393224 | tf_op jit(solution)/shard_map/ppermute | solution.py:375
  80.4 5.9 %forward_same.1.own_ref = f32[64,1024]{1,0:T(8,128)} custom-call(bf16[512,1024]{1,0:T(8,128)(2,1)} %copy-done.7, bf16[512,1024]{1,0:T(8,128)(2,1)} %copy-done.8, bf16[1024,1792]{1,0:T(8,128)(2,1)} %get-tuple-element.9.refs_2_.matrix_ref.refs_3_), custom_call_target="tpu_custom_call" | custom-call | flops 1342177280 | bytes 1048576 | tf_op jit(solution)/shard_map/forward_same/pallas_call | solution.py:294
  88.0 1.9 %collective-permute-start.15 = (bf16[64,1024]{1,0:T(8,128)(2,1)S(1)}, bf16[64,1024]{1,0:T(8,128)(2,1)S(1)}, u32[]{:S(2)}, u32[]{:S(2)}) collective-permute-start(bf16[64,1024]{1,0:T(8,128)(2,1)S(1)} %get-tuple-element.13.grad_ref), channel_id=1, source_target_pairs={{0,1},{1,2},{2,3},{3,4},{4,5},{5,6},{6,7},{7,8},{8,9},{9,10},{10,1... | collective-permute-start | bytes 393224 | tf_op jit(solution)/shard_map/ppermute | solution.py:401
  89.9 6.6 %collective-permute-start.14 = (bf16[64,1024]{1,0:T(8,128)(2,1)S(1)}, bf16[64,1024]{1,0:T(8,128)(2,1)S(1)}, u32[]{:S(2)}, u32[]{:S(2)}) collective-permute-start(bf16[64,1024]{1,0:T(8,128)(2,1)S(1)} %get-tuple-element.13.grad_ref), channel_id=1, source_target_pairs={{1,0},{2,1},{3,2},{4,3},{5,4},{6,5},{7,6},{8,7},{9,8},{10,9},{11,1... | collective-permute-start | bytes 393224 | tf_op jit(solution)/shard_map/ppermute | solution.py:402
  96.6 2.7 %backward_same.1.refs_2_ = f32[1024,1024]{1,0:T(8,128)S(1)} custom-call(bf16[64,1024]{1,0:T(8,128)(2,1)S(1)} %get-tuple-element.13.grad_ref, bf16[1024,1792]{1,0:T(8,128)(2,1)S(1)} %copy-done), custom_call_target="tpu_custom_call" | custom-call | flops 1342177280 | bytes 1048576 | tf_op jit(solution)/shard_map/backward_same/pallas_call | solution.py:294
  99.3 3.1 %backward_far.1 = bf16[512,1024]{1,0:T(8,128)(2,1)S(1)} custom-call(bf16[64,1024]{1,0:T(8,128)(2,1)S(1)} %collective-permute-done.14.refs_0_, bf16[64,1024]{1,0:T(8,128)(2,1)S(1)} %collective-permute-done.15.refs_1_, f32[1024,1024]{1,0:T(8,128)S(1)} %backward_same.1.refs_2_, bf16[1024,1792]{1,0:T(8,128)(2,1)S(1)} %copy-done), custom_call_target="tpu_custom_call" | custom-call | flops 1207959552 | bytes 1048576 | tf_op jit(solution)/shard_map/backward_far/pallas_call | solution.py:294
  102.6 3.1 %backward_near.1 = bf16[512,1024]{1,0:T(8,128)(2,1)S(1)} custom-call(bf16[64,1024]{1,0:T(8,128)(2,1)S(1)} %collective-permute-done.14.refs_0_, bf16[64,1024]{1,0:T(8,128)(2,1)S(1)} %collective-permute-done.15.refs_1_, f32[1024,1024]{1,0:T(8,128)S(1)} %backward_same.1.refs_2_, bf16[1024,1792]{1,0:T(8,128)(2,1)S(1)} %copy-done), custom_call_target="tpu_custom_call" | custom-call | flops 1207959552 | bytes 1048576 | tf_op jit(solution)/shard_map/backward_near/pallas_call | solution.py:294
  109.8 1.8 %collective-permute-start.22 = (bf16[64,1024]{1,0:T(8,128)(2,1)S(1)}, bf16[64,1024]{1,0:T(8,128)(2,1)S(1)}, u32[]{:S(2)}, u32[]{:S(2)}) collective-permute-start(bf16[64,1024]{1,0:T(8,128)(2,1)S(1)} %get-tuple-element.19), channel_id=1, source_target_pairs={{0,64},{16,80},{32,96},{48,112},{64,0},{80,16},{96,32},{112,48},{1... | collective-permute-start | bytes 393224 | tf_op jit(solution)/shard_map/ppermute | solution.py:342
  112.4 2.6 %collective-permute-start.19 = (bf16[64,1024]{1,0:T(8,128)(2,1)S(1)}, bf16[64,1024]{1,0:T(8,128)(2,1)S(1)}, u32[]{:S(2)}, u32[]{:S(2)}) collective-permute-start(bf16[64,1024]{1,0:T(8,128)(2,1)S(1)} %get-tuple-element.15), channel_id=1, source_target_pairs={{0,96},{16,112},{32,0},{48,16},{64,32},{80,48},{96,64},{112,80},{1... | collective-permute-start | bytes 393224 | tf_op jit(solution)/shard_map/ppermute | solution.py:342
  115.6 2.3 %collective-permute-done.22 = bf16[64,1024]{1,0:T(8,128)(2,1)S(1)} collective-permute-done((bf16[64,1024]{1,0:T(8,128)(2,1)S(1)}, bf16[64,1024]{1,0:T(8,128)(2,1)S(1)}, u32[]{:S(2)}, u32[]{:S(2)}) %collective-permute-start.22) | collective-permute-done | bytes 131104 | tf_op jit(solution)/shard_map/ppermute | solution.py:342
  118.0 5.8 %collective-permute-start.24 = (bf16[64,1024]{1,0:T(8,128)(2,1)S(1)}, bf16[64,1024]{1,0:T(8,128)(2,1)S(1)}, u32[]{:S(2)}, u32[]{:S(2)}) collective-permute-start(bf16[64,1024]{1,0:T(8,128)(2,1)S(1)} %add_convert_fusion.1), channel_id=1, source_target_pairs={{0,128},{16,144},{32,160},{48,176},{64,192},{80,208},{96,224},{112... | collective-permute-start | bytes 393224 | tf_op jit(solution)/shard_map/ppermute | solution.py:432
  123.8 4.8 %collective-permute-done.24 = bf16[64,1024]{1,0:T(8,128)(2,1)S(1)} collective-permute-done((bf16[64,1024]{1,0:T(8,128)(2,1)S(1)}, bf16[64,1024]{1,0:T(8,128)(2,1)S(1)}, u32[]{:S(2)}, u32[]{:S(2)}) %collective-permute-start.24) | collective-permute-done | bytes 131104 | tf_op jit(solution)/shard_map/ppermute | solution.py:432
  (78 shorter events, 18.1 us)
Async XLA Ops:
  1.8 10.8 %collective-permute-start.2 = (bf16[64,1792]{1,0:T(8,128)(2,1)S(1)}, bf16[64,1792]{1,0:T(8,128)(2,1)S(1)}, u32[]{:S(2)}, u32[]{:S(2)}) collective-permute-start(bf16[64,1792]{1,0:T(8,128)(2,1)S(1)} %weights_transpose.1), channel_id=1, source_target_pairs={{0,3},{1,0},{2,1},{3,2},{4,7},{5,4},{6,5},{7,6},{8,11},{9,8},{10,9... | collective-permute-start | bytes 688136 | tf_op jit(solution)/shard_map/ppermute | solution.py:313
  6.5 19.0 %collective-permute-start.1 = (bf16[64,1792]{1,0:T(8,128)(2,1)S(1)}, bf16[64,1792]{1,0:T(8,128)(2,1)S(1)}, u32[]{:S(2)}, u32[]{:S(2)}) collective-permute-start(bf16[64,1792]{1,0:T(8,128)(2,1)S(1)} %weights_transpose.1), channel_id=1, source_target_pairs={{0,2},{1,3},{2,0},{3,1},{4,6},{5,7},{6,4},{7,5},{8,10},{9,11},{10,... | collective-permute-start | bytes 688136 | tf_op jit(solution)/shard_map/ppermute | solution.py:313
  6.5 19.0 %collective-permute-start = (bf16[64,1792]{1,0:T(8,128)(2,1)S(1)}, bf16[64,1792]{1,0:T(8,128)(2,1)S(1)}, u32[]{:S(2)}, u32[]{:S(2)}) collective-permute-start(bf16[64,1792]{1,0:T(8,128)(2,1)S(1)} %weights_transpose.1), channel_id=1, source_target_pairs={{0,1},{1,2},{2,3},{3,0},{4,5},{5,6},{6,7},{7,4},{8,9},{9,10},{10,1... | collective-permute-start | bytes 688136 | tf_op jit(solution)/shard_map/ppermute | solution.py:313
  25.6 21.5 %collective-permute-start.10 = (bf16[256,1792]{1,0:T(8,128)(2,1)S(1)}, bf16[256,1792]{1,0:T(8,128)(2,1)S(1)}, u32[]{:S(2)}, u32[]{:S(2)}) collective-permute-start(bf16[256,1792]{1,0:T(8,128)(2,1)S(1)} %pad_maximum_fusion.refs_2_), channel_id=1, source_target_pairs={{0,12},{1,13},{2,14},{3,15},{4,0},{5,1},{6,2},{7,3},{8,4},{9,5},{1... | collective-permute-start | bytes 2752520 | tf_op jit(solution)/shard_map/ppermute | solution.py:319
  26.1 22.4 %collective-permute-start.8 = (bf16[256,1792]{1,0:T(8,128)(2,1)S(1)}, bf16[256,1792]{1,0:T(8,128)(2,1)S(1)}, u32[]{:S(2)}, u32[]{:S(2)}) collective-permute-start(bf16[256,1792]{1,0:T(8,128)(2,1)S(1)} %pad_maximum_fusion.refs_2_), channel_id=1, source_target_pairs={{0,4},{1,5},{2,6},{3,7},{4,8},{5,9},{6,10},{7,11},{8,12},{9,13},{1... | collective-permute-start | bytes 2752520 | tf_op jit(solution)/shard_map/ppermute | solution.py:318
  27.7 10.5 %collective-permute-start.3 = (bf16[64,1024]{1,0:T(8,128)(2,1)S(1)}, bf16[64,1024]{1,0:T(8,128)(2,1)S(1)}, u32[]{:S(2)}, u32[]{:S(2)}) collective-permute-start(bf16[64,1024]{1,0:T(8,128)(2,1)S(1)} %bitcast.12), channel_id=1, source_target_pairs={{0,128},{16,144},{32,160},{48,176},{64,192},{80,208},{96,224},{112... | collective-permute-start | bytes 393224 | tf_op jit(solution)/shard_map/ppermute | solution.py:327
  38.2 11.6 %collective-permute-start.5 = (bf16[128,1024]{1,0:T(8,128)(2,1)S(1)}, bf16[128,1024]{1,0:T(8,128)(2,1)S(1)}, u32[]{:S(2)}, u32[]{:S(2)}) collective-permute-start(bf16[128,1024]{1,0:T(8,128)(2,1)S(1)} %pad_maximum_fusion.1), channel_id=1, source_target_pairs={{0,64},{16,80},{32,96},{48,112},{64,0},{80,16},{96,32},{112,48},{1... | collective-permute-start | bytes 786440 | tf_op jit(solution)/shard_map/ppermute | solution.py:330
  41.3 8.5 %collective-permute-start.4 = (bf16[128,1024]{1,0:T(8,128)(2,1)S(1)}, bf16[128,1024]{1,0:T(8,128)(2,1)S(1)}, u32[]{:S(2)}, u32[]{:S(2)}) collective-permute-start(bf16[128,1024]{1,0:T(8,128)(2,1)S(1)} %pad_maximum_fusion.1), channel_id=1, source_target_pairs={{0,32},{16,48},{32,64},{48,80},{64,96},{80,112},{96,0},{112,16},{1... | collective-permute-start | bytes 786440 | tf_op jit(solution)/shard_map/ppermute | solution.py:330
  41.9 8.0 %collective-permute-start.6 = (bf16[128,1024]{1,0:T(8,128)(2,1)S(1)}, bf16[128,1024]{1,0:T(8,128)(2,1)S(1)}, u32[]{:S(2)}, u32[]{:S(2)}) collective-permute-start(bf16[128,1024]{1,0:T(8,128)(2,1)S(1)} %pad_maximum_fusion.1), channel_id=1, source_target_pairs={{0,96},{16,112},{32,0},{48,16},{64,32},{80,48},{96,64},{112,80},{1... | collective-permute-start | bytes 786440 | tf_op jit(solution)/shard_map/ppermute | solution.py:330
  47.1 10.7 %collective-permute-start.11 = (bf16[128,1792]{1,0:T(8,128)(2,1)S(1)}, bf16[128,1792]{1,0:T(8,128)(2,1)S(1)}, u32[]{:S(2)}, u32[]{:S(2)}) collective-permute-start(bf16[128,1792]{1,0:T(8,128)(2,1)S(1)} %slice.81), channel_id=1, source_target_pairs={{0,12},{1,13},{2,14},{3,15},{4,0},{5,1},{6,2},{7,3},{8,4},{9,5},{1... | collective-permute-start | bytes 1376264 | tf_op jit(solution)/shard_map/ppermute | solution.py:321
  48.6 12.1 %collective-permute-start.9 = (bf16[128,1792]{1,0:T(8,128)(2,1)S(1)}, bf16[128,1792]{1,0:T(8,128)(2,1)S(1)}, u32[]{:S(2)}, u32[]{:S(2)}) collective-permute-start(bf16[128,1792]{1,0:T(8,128)(2,1)S(1)} %slice.80), channel_id=1, source_target_pairs={{0,4},{1,5},{2,6},{3,7},{4,8},{5,9},{6,10},{7,11},{8,12},{9,13},{1... | collective-permute-start | bytes 1376264 | tf_op jit(solution)/shard_map/ppermute | solution.py:320
  49.9 12.1 %collective-permute-start.7 = (bf16[512,1024]{1,0:T(8,128)(2,1)S(1)}, bf16[512,1024]{1,0:T(8,128)(2,1)S(1)}, u32[]{:S(2)}, u32[]{:S(2)}) collective-permute-start(bf16[512,1024]{1,0:T(8,128)(2,1)S(1)} %constant_dynamic-update-slice_fusion.refs_0_), channel_id=1, source_target_pairs={{0,16},{16,0},{32,48},{48,32},{64,80},{80,64},{96,112},{112,96},{1... | collective-permute-start | bytes 3145736 | tf_op jit(solution)/shard_map/ppermute | solution.py:332
  71.5 14.8 %collective-permute-start.12 = (bf16[64,1024]{1,0:T(8,128)(2,1)}, bf16[64,1024]{1,0:T(8,128)(2,1)S(1)}, u32[]{:S(2)}, u32[]{:S(2)}) collective-permute-start(bf16[64,1024]{1,0:T(8,128)(2,1)} %get-tuple-element.10), channel_id=1, source_target_pairs={{0,1},{1,2},{2,3},{3,4},{4,5},{5,6},{6,7},{7,8},{8,9},{9,10},{10,1... | collective-permute-start | bytes 393224 | tf_op jit(solution)/shard_map/ppermute | solution.py:374
  74.8 11.5 %collective-permute-start.13 = (bf16[64,1024]{1,0:T(8,128)(2,1)}, bf16[64,1024]{1,0:T(8,128)(2,1)S(1)}, u32[]{:S(2)}, u32[]{:S(2)}) collective-permute-start(bf16[64,1024]{1,0:T(8,128)(2,1)} %get-tuple-element.11), channel_id=1, source_target_pairs={{1,0},{2,1},{3,2},{4,3},{5,4},{6,5},{7,6},{8,7},{9,8},{10,9},{11,1... | collective-permute-start | bytes 393224 | tf_op jit(solution)/shard_map/ppermute | solution.py:375
  88.0 11.2 %collective-permute-start.15 = (bf16[64,1024]{1,0:T(8,128)(2,1)S(1)}, bf16[64,1024]{1,0:T(8,128)(2,1)S(1)}, u32[]{:S(2)}, u32[]{:S(2)}) collective-permute-start(bf16[64,1024]{1,0:T(8,128)(2,1)S(1)} %get-tuple-element.13.grad_ref), channel_id=1, source_target_pairs={{0,1},{1,2},{2,3},{3,4},{4,5},{5,6},{6,7},{7,8},{8,9},{9,10},{10,1... | collective-permute-start | bytes 393224 | tf_op jit(solution)/shard_map/ppermute | solution.py:401
  89.9 9.3 %collective-permute-start.14 = (bf16[64,1024]{1,0:T(8,128)(2,1)S(1)}, bf16[64,1024]{1,0:T(8,128)(2,1)S(1)}, u32[]{:S(2)}, u32[]{:S(2)}) collective-permute-start(bf16[64,1024]{1,0:T(8,128)(2,1)S(1)} %get-tuple-element.13.grad_ref), channel_id=1, source_target_pairs={{1,0},{2,1},{3,2},{4,3},{5,4},{6,5},{7,6},{8,7},{9,8},{10,9},{11,1... | collective-permute-start | bytes 393224 | tf_op jit(solution)/shard_map/ppermute | solution.py:402
  105.8 5.8 %collective-permute-start.16 = (bf16[256,1024]{1,0:T(8,128)(2,1)S(1)}, bf16[256,1024]{1,0:T(8,128)(2,1)S(1)}, u32[]{:S(2)}, u32[]{:S(2)}) collective-permute-start(bf16[256,1024]{1,0:T(8,128)(2,1)S(1)} %slice.83), channel_id=1, source_target_pairs={{0,16},{16,0},{32,48},{48,32},{64,80},{80,64},{96,112},{112,96},{1... | collective-permute-start | bytes 1572872 | tf_op jit(solution)/shard_map/ppermute | solution.py:337
  106.5 8.6 %collective-permute-start.21 = (bf16[64,1024]{1,0:T(8,128)(2,1)S(1)}, bf16[64,1024]{1,0:T(8,128)(2,1)S(1)}, u32[]{:S(2)}, u32[]{:S(2)}) collective-permute-start(bf16[64,1024]{1,0:T(8,128)(2,1)S(1)} %get-tuple-element.17), channel_id=1, source_target_pairs={{0,32},{16,48},{32,64},{48,80},{64,96},{80,112},{96,0},{112,16},{1... | collective-permute-start | bytes 393224 | tf_op jit(solution)/shard_map/ppermute | solution.py:342
  108.0 7.5 %collective-permute-start.23 = (bf16[64,1024]{1,0:T(8,128)(2,1)S(1)}, bf16[64,1024]{1,0:T(8,128)(2,1)S(1)}, u32[]{:S(2)}, u32[]{:S(2)}) collective-permute-start(bf16[64,1024]{1,0:T(8,128)(2,1)S(1)} %get-tuple-element.18), channel_id=1, source_target_pairs={{0,96},{16,112},{32,0},{48,16},{64,32},{80,48},{96,64},{112,80},{1... | collective-permute-start | bytes 393224 | tf_op jit(solution)/shard_map/ppermute | solution.py:342
  109.8 8.1 %collective-permute-start.22 = (bf16[64,1024]{1,0:T(8,128)(2,1)S(1)}, bf16[64,1024]{1,0:T(8,128)(2,1)S(1)}, u32[]{:S(2)}, u32[]{:S(2)}) collective-permute-start(bf16[64,1024]{1,0:T(8,128)(2,1)S(1)} %get-tuple-element.19), channel_id=1, source_target_pairs={{0,64},{16,80},{32,96},{48,112},{64,0},{80,16},{96,32},{112,48},{1... | collective-permute-start | bytes 393224 | tf_op jit(solution)/shard_map/ppermute | solution.py:342
  111.7 12.0 %collective-permute-start.17 = (bf16[64,1024]{1,0:T(8,128)(2,1)S(1)}, bf16[64,1024]{1,0:T(8,128)(2,1)S(1)}, u32[]{:S(2)}, u32[]{:S(2)}) collective-permute-start(bf16[64,1024]{1,0:T(8,128)(2,1)S(1)} %get-tuple-element.14), channel_id=1, source_target_pairs={{0,32},{16,48},{32,64},{48,80},{64,96},{80,112},{96,0},{112,16},{1... | collective-permute-start | bytes 393224 | tf_op jit(solution)/shard_map/ppermute | solution.py:342
  112.4 11.3 %collective-permute-start.19 = (bf16[64,1024]{1,0:T(8,128)(2,1)S(1)}, bf16[64,1024]{1,0:T(8,128)(2,1)S(1)}, u32[]{:S(2)}, u32[]{:S(2)}) collective-permute-start(bf16[64,1024]{1,0:T(8,128)(2,1)S(1)} %get-tuple-element.15), channel_id=1, source_target_pairs={{0,96},{16,112},{32,0},{48,16},{64,32},{80,48},{96,64},{112,80},{1... | collective-permute-start | bytes 393224 | tf_op jit(solution)/shard_map/ppermute | solution.py:342
  115.1 8.7 %collective-permute-start.18 = (bf16[64,1024]{1,0:T(8,128)(2,1)S(1)}, bf16[64,1024]{1,0:T(8,128)(2,1)S(1)}, u32[]{:S(2)}, u32[]{:S(2)}) collective-permute-start(bf16[64,1024]{1,0:T(8,128)(2,1)S(1)} %get-tuple-element.16), channel_id=1, source_target_pairs={{0,64},{16,80},{32,96},{48,112},{64,0},{80,16},{96,32},{112,48},{1... | collective-permute-start | bytes 393224 | tf_op jit(solution)/shard_map/ppermute | solution.py:342
  118.0 10.6 %collective-permute-start.24 = (bf16[64,1024]{1,0:T(8,128)(2,1)S(1)}, bf16[64,1024]{1,0:T(8,128)(2,1)S(1)}, u32[]{:S(2)}, u32[]{:S(2)}) collective-permute-start(bf16[64,1024]{1,0:T(8,128)(2,1)S(1)} %add_convert_fusion.1), channel_id=1, source_target_pairs={{0,128},{16,144},{32,160},{48,176},{64,192},{80,208},{96,224},{112... | collective-permute-start | bytes 393224 | tf_op jit(solution)/shard_map/ppermute | solution.py:432
  (15 other events, 127.3 us)

commit v3 on v2

v3 whole, which is shorter than its diff:
```python
import functools

import jax
import jax.numpy as jnp
from jax import lax
from jax.experimental import pallas as pl
from jax.experimental.pallas import tpu as pltpu
from jax.sharding import PartitionSpec as P

HH = 32
WW = 32
CELLS = HH * WW
TAPS = 27
SLOT_TAPS = [*range(9, 18), None, *range(0, 9), *range(18, 27)]
SLOTS = 28
BLOCK = 64
COLS = SLOTS * BLOCK
SAME = 10 * BLOCK
BESIDE = COLS - SAME
BLOCKS = 16
CHANNELS = BLOCKS * BLOCK

ZH, XN, CN = 2, 4, 2
YN, ZN = 4, 4

BF16 = jnp.bfloat16
F32 = jnp.float32


def filt_index(zh, x, c):
    return (zh * XN + x) * CN + c


FILT = [(zh, x, c) for zh in range(ZH) for x in range(XN) for c in range(CN)]
SLAB = [(y, z) for y in range(YN) for z in range(ZN)]
TO_CORE = [(filt_index(*d), filt_index(d[0], d[1], 1 - d[2])) for d in FILT]
TO_ZHI = [(filt_index(*d), filt_index(1 - d[0], d[1], d[2])) for d in FILT]


def to_x(k):
    return [(filt_index(*d), filt_index(d[0], (d[1] + k) % XN, d[2])) for d in FILT]


def to_y(k):
    return [(y * ZN + z, ((y + k) % YN) * ZN + z) for y, z in SLAB]


def to_z(k):
    return [(y * ZN + z, y * ZN + (z + k) % ZN) for y, z in SLAB]


UP = [(i, i + 1) for i in range(YN * ZN - 1)]
DOWN = [(i + 1, i) for i in range(YN * ZN - 1)]

VMEM = pl.BlockSpec(memory_space=pltpu.VMEM)
ANY = pl.BlockSpec(memory_space=pl.ANY)


def transpose_kernel(w_ref, out_ref):
    for pair in range(0, SLOTS, 2):
        parts = []
        for slot in (pair, pair + 1):
            tap = SLOT_TAPS[slot]
            if tap is None:
                parts.append(jnp.zeros((BLOCK, BLOCK), F32))
            else:
                parts.append(w_ref[tap * BLOCK : (tap + 1) * BLOCK, :].astype(F32))
        turned = jnp.concatenate(parts, axis=0).T
        out_ref[:, pair * BLOCK : (pair + 2) * BLOCK] = turned.astype(BF16)


def filt_position():
    mine = lax.axis_index("filt")
    return mine // (XN * CN), (mine // CN) % XN, mine % CN


def slab_position():
    mine = lax.axis_index("slab")
    return mine // ZN, mine % ZN


def rows_of(block):
    return pl.ds(pl.multiple_of(block * BLOCK, BLOCK), BLOCK)


def assemble_weights(pieces, same_ref, beside_ref):
    y, z = slab_position()
    half = BLOCK // 2
    for step_y in range(YN):
        for step_z in range(ZN):
            group, index = (0, 0) if step_z == 0 else (5, step_z - 1)
            block = ((y + YN - step_y) % YN) * ZN + (z + ZN - step_z) % ZN
            for part in range(2):
                start = index * BLOCK + part * half
                if step_y == 2:
                    middle = half if step_z == 0 else 3 * half
                    ref = pieces[group + (2 if start < middle else 3)]
                    start %= middle
                else:
                    ref = pieces[group + {0: 0, 1: 1, 3: 4}[step_y]]
                rows = pl.ds(pl.multiple_of(block * BLOCK + part * half, half), half)
                same_ref[rows, :] = ref[start : start + half, :SAME]
                beside_ref[rows, :] = ref[start : start + half, SAME:]


def assemble_inputs(pieces, x_ref):
    zh, x, c = filt_position()
    for other in range(CN):
        for step in range(XN):
            for far in range(ZH):
                core = c if other == 0 else 1 - c
                high = zh if far == 0 else 1 - zh
                block = filt_index(high, (x + XN - step) % XN, core)
                start = (step * ZH + far) * BLOCK
                x_ref[rows_of(block), :] = pieces[other][start : start + BLOCK, :]


def shifted_sum(y_scr, first, base):
    cell = lax.broadcasted_iota(jnp.int32, (8, CELLS), 1)
    column = cell % WW
    row_ok = {0: cell >= WW, 2: cell < CELLS - WW}
    col_ok = {0: column >= 1, 2: column < WW - 1}
    total = None
    for col in range(3):
        lane = None
        for row in range(3):
            value = y_scr[pl.ds((first + 3 * row + col) * BLOCK + base, 8), :]
            if row != 1:
                value = pltpu.roll(value, ((1 - row) * WW) % CELLS, 1)
                value = jnp.where(row_ok[row], value, 0.0)
            lane = value if lane is None else lane + value
        if col != 1:
            lane = pltpu.roll(lane, (1 - col) % CELLS, 1)
            lane = jnp.where(col_ok[col], lane, 0.0)
        total = lane if total is None else total + lane
    return total


def convolve(planes, w, x, out_refs, y_scr):
    y_scr[...] = lax.dot_general(w, x, (((0,), (0,)), ((), ())), preferred_element_type=F32)

    def body(part, carry):
        base = pl.multiple_of(part * 8, 8)
        for first, out in zip(planes, out_refs):
            out[pl.ds(base, 8), :] = shifted_sum(y_scr, first, base).astype(out.dtype)
        return carry

    lax.fori_loop(0, BLOCK // 8, body, 0)


def forward_beside_kernel(*refs):
    x_pieces, w_pieces = refs[:2], refs[2:12]
    x_ref, same_ref, beside_ref, up_ref, down_ref, w_scr, y_scr, sem = refs[13:]
    assemble_inputs(x_pieces, x_ref)
    assemble_weights(w_pieces, same_ref, w_scr)
    keep = pltpu.make_async_copy(w_scr, beside_ref, sem)
    keep.start()
    convolve((0, 9), w_scr[...], x_ref[...], (up_ref, down_ref), y_scr)
    keep.wait()


def ready_kernel(*refs):
    refs[-1][...] = jnp.zeros((8, 128), BF16)


def forward_same_kernel(x_ref, same_ref, own_ref, y_scr):
    convolve((0,), same_ref[...], x_ref[...], (own_ref,), y_scr)


def pointwise_kernel(own_ref, below_ref, above_ref, bias_ref, cot_ref, act_ref, grad_ref):
    preact = (
        own_ref[...]
        + below_ref[...].astype(F32)
        + above_ref[...].astype(F32)
        + bias_ref[...].astype(F32)
    )
    sig = jax.nn.sigmoid(preact)
    act_ref[...] = (preact * sig).astype(BF16)
    slope = sig * (1.0 + preact * (1.0 - sig))
    grad_ref[...] = (cot_ref[...].astype(F32) * slope).astype(BF16)


def stack_taps(grad_refs, g_scr):
    cell = lax.broadcasted_iota(jnp.int32, (16, CELLS), 1)
    column = cell % WW
    row_ok = {2: cell >= WW, 0: cell < CELLS - WW}
    col_ok = {2: column >= 1, 0: column < WW - 1}

    def body(part, carry):
        base = pl.multiple_of(part * 16, 16)
        for at, grad in enumerate(grad_refs):
            plane = grad[pl.ds(base, 16), :].astype(F32)
            for col in range(3):
                lane = plane
                if col != 1:
                    lane = pltpu.roll(lane, (col - 1) % CELLS, 1)
                    lane = jnp.where(col_ok[col], lane, 0.0)
                for row in range(3):
                    value = lane
                    if row != 1:
                        value = pltpu.roll(value, ((row - 1) * WW) % CELLS, 1)
                        value = jnp.where(row_ok[row], value, 0.0)
                    slot = 9 * at + 3 * row + col
                    g_scr[pl.ds(slot * BLOCK + base, 16), :] = value.astype(BF16)
        return carry

    lax.fori_loop(0, BLOCK // 16, body, 0)


def backward_same_kernel(grad_ref, w_ref, out_ref, g_scr):
    stack_taps([grad_ref], g_scr)
    g_scr[9 * BLOCK :, :] = jnp.zeros((BLOCK, CELLS), BF16)
    half = CHANNELS // 2
    for start in (0, half):
        out_ref[start : start + half, :] = jnp.dot(
            w_ref[start : start + half, :], g_scr[...], preferred_element_type=F32
        )


def backward_beside_kernel(far, above_ref, below_ref, same_ref, w_ref, out_ref, g_scr):
    zh, x, c = filt_position()
    size = CHANNELS // 2
    first = pl.multiple_of(((zh + far) % ZH) * size, size)
    stack_taps([above_ref, below_ref], g_scr)
    total = same_ref[pl.ds(first, size), :] + jnp.dot(
        w_ref[pl.ds(first, size), :], g_scr[...], preferred_element_type=F32
    )
    total = total.astype(BF16)
    for at in range(size // BLOCK):
        along, core = at // CN, at % CN
        place = (core + c) % CN * XN + (along + XN - x) % XN
        out_ref[rows_of(place), :] = total[at * BLOCK : (at + 1) * BLOCK, :]


def shape(rows, columns, dtype=BF16):
    return jax.ShapeDtypeStruct((rows, columns), dtype)


def call(kernel, name, outs, scratch, columns, operands, in_any=(), out_any=(), limit=24):
    cost = None
    if columns:
        cost = pl.CostEstimate(
            flops=2 * columns * CHANNELS * CELLS, bytes_accessed=2**20, transcendentals=0
        )
    return pl.pallas_call(
        kernel,
        out_shape=outs,
        in_specs=[ANY if at in in_any else VMEM for at in range(len(operands))],
        out_specs=tuple(ANY if at in out_any else VMEM for at in range(len(outs))),
        scratch_shapes=scratch,
        compiler_params=pltpu.CompilerParams(vmem_limit_bytes=limit * 2**20),
        cost_estimate=cost,
        name=name,
    )(*operands)


def gather_weights(weights):
    taps_first = jnp.transpose(weights, (1, 0, 2)).reshape(TAPS * BLOCK, BLOCK)
    (own,) = call(
        transpose_kernel, "weights_transpose", (shape(BLOCK, COLS),), [], 0, [taps_first]
    )
    beside = [lax.ppermute(own, "slab", to_z(k)) for k in range(1, ZN)]
    pieces = along_y(own)
    line = jnp.concatenate(beside, axis=0)
    return pieces + along_y(once(line, pieces[2], pieces[3]))


def once(value, *others):
    return lax.optimization_barrier((value, *others))[0]


def along_y(line):
    half = line.shape[0] // 2
    before = lax.ppermute(line, "slab", to_y(1))
    after = lax.ppermute(line, "slab", to_y(-1))
    first = lax.ppermute(before[:half], "slab", to_y(1))
    second = lax.ppermute(after[half:], "slab", to_y(-1))
    return [line, before, first, second, after]


def gather_inputs(inputs, w_pieces):
    far = lax.ppermute(once(inputs, w_pieces[5]), "filt", TO_ZHI)
    pair = jnp.concatenate([inputs, far], axis=0)
    row = jnp.concatenate(
        [pair] + [lax.ppermute(pair, "filt", to_x(k)) for k in range(1, XN)], axis=0
    )
    return [row, lax.ppermute(row, "filt", TO_CORE)]


def sum_over_row(part):
    size = part.shape[0] // 2
    received = lax.ppermute(part[size:], "filt", TO_CORE)
    sums = []
    for k in range(XN):
        rows = slice(k * BLOCK, (k + 1) * BLOCK)
        sums.append((part[rows].astype(F32) + received[rows].astype(F32)).astype(BF16))
    arrived = [lax.ppermute(sums[k], "filt", to_x(k)) for k in range(1, XN)]
    result = sums[0].astype(F32)
    for piece in arrived:
        result = result + piece.astype(F32)
    return result


def local(inputs, weights, bias, cotangent):
    w_pieces = gather_weights(weights)
    x_pieces = gather_inputs(inputs.reshape(BLOCK, CELLS), w_pieces)
    (ready,) = call(
        ready_kernel, "weights_ready", (shape(8, 128),), [], 7168, w_pieces[7:9], in_any=range(2)
    )
    channels, same_taps, beside_taps, up, down = call(
        forward_beside_kernel,
        "forward_beside",
        (
            shape(CHANNELS, CELLS),
            shape(CHANNELS, SAME),
            shape(CHANNELS, BESIDE),
            shape(BLOCK, CELLS),
            shape(BLOCK, CELLS),
        ),
        [
            pltpu.VMEM((CHANNELS, BESIDE), BF16),
            pltpu.VMEM((BESIDE, CELLS), F32),
            pltpu.SemaphoreType.DMA,
        ],
        BESIDE,
        x_pieces + w_pieces + [ready],
        in_any=(12,),
        out_any=(2,),
        limit=46,
    )
    below = lax.ppermute(up, "slab", UP)
    above = lax.ppermute(down, "slab", DOWN)
    (own,) = call(
        forward_same_kernel,
        "forward_same",
        (shape(BLOCK, CELLS, F32),),
        [pltpu.VMEM((SAME, CELLS), F32)],
        SAME,
        [channels, same_taps],
    )
    activated, grad = call(
        pointwise_kernel,
        "silu_and_slope",
        (shape(BLOCK, CELLS), shape(BLOCK, CELLS)),
        [],
        0,
        [own, below, above, bias.reshape(BLOCK, 1), cotangent.reshape(BLOCK, CELLS)],
    )
    grad_below = lax.ppermute(grad, "slab", UP)
    grad_above = lax.ppermute(grad, "slab", DOWN)
    (same,) = call(
        backward_same_kernel,
        "backward_same",
        (shape(CHANNELS, CELLS, F32),),
        [pltpu.VMEM((SAME, CELLS), BF16)],
        SAME,
        [grad, same_taps],
    )
    sums = []
    for far, name in ((1, "backward_far"), (0, "backward_near")):
        (part,) = call(
            functools.partial(backward_beside_kernel, far),
            name,
            (shape(CHANNELS // 2, CELLS),),
            [pltpu.VMEM((BESIDE, CELLS), BF16)],
            BESIDE // 2,
            [grad_above, grad_below, same, beside_taps],
        )
        sums.append(sum_over_row(part))
    arrived = lax.ppermute(sums[0].astype(BF16), "filt", TO_ZHI)
    input_grad = (sums[1] + arrived.astype(F32)).astype(BF16)
    return activated.reshape(cotangent.shape), input_grad.reshape(inputs.shape)


def solution(mesh):
    return jax.shard_map(
        local,
        mesh=mesh,
        in_specs=(
            P("filt", "slab", None),
            P("filt", None, "slab"),
            P("filt"),
            P("filt", "slab", None),
        ),
        out_specs=(P("filt", "slab", None), P("filt", "slab", None)),
        check_vma=False,
    )
```

time: 130 us -> 123 us (0.946)
  waiting for transfers between devices: 43.7 us -> 37.2 us
  starting transfers between devices: 54.6 us -> 60.8 us
  Pallas kernels: 24.3 us -> 18.9 us
  local copies, waits for them, and re-layouts: 4.62 us -> 2.94 us
    ppermute x8 -> x12, waiting for transfers between devices: 36.1 us -> 19.1 us  [the longest x3 11.2 us: gather_weights(): beside = [lax.ppermute(own, 'slab', to_z(k)) for k in range(1, ZN)]]
    ppermute x1, starting transfers between devices: 3.3 us -> 10.1 us  [local(): below = lax.ppermute(up, 'slab', UP)]
    ppermute x8 -> x12, starting transfers between devices: 15.4 us -> 21.9 us  [the longest x1 6.12 us: gather_inputs(): far = lax.ppermute(once(inputs, w_pieces[5]), 'filt', TO_ZHI)]
    pallas_call x8, Pallas kernels: 24.3 us -> 18.9 us  [call(): pl.pallas_call(kernel, out_shape=outs, in_specs=[ANY if at in in_any else...]
    ppermute x1, waiting for transfers between devices: 0.01 us -> 5.07 us  [local(): grad_below = lax.ppermute(grad, 'slab', UP)]
    ppermute x1, starting transfers between devices: 5.42 us -> 1.92 us  [local(): above = lax.ppermute(down, 'slab', DOWN)]
    ppermute x3, waiting for transfers between devices: 0.46 us -> 2.92 us  [gather_inputs(): lax.ppermute(pair, 'filt', to_x(k))]
    ppermute x1, starting transfers between devices: 5.79 us -> 3.55 us  [local(): arrived = lax.ppermute(sums[0].astype(BF16), 'filt', TO_ZHI)]
  transfers between devices with their start and end apart: 25 -> 29, of which waited for: 10 -> 15; matrix products, arithmetic and copies ran while one was open for 1% -> 1% of each run, Pallas kernels for 9% -> 7%
where the time goes in v3:
time: 123 us; the launch traced here: 122 us
  starting transfers between devices  60.8 us (49%)
  waiting for transfers between devices  37.2 us (30%)
  Pallas kernels  18.9 us (15%)
  local copies, waits for them, and re-layouts  2.94 us (2%)
    pallas_call x8, Pallas kernels, call(): pl.pallas_call(kernel, out_shape=outs, in_specs=[ANY if at in in_any else...  18.9 us
    ppermute x3, waiting for transfers between devices, gather_weights(): beside = [lax.ppermute(own, 'slab', to_z(k)) for k in range(1, ZN)]  11.2 us
    ppermute x1, starting transfers between devices, local(): below = lax.ppermute(up, 'slab', UP)  10.1 us
    ppermute x6, starting transfers between devices, sum_over_row(): arrived = [lax.ppermute(sums[k], 'filt', to_x(k)) for k in range(1, XN)]  8.95 us
    ppermute x1, waiting for transfers between devices, local(): arrived = lax.ppermute(sums[0].astype(BF16), 'filt', TO_ZHI)  6.46 us
    ppermute x1, starting transfers between devices, gather_inputs(): far = lax.ppermute(once(inputs, w_pieces[5]), 'filt', TO_ZHI)  6.12 us
    ppermute x3, starting transfers between devices, gather_weights(): beside = [lax.ppermute(own, 'slab', to_z(k)) for k in range(1, ZN)]  5.95 us
    ppermute x3, starting transfers between devices, gather_inputs(): lax.ppermute(pair, 'filt', to_x(k))  5.81 us
  transfers between devices with their start and end apart: 29, of which 15 were waited for; matrix products, arithmetic and copies ran while one was open for 1% of the time, Pallas kernels for 7%

profile of v3, /device:TPU:8, one launch (start us, length us, event | category | flops | bytes accessed | tf_op | source)
XLA Modules:
  0.0 121.9 jit_solution(529252124348429994)
XLA Ops:
  4.2 1.7 %collective-permute-start = (bf16[64,1792]{1,0:T(8,128)(2,1)S(1)}, bf16[64,1792]{1,0:T(8,128)(2,1)S(1)}, u32[]{:S(2)}, u32[]{:S(2)}) collective-permute-start(bf16[64,1792]{1,0:T(8,128)(2,1)S(1)} %weights_transpose.1.refs_2_), channel_id=1, source_target_pairs={{0,1},{1,2},{2,3},{3,0},{4,5},{5,6},{6,7},{7,4},{8,9},{9,10},{10,1... | collective-permute-start | bytes 688136 | tf_op jit(solution)/shard_map/ppermute | solution.py:262
  5.9 3.3 %collective-permute-start.1 = (bf16[64,1792]{1,0:T(8,128)(2,1)S(1)}, bf16[64,1792]{1,0:T(8,128)(2,1)S(1)}, u32[]{:S(2)}, u32[]{:S(2)}) collective-permute-start(bf16[64,1792]{1,0:T(8,128)(2,1)S(1)} %weights_transpose.1.refs_2_), channel_id=1, source_target_pairs={{0,2},{1,3},{2,0},{3,1},{4,6},{5,7},{6,4},{7,5},{8,10},{9,11},{10,... | collective-permute-start | bytes 688136 | tf_op jit(solution)/shard_map/ppermute | solution.py:262
  12.3 2.9 %collective-permute-done = bf16[64,1792]{1,0:T(8,128)(2,1)S(1)} collective-permute-done((bf16[64,1792]{1,0:T(8,128)(2,1)S(1)}, bf16[64,1792]{1,0:T(8,128)(2,1)S(1)}, u32[]{:S(2)}, u32[]{:S(2)}) %collective-permute-start) | collective-permute-done | bytes 229408 | tf_op jit(solution)/shard_map/ppermute | solution.py:262
  15.2 8.4 %collective-permute-done.1 = bf16[64,1792]{1,0:T(8,128)(2,1)S(1)} collective-permute-done((bf16[64,1792]{1,0:T(8,128)(2,1)S(1)}, bf16[64,1792]{1,0:T(8,128)(2,1)S(1)}, u32[]{:S(2)}, u32[]{:S(2)}) %collective-permute-start.1) | collective-permute-done | bytes 229408 | tf_op jit(solution)/shard_map/ppermute | solution.py:262
  25.7 6.1 %collective-permute-start.7 = (bf16[64,1024]{1,0:T(8,128)(2,1)S(1)}, bf16[64,1024]{1,0:T(8,128)(2,1)S(1)}, u32[]{:S(2)}, u32[]{:S(2)}) collective-permute-start(bf16[64,1024]{1,0:T(8,128)(2,1)S(1)} %bitcast.12), channel_id=1, source_target_pairs={{0,128},{16,144},{32,160},{48,176},{64,192},{80,208},{96,224},{112... | collective-permute-start | bytes 393224 | tf_op jit(solution)/shard_map/ppermute | solution.py:282
  31.9 5.3 %collective-permute-done.7 = bf16[64,1024]{1,0:T(8,128)(2,1)S(1)} collective-permute-done((bf16[64,1024]{1,0:T(8,128)(2,1)S(1)}, bf16[64,1024]{1,0:T(8,128)(2,1)S(1)}, u32[]{:S(2)}, u32[]{:S(2)}) %collective-permute-start.7) | collective-permute-done | bytes 131104 | tf_op jit(solution)/shard_map/ppermute | solution.py:282
  38.8 2.7 %collective-permute-start.9 = (bf16[128,1024]{1,0:T(8,128)(2,1)S(1)}, bf16[128,1024]{1,0:T(8,128)(2,1)S(1)}, u32[]{:S(2)}, u32[]{:S(2)}) collective-permute-start(bf16[128,1024]{1,0:T(8,128)(2,1)S(1)} %pad_maximum_fusion.1), channel_id=1, source_target_pairs={{0,64},{16,80},{32,96},{48,112},{64,0},{80,16},{96,32},{112,48},{1... | collective-permute-start | bytes 786440 | tf_op jit(solution)/shard_map/ppermute | solution.py:285
  46.5 2.8 %collective-permute-done.9 = bf16[128,1024]{1,0:T(8,128)(2,1)S(1)} collective-permute-done((bf16[128,1024]{1,0:T(8,128)(2,1)S(1)}, bf16[128,1024]{1,0:T(8,128)(2,1)S(1)}, u32[]{:S(2)}, u32[]{:S(2)}) %collective-permute-start.9) | collective-permute-done | bytes 262176 | tf_op jit(solution)/shard_map/ppermute | solution.py:285
  49.6 1.8 %collective-permute-done.13.refs_0_.refs_9_ = bf16[96,1792]{1,0:T(8,128)(2,1)S(1)} collective-permute-done((bf16[96,1792]{1,0:T(8,128)(2,1)S(1)}, bf16[96,1792]{1,0:T(8,128)(2,1)S(1)}, u32[]{:S(2)}, u32[]{:S(2)}) %collective-permute-start.13) | collective-permute-done | bytes 344096 | tf_op jit(solution)/shard_map/ppermute | solution.py:276
  52.2 6.4 %forward_beside.1 = (bf16[1024,1024]{1,0:T(8,128)(2,1)}, bf16[1024,640]{1,0:T(8,128)(2,1)S(1)}, bf16[1024,1152]{1,0:T(8,128)(2,1)}, bf16[64,1024]{1,0:T(8,128)(2,1)S(1)}, bf16[64,1024]{1,0:T(8,128)(2,1)S(1)}) custom-call(bf16[512,1024]{1,0:T(8,128)(2,1)S(1)} %constant_dynamic-update-slice_fusion.refs_0_, ...), custom_call_target="tpu_custom_call" | custom-call | flops 2415919104 | bytes 1048576 | tf_op jit(solution)/shard_map/forward_beside/pallas_call | solution.py:245
  58.7 10.1 %collective-permute-start.16 = (bf16[64,1024]{1,0:T(8,128)(2,1)S(1)}, bf16[64,1024]{1,0:T(8,128)(2,1)S(1)}, u32[]{:S(2)}, u32[]{:S(2)}) collective-permute-start(bf16[64,1024]{1,0:T(8,128)(2,1)S(1)} %get-tuple-element.15), channel_id=1, source_target_pairs={{0,1},{1,2},{2,3},{3,4},{4,5},{5,6},{6,7},{7,8},{8,9},{9,10},{10,1... | collective-permute-start | bytes 393224 | tf_op jit(solution)/shard_map/ppermute | solution.py:331
  68.8 1.9 %collective-permute-start.17 = (bf16[64,1024]{1,0:T(8,128)(2,1)S(1)}, bf16[64,1024]{1,0:T(8,128)(2,1)S(1)}, u32[]{:S(2)}, u32[]{:S(2)}) collective-permute-start(bf16[64,1024]{1,0:T(8,128)(2,1)S(1)} %get-tuple-element.16), channel_id=1, source_target_pairs={{1,0},{2,1},{3,2},{4,3},{5,4},{6,5},{7,6},{8,7},{9,8},{10,9},{11,1... | collective-permute-start | bytes 393224 | tf_op jit(solution)/shard_map/ppermute | solution.py:332
  72.4 2.9 %forward_same.1.own_ref = f32[64,1024]{1,0:T(8,128)S(1)} custom-call(bf16[1024,1024]{1,0:T(8,128)(2,1)S(1)} %copy-done.3, bf16[1024,640]{1,0:T(8,128)(2,1)S(1)} %get-tuple-element.14.same_ref.w_ref), custom_call_target="tpu_custom_call" | custom-call | flops 1342177280 | bytes 1048576 | tf_op jit(solution)/shard_map/forward_same/pallas_call | solution.py:245
  76.7 5.8 %collective-permute-start.18 = (bf16[64,1024]{1,0:T(8,128)(2,1)S(1)}, bf16[64,1024]{1,0:T(8,128)(2,1)S(1)}, u32[]{:S(2)}, u32[]{:S(2)}) collective-permute-start(bf16[64,1024]{1,0:T(8,128)(2,1)S(1)} %get-tuple-element.18.grad_ref), channel_id=1, source_target_pairs={{1,0},{2,1},{3,2},{4,3},{5,4},{6,5},{7,6},{8,7},{9,8},{10,9},{11,1... | collective-permute-start | bytes 393224 | tf_op jit(solution)/shard_map/ppermute | solution.py:350
  82.5 1.9 %collective-permute-start.19 = (bf16[64,1024]{1,0:T(8,128)(2,1)S(1)}, bf16[64,1024]{1,0:T(8,128)(2,1)S(1)}, u32[]{:S(2)}, u32[]{:S(2)}) collective-permute-start(bf16[64,1024]{1,0:T(8,128)(2,1)S(1)} %get-tuple-element.18.grad_ref), channel_id=1, source_target_pairs={{0,1},{1,2},{2,3},{3,4},{4,5},{5,6},{6,7},{7,8},{8,9},{9,10},{10,1... | collective-permute-start | bytes 393224 | tf_op jit(solution)/shard_map/ppermute | solution.py:349
  84.4 2.5 %backward_same.1.same_ref = f32[1024,1024]{1,0:T(8,128)S(1)} custom-call(bf16[64,1024]{1,0:T(8,128)(2,1)S(1)} %get-tuple-element.18.grad_ref, bf16[1024,640]{1,0:T(8,128)(2,1)S(1)} %get-tuple-element.14.same_ref.w_ref), custom_call_target="tpu_custom_call" | custom-call | flops 1342177280 | bytes 1048576 | tf_op jit(solution)/shard_map/backward_same/pallas_call | solution.py:245
  87.0 5.1 %collective-permute-done.19.below_ref = bf16[64,1024]{1,0:T(8,128)(2,1)S(1)} collective-permute-done((bf16[64,1024]{1,0:T(8,128)(2,1)S(1)}, bf16[64,1024]{1,0:T(8,128)(2,1)S(1)}, u32[]{:S(2)}, u32[]{:S(2)}) %collective-permute-start.19) | collective-permute-done | bytes 131104 | tf_op jit(solution)/shard_map/ppermute | solution.py:349
  92.0 3.0 %backward_far.1 = bf16[512,1024]{1,0:T(8,128)(2,1)S(1)} custom-call(bf16[64,1024]{1,0:T(8,128)(2,1)S(1)} %collective-permute-done.18.above_ref, bf16[64,1024]{1,0:T(8,128)(2,1)S(1)} %collective-permute-done.19.below_ref, f32[1024,1024]{1,0:T(8,128)S(1)} %backward_same.1.same_ref, bf16[1024,1152]{1,0:T(8,128)(2,1)S(1)} %copy-done), custom_call_target="tpu_custom_call" | custom-call | flops 1207959552 | bytes 1048576 | tf_op jit(solution)/shard_map/backward_far/pallas_call | solution.py:245
  95.2 3.0 %backward_near.1 = bf16[512,1024]{1,0:T(8,128)(2,1)S(1)} custom-call(bf16[64,1024]{1,0:T(8,128)(2,1)S(1)} %collective-permute-done.18.above_ref, bf16[64,1024]{1,0:T(8,128)(2,1)S(1)} %collective-permute-done.19.below_ref, f32[1024,1024]{1,0:T(8,128)S(1)} %backward_same.1.same_ref, bf16[1024,1152]{1,0:T(8,128)(2,1)S(1)} %copy-done), custom_call_target="tpu_custom_call" | custom-call | flops 1207959552 | bytes 1048576 | tf_op jit(solution)/shard_map/backward_near/pallas_call | solution.py:245
  100.5 2.3 %collective-permute-start.26 = (bf16[64,1024]{1,0:T(8,128)(2,1)S(1)}, bf16[64,1024]{1,0:T(8,128)(2,1)S(1)}, u32[]{:S(2)}, u32[]{:S(2)}) collective-permute-start(bf16[64,1024]{1,0:T(8,128)(2,1)S(1)} %get-tuple-element.25), channel_id=1, source_target_pairs={{0,64},{16,80},{32,96},{48,112},{64,0},{80,16},{96,32},{112,48},{1... | collective-permute-start | bytes 393224 | tf_op jit(solution)/shard_map/ppermute | solution.py:297
  106.2 1.8 %collective-permute-start.23 = (bf16[64,1024]{1,0:T(8,128)(2,1)S(1)}, bf16[64,1024]{1,0:T(8,128)(2,1)S(1)}, u32[]{:S(2)}, u32[]{:S(2)}) collective-permute-start(bf16[64,1024]{1,0:T(8,128)(2,1)S(1)} %get-tuple-element.21), channel_id=1, source_target_pairs={{0,96},{16,112},{32,0},{48,16},{64,32},{80,48},{96,64},{112,80},{1... | collective-permute-start | bytes 393224 | tf_op jit(solution)/shard_map/ppermute | solution.py:297
  108.1 1.8 %collective-permute-done.26 = bf16[64,1024]{1,0:T(8,128)(2,1)S(1)} collective-permute-done((bf16[64,1024]{1,0:T(8,128)(2,1)S(1)}, bf16[64,1024]{1,0:T(8,128)(2,1)S(1)}, u32[]{:S(2)}, u32[]{:S(2)}) %collective-permute-start.26) | collective-permute-done | bytes 131104 | tf_op jit(solution)/shard_map/ppermute | solution.py:297
  110.9 3.5 %collective-permute-start.28 = (bf16[64,1024]{1,0:T(8,128)(2,1)S(1)}, bf16[64,1024]{1,0:T(8,128)(2,1)S(1)}, u32[]{:S(2)}, u32[]{:S(2)}) collective-permute-start(bf16[64,1024]{1,0:T(8,128)(2,1)S(1)} %add_convert_fusion.1), channel_id=1, source_target_pairs={{0,128},{16,144},{32,160},{48,176},{64,192},{80,208},{96,224},{112... | collective-permute-start | bytes 393224 | tf_op jit(solution)/shard_map/ppermute | solution.py:370
  114.7 6.5 %collective-permute-done.28 = bf16[64,1024]{1,0:T(8,128)(2,1)S(1)} collective-permute-done((bf16[64,1024]{1,0:T(8,128)(2,1)S(1)}, bf16[64,1024]{1,0:T(8,128)(2,1)S(1)}, u32[]{:S(2)}, u32[]{:S(2)}) %collective-permute-start.28) | collective-permute-done | bytes 131104 | tf_op jit(solution)/shard_map/ppermute | solution.py:370
  (72 shorter events, 27.4 us)
Async XLA Ops:
  1.8 8.3 %collective-permute-start.3 = (bf16[64,1792]{1,0:T(8,128)(2,1)S(1)}, bf16[64,1792]{1,0:T(8,128)(2,1)S(1)}, u32[]{:S(2)}, u32[]{:S(2)}) collective-permute-start(bf16[64,1792]{1,0:T(8,128)(2,1)S(1)} %weights_transpose.1.refs_2_), channel_id=1, source_target_pairs={{0,4},{1,5},{2,6},{3,7},{4,8},{5,9},{6,10},{7,11},{8,12},{9,13},{1... | collective-permute-start | bytes 688136 | tf_op jit(solution)/shard_map/ppermute | solution.py:274
  3.5 8.3 %collective-permute-start.5 = (bf16[64,1792]{1,0:T(8,128)(2,1)S(1)}, bf16[64,1792]{1,0:T(8,128)(2,1)S(1)}, u32[]{:S(2)}, u32[]{:S(2)}) collective-permute-start(bf16[64,1792]{1,0:T(8,128)(2,1)S(1)} %weights_transpose.1.refs_2_), channel_id=1, source_target_pairs={{0,12},{1,13},{2,14},{3,15},{4,0},{5,1},{6,2},{7,3},{8,4},{9,5},{1... | collective-permute-start | bytes 688136 | tf_op jit(solution)/shard_map/ppermute | solution.py:275
  4.2 11.0 %collective-permute-start = (bf16[64,1792]{1,0:T(8,128)(2,1)S(1)}, bf16[64,1792]{1,0:T(8,128)(2,1)S(1)}, u32[]{:S(2)}, u32[]{:S(2)}) collective-permute-start(bf16[64,1792]{1,0:T(8,128)(2,1)S(1)} %weights_transpose.1.refs_2_), channel_id=1, source_target_pairs={{0,1},{1,2},{2,3},{3,0},{4,5},{5,6},{6,7},{7,4},{8,9},{9,10},{10,1... | collective-permute-start | bytes 688136 | tf_op jit(solution)/shard_map/ppermute | solution.py:262
  5.9 17.7 %collective-permute-start.1 = (bf16[64,1792]{1,0:T(8,128)(2,1)S(1)}, bf16[64,1792]{1,0:T(8,128)(2,1)S(1)}, u32[]{:S(2)}, u32[]{:S(2)}) collective-permute-start(bf16[64,1792]{1,0:T(8,128)(2,1)S(1)} %weights_transpose.1.refs_2_), channel_id=1, source_target_pairs={{0,2},{1,3},{2,0},{3,1},{4,6},{5,7},{6,4},{7,5},{8,10},{9,11},{10,... | collective-permute-start | bytes 688136 | tf_op jit(solution)/shard_map/ppermute | solution.py:262
  9.1 14.4 %collective-permute-start.2 = (bf16[64,1792]{1,0:T(8,128)(2,1)S(1)}, bf16[64,1792]{1,0:T(8,128)(2,1)S(1)}, u32[]{:S(2)}, u32[]{:S(2)}) collective-permute-start(bf16[64,1792]{1,0:T(8,128)(2,1)S(1)} %weights_transpose.1.refs_2_), channel_id=1, source_target_pairs={{0,3},{1,0},{2,1},{3,2},{4,7},{5,4},{6,5},{7,6},{8,11},{9,8},{10,9... | collective-permute-start | bytes 688136 | tf_op jit(solution)/shard_map/ppermute | solution.py:262
  10.2 13.5 %collective-permute-start.4 = (bf16[32,1792]{1,0:T(8,128)(2,1)S(1)}, bf16[32,1792]{1,0:T(8,128)(2,1)S(1)}, u32[]{:S(2)}, u32[]{:S(2)}) collective-permute-start(bf16[32,1792]{1,0:T(8,128)(2,1)S(1)} %slice.88), channel_id=1, source_target_pairs={{0,4},{1,5},{2,6},{3,7},{4,8},{5,9},{6,10},{7,11},{8,12},{9,13},{1... | collective-permute-start | bytes 344072 | tf_op jit(solution)/shard_map/ppermute | solution.py:276
  11.8 11.8 %collective-permute-start.6 = (bf16[32,1792]{1,0:T(8,128)(2,1)S(1)}, bf16[32,1792]{1,0:T(8,128)(2,1)S(1)}, u32[]{:S(2)}, u32[]{:S(2)}) collective-permute-start(bf16[32,1792]{1,0:T(8,128)(2,1)S(1)} %slice.89), channel_id=1, source_target_pairs={{0,12},{1,13},{2,14},{3,15},{4,0},{5,1},{6,2},{7,3},{8,4},{9,5},{1... | collective-permute-start | bytes 344072 | tf_op jit(solution)/shard_map/ppermute | solution.py:277
  23.6 19.4 %collective-permute-start.12 = (bf16[192,1792]{1,0:T(8,128)(2,1)S(1)}, bf16[192,1792]{1,0:T(8,128)(2,1)S(1)}, u32[]{:S(2)}, u32[]{:S(2)}) collective-permute-start(bf16[192,1792]{1,0:T(8,128)(2,1)S(1)} %pad_maximum_fusion.refs_7_), channel_id=1, source_target_pairs={{0,4},{1,5},{2,6},{3,7},{4,8},{5,9},{6,10},{7,11},{8,12},{9,13},{1... | collective-permute-start | bytes 2064392 | tf_op jit(solution)/shard_map/ppermute | solution.py:274
  25.3 19.4 %collective-permute-start.14 = (bf16[192,1792]{1,0:T(8,128)(2,1)S(1)}, bf16[192,1792]{1,0:T(8,128)(2,1)S(1)}, u32[]{:S(2)}, u32[]{:S(2)}) collective-permute-start(bf16[192,1792]{1,0:T(8,128)(2,1)S(1)} %pad_maximum_fusion.refs_7_), channel_id=1, source_target_pairs={{0,12},{1,13},{2,14},{3,15},{4,0},{5,1},{6,2},{7,3},{8,4},{9,5},{1... | collective-permute-start | bytes 2064392 | tf_op jit(solution)/shard_map/ppermute | solution.py:275
  25.7 11.5 %collective-permute-start.7 = (bf16[64,1024]{1,0:T(8,128)(2,1)S(1)}, bf16[64,1024]{1,0:T(8,128)(2,1)S(1)}, u32[]{:S(2)}, u32[]{:S(2)}) collective-permute-start(bf16[64,1024]{1,0:T(8,128)(2,1)S(1)} %bitcast.12), channel_id=1, source_target_pairs={{0,128},{16,144},{32,160},{48,176},{64,192},{80,208},{96,224},{112... | collective-permute-start | bytes 393224 | tf_op jit(solution)/shard_map/ppermute | solution.py:282
  37.2 9.2 %collective-permute-start.8 = (bf16[128,1024]{1,0:T(8,128)(2,1)S(1)}, bf16[128,1024]{1,0:T(8,128)(2,1)S(1)}, u32[]{:S(2)}, u32[]{:S(2)}) collective-permute-start(bf16[128,1024]{1,0:T(8,128)(2,1)S(1)} %pad_maximum_fusion.1), channel_id=1, source_target_pairs={{0,32},{16,48},{32,64},{48,80},{64,96},{80,112},{96,0},{112,16},{1... | collective-permute-start | bytes 786440 | tf_op jit(solution)/shard_map/ppermute | solution.py:285
  38.8 10.5 %collective-permute-start.9 = (bf16[128,1024]{1,0:T(8,128)(2,1)S(1)}, bf16[128,1024]{1,0:T(8,128)(2,1)S(1)}, u32[]{:S(2)}, u32[]{:S(2)}) collective-permute-start(bf16[128,1024]{1,0:T(8,128)(2,1)S(1)} %pad_maximum_fusion.1), channel_id=1, source_target_pairs={{0,64},{16,80},{32,96},{48,112},{64,0},{80,16},{96,32},{112,48},{1... | collective-permute-start | bytes 786440 | tf_op jit(solution)/shard_map/ppermute | solution.py:285
  41.5 7.7 %collective-permute-start.10 = (bf16[128,1024]{1,0:T(8,128)(2,1)S(1)}, bf16[128,1024]{1,0:T(8,128)(2,1)S(1)}, u32[]{:S(2)}, u32[]{:S(2)}) collective-permute-start(bf16[128,1024]{1,0:T(8,128)(2,1)S(1)} %pad_maximum_fusion.1), channel_id=1, source_target_pairs={{0,96},{16,112},{32,0},{48,16},{64,32},{80,48},{96,64},{112,80},{1... | collective-permute-start | bytes 786440 | tf_op jit(solution)/shard_map/ppermute | solution.py:285
  43.1 8.3 %collective-permute-start.13 = (bf16[96,1792]{1,0:T(8,128)(2,1)S(1)}, bf16[96,1792]{1,0:T(8,128)(2,1)S(1)}, u32[]{:S(2)}, u32[]{:S(2)}) collective-permute-start(bf16[96,1792]{1,0:T(8,128)(2,1)S(1)} %slice.90), channel_id=1, source_target_pairs={{0,4},{1,5},{2,6},{3,7},{4,8},{5,9},{6,10},{7,11},{8,12},{9,13},{1... | collective-permute-start | bytes 1032200 | tf_op jit(solution)/shard_map/ppermute | solution.py:276
  44.8 7.3 %collective-permute-start.15 = (bf16[96,1792]{1,0:T(8,128)(2,1)S(1)}, bf16[96,1792]{1,0:T(8,128)(2,1)S(1)}, u32[]{:S(2)}, u32[]{:S(2)}) collective-permute-start(bf16[96,1792]{1,0:T(8,128)(2,1)S(1)} %slice.91), channel_id=1, source_target_pairs={{0,12},{1,13},{2,14},{3,15},{4,0},{5,1},{6,2},{7,3},{8,4},{9,5},{1... | collective-permute-start | bytes 1032200 | tf_op jit(solution)/shard_map/ppermute | solution.py:277
  58.7 16.7 %collective-permute-start.16 = (bf16[64,1024]{1,0:T(8,128)(2,1)S(1)}, bf16[64,1024]{1,0:T(8,128)(2,1)S(1)}, u32[]{:S(2)}, u32[]{:S(2)}) collective-permute-start(bf16[64,1024]{1,0:T(8,128)(2,1)S(1)} %get-tuple-element.15), channel_id=1, source_target_pairs={{0,1},{1,2},{2,3},{3,4},{4,5},{5,6},{6,7},{7,8},{8,9},{9,10},{10,1... | collective-permute-start | bytes 393224 | tf_op jit(solution)/shard_map/ppermute | solution.py:331
  76.7 10.3 %collective-permute-start.18 = (bf16[64,1024]{1,0:T(8,128)(2,1)S(1)}, bf16[64,1024]{1,0:T(8,128)(2,1)S(1)}, u32[]{:S(2)}, u32[]{:S(2)}) collective-permute-start(bf16[64,1024]{1,0:T(8,128)(2,1)S(1)} %get-tuple-element.18.grad_ref), channel_id=1, source_target_pairs={{1,0},{2,1},{3,2},{4,3},{5,4},{6,5},{7,6},{8,7},{9,8},{10,9},{11,1... | collective-permute-start | bytes 393224 | tf_op jit(solution)/shard_map/ppermute | solution.py:350
  82.5 9.6 %collective-permute-start.19 = (bf16[64,1024]{1,0:T(8,128)(2,1)S(1)}, bf16[64,1024]{1,0:T(8,128)(2,1)S(1)}, u32[]{:S(2)}, u32[]{:S(2)}) collective-permute-start(bf16[64,1024]{1,0:T(8,128)(2,1)S(1)} %get-tuple-element.18.grad_ref), channel_id=1, source_target_pairs={{0,1},{1,2},{2,3},{3,4},{4,5},{5,6},{6,7},{7,8},{8,9},{9,10},{10,1... | collective-permute-start | bytes 393224 | tf_op jit(solution)/shard_map/ppermute | solution.py:349
  100.5 9.4 %collective-permute-start.26 = (bf16[64,1024]{1,0:T(8,128)(2,1)S(1)}, bf16[64,1024]{1,0:T(8,128)(2,1)S(1)}, u32[]{:S(2)}, u32[]{:S(2)}) collective-permute-start(bf16[64,1024]{1,0:T(8,128)(2,1)S(1)} %get-tuple-element.25), channel_id=1, source_target_pairs={{0,64},{16,80},{32,96},{48,112},{64,0},{80,16},{96,32},{112,48},{1... | collective-permute-start | bytes 393224 | tf_op jit(solution)/shard_map/ppermute | solution.py:297
  102.8 8.0 %collective-permute-start.27 = (bf16[64,1024]{1,0:T(8,128)(2,1)S(1)}, bf16[64,1024]{1,0:T(8,128)(2,1)S(1)}, u32[]{:S(2)}, u32[]{:S(2)}) collective-permute-start(bf16[64,1024]{1,0:T(8,128)(2,1)S(1)} %get-tuple-element.24), channel_id=1, source_target_pairs={{0,96},{16,112},{32,0},{48,16},{64,32},{80,48},{96,64},{112,80},{1... | collective-permute-start | bytes 393224 | tf_op jit(solution)/shard_map/ppermute | solution.py:297
  104.5 9.9 %collective-permute-start.21 = (bf16[64,1024]{1,0:T(8,128)(2,1)S(1)}, bf16[64,1024]{1,0:T(8,128)(2,1)S(1)}, u32[]{:S(2)}, u32[]{:S(2)}) collective-permute-start(bf16[64,1024]{1,0:T(8,128)(2,1)S(1)} %get-tuple-element.20), channel_id=1, source_target_pairs={{0,32},{16,48},{32,64},{48,80},{64,96},{80,112},{96,0},{112,16},{1... | collective-permute-start | bytes 393224 | tf_op jit(solution)/shard_map/ppermute | solution.py:297
  105.0 9.6 %collective-permute-start.22 = (bf16[64,1024]{1,0:T(8,128)(2,1)S(1)}, bf16[64,1024]{1,0:T(8,128)(2,1)S(1)}, u32[]{:S(2)}, u32[]{:S(2)}) collective-permute-start(bf16[64,1024]{1,0:T(8,128)(2,1)S(1)} %get-tuple-element.22), channel_id=1, source_target_pairs={{0,64},{16,80},{32,96},{48,112},{64,0},{80,16},{96,32},{112,48},{1... | collective-permute-start | bytes 393224 | tf_op jit(solution)/shard_map/ppermute | solution.py:297
  106.2 8.5 %collective-permute-start.23 = (bf16[64,1024]{1,0:T(8,128)(2,1)S(1)}, bf16[64,1024]{1,0:T(8,128)(2,1)S(1)}, u32[]{:S(2)}, u32[]{:S(2)}) collective-permute-start(bf16[64,1024]{1,0:T(8,128)(2,1)S(1)} %get-tuple-element.21), channel_id=1, source_target_pairs={{0,96},{16,112},{32,0},{48,16},{64,32},{80,48},{96,64},{112,80},{1... | collective-permute-start | bytes 393224 | tf_op jit(solution)/shard_map/ppermute | solution.py:297
  110.9 10.3 %collective-permute-start.28 = (bf16[64,1024]{1,0:T(8,128)(2,1)S(1)}, bf16[64,1024]{1,0:T(8,128)(2,1)S(1)}, u32[]{:S(2)}, u32[]{:S(2)}) collective-permute-start(bf16[64,1024]{1,0:T(8,128)(2,1)S(1)} %add_convert_fusion.1), channel_id=1, source_target_pairs={{0,128},{16,144},{32,160},{48,176},{64,192},{80,208},{96,224},{112... | collective-permute-start | bytes 393224 | tf_op jit(solution)/shard_map/ppermute | solution.py:370
  (11 other events, 83.6 us)

commit v4 on v3

--- a/solution.py
+++ b/solution.py
@@ -1,5 +1,3 @@
-import functools
-
 import jax
 import jax.numpy as jnp
 from jax import lax
@@ -150,12 +148,12 @@
 
 def forward_beside_kernel(*refs):
     x_pieces, w_pieces = refs[:2], refs[2:12]
-    x_ref, same_ref, beside_ref, up_ref, down_ref, w_scr, y_scr, sem = refs[13:]
-    assemble_inputs(x_pieces, x_ref)
+    same_ref, beside_ref, up_ref, down_ref, x_scr, w_scr, y_scr, sem = refs[13:]
+    assemble_inputs(x_pieces, x_scr)
     assemble_weights(w_pieces, same_ref, w_scr)
     keep = pltpu.make_async_copy(w_scr, beside_ref, sem)
     keep.start()
-    convolve((0, 9), w_scr[...], x_ref[...], (up_ref, down_ref), y_scr)
+    convolve((0, 9), w_scr[...], x_scr[...], (up_ref, down_ref), y_scr)
     keep.wait()
 
 
@@ -163,8 +161,9 @@
     refs[-1][...] = jnp.zeros((8, 128), BF16)
 
 
-def forward_same_kernel(x_ref, same_ref, own_ref, y_scr):
-    convolve((0,), same_ref[...], x_ref[...], (own_ref,), y_scr)
+def forward_same_kernel(first_ref, second_ref, same_ref, own_ref, x_scr, y_scr):
+    assemble_inputs((first_ref, second_ref), x_scr)
+    convolve((0,), same_ref[...], x_scr[...], (own_ref,), y_scr)
 
 
 def pointwise_kernel(own_ref, below_ref, above_ref, bias_ref, cot_ref, act_ref, grad_ref):
@@ -217,13 +216,21 @@
         )
 
 
-def backward_beside_kernel(far, above_ref, below_ref, same_ref, w_ref, out_ref, g_scr):
+def backward_far_kernel(above_ref, below_ref, same_ref, w_ref, out_ref, g_ref):
+    stack_taps([above_ref, below_ref], g_ref)
+    backward_rows(1, g_ref, same_ref, w_ref, out_ref)
+
+
+def backward_near_kernel(g_ref, same_ref, w_ref, out_ref):
+    backward_rows(0, g_ref, same_ref, w_ref, out_ref)
+
+
+def backward_rows(far, g_ref, same_ref, w_ref, out_ref):
     zh, x, c = filt_position()
     size = CHANNELS // 2
     first = pl.multiple_of(((zh + far) % ZH) * size, size)
-    stack_taps([above_ref, below_ref], g_scr)
     total = same_ref[pl.ds(first, size), :] + jnp.dot(
-        w_ref[pl.ds(first, size), :], g_scr[...], preferred_element_type=F32
+        w_ref[pl.ds(first, size), :], g_ref[...], preferred_element_type=F32
     )
     total = total.astype(BF16)
     for at in range(size // BLOCK):
@@ -307,17 +314,17 @@
     (ready,) = call(
         ready_kernel, "weights_ready", (shape(8, 128),), [], 7168, w_pieces[7:9], in_any=range(2)
     )
-    channels, same_taps, beside_taps, up, down = call(
+    same_taps, beside_taps, up, down = call(
         forward_beside_kernel,
         "forward_beside",
         (
-            shape(CHANNELS, CELLS),
             shape(CHANNELS, SAME),
             shape(CHANNELS, BESIDE),
             shape(BLOCK, CELLS),
             shape(BLOCK, CELLS),
         ),
         [
+            pltpu.VMEM((CHANNELS, CELLS), BF16),
             pltpu.VMEM((CHANNELS, BESIDE), BF16),
             pltpu.VMEM((BESIDE, CELLS), F32),
             pltpu.SemaphoreType.DMA,
@@ -325,7 +332,7 @@
         BESIDE,
         x_pieces + w_pieces + [ready],
         in_any=(12,),
-        out_any=(2,),
+        out_any=(1,),
         limit=46,
     )
     below = lax.ppermute(up, "slab", UP)
@@ -334,9 +341,9 @@
         forward_same_kernel,
         "forward_same",
         (shape(BLOCK, CELLS, F32),),
-        [pltpu.VMEM((SAME, CELLS), F32)],
+        [pltpu.VMEM((CHANNELS, CELLS), BF16), pltpu.VMEM((SAME, CELLS), F32)],
         SAME,
-        [channels, same_taps],
+        x_pieces + [same_taps],
     )
     activated, grad = call(
         pointwise_kernel,
@@ -356,19 +363,25 @@
         SAME,
         [grad, same_taps],
     )
-    sums = []
-    for far, name in ((1, "backward_far"), (0, "backward_near")):
-        (part,) = call(
-            functools.partial(backward_beside_kernel, far),
-            name,
-            (shape(CHANNELS // 2, CELLS),),
-            [pltpu.VMEM((BESIDE, CELLS), BF16)],
-            BESIDE // 2,
-            [grad_above, grad_below, same, beside_taps],
-        )
-        sums.append(sum_over_row(part))
-    arrived = lax.ppermute(sums[0].astype(BF16), "filt", TO_ZHI)
-    input_grad = (sums[1] + arrived.astype(F32)).astype(BF16)
+    far, stacked = call(
+        backward_far_kernel,
+        "backward_far",
+        (shape(CHANNELS // 2, CELLS), shape(BESIDE, CELLS)),
+        [],
+        BESIDE // 2,
+        [grad_above, grad_below, same, beside_taps],
+    )
+    (near,) = call(
+        backward_near_kernel,
+        "backward_near",
+        (shape(CHANNELS // 2, CELLS),),
+        [],
+        BESIDE // 2,
+        [stacked, same, beside_taps],
+    )
+    far, near = sum_over_row(far), sum_over_row(near)
+    arrived = lax.ppermute(far.astype(BF16), "filt", TO_ZHI)
+    input_grad = (near + arrived.astype(F32)).astype(BF16)
     return activated.reshape(cotangent.shape), input_grad.reshape(inputs.shape)
 
 

time: 123 us -> 116 us (0.943)
  waiting for transfers between devices: 37.2 us -> 32.7 us
  Pallas kernels: 18.9 us -> 16.2 us
    ppermute x1, starting transfers between devices: 10.1 us -> 3.39 us  [local(): below = lax.ppermute(up, 'slab', UP)]
    ppermute x1, waiting for transfers between devices: 5.07 us -> 0.01 us  [local(): grad_below = lax.ppermute(grad, 'slab', UP)]
    ppermute x3, waiting for transfers between devices: 11.2 us -> 15.5 us  [gather_weights(): beside = [lax.ppermute(own, 'slab', to_z(k)) for k in range(1, ZN)]]
    ppermute x1, waiting for transfers between devices: 6.46 us -> 3.06 us  [local(): arrived = lax.ppermute(far.astype(BF16), 'filt', TO_ZHI)]
    ppermute x1, starting transfers between devices: 1.92 us -> 5.15 us  [local(): above = lax.ppermute(down, 'slab', DOWN)]
    ppermute x2, starting transfers between devices: 3.31 us -> 0.31 us  [along_y(): before = lax.ppermute(line, 'slab', to_y(1))]
    ppermute x1, starting transfers between devices: 3.55 us -> 6.47 us  [local(): arrived = lax.ppermute(far.astype(BF16), 'filt', TO_ZHI)]
    ppermute x2, starting transfers between devices: 1.15 us -> 4.06 us  [along_y(): after = lax.ppermute(line, 'slab', to_y(-1))]
  transfers between devices with their start and end apart: 29 -> 29, of which waited for: 15 -> 9; matrix products, arithmetic and copies ran while one was open for 1% -> 1% of each run, Pallas kernels for 7% -> 6%
where the time goes in v4:
time: 116 us; the launch traced here: 114 us
  starting transfers between devices  60.6 us (52%)
  waiting for transfers between devices  32.7 us (28%)
  Pallas kernels  16.2 us (14%)
  local copies, waits for them, and re-layouts  2.57 us (2%)
  other arithmetic  1.18 us (1%)
    pallas_call x8, Pallas kernels, call(): pl.pallas_call(kernel, out_shape=outs, in_specs=[ANY if at in in_any else...  16.2 us
    ppermute x3, waiting for transfers between devices, gather_weights(): beside = [lax.ppermute(own, 'slab', to_z(k)) for k in range(1, ZN)]  15.5 us
    ppermute x6, starting transfers between devices, sum_over_row(): arrived = [lax.ppermute(sums[k], 'filt', to_x(k)) for k in range(1, XN)]  8.95 us
    ppermute x1, starting transfers between devices, local(): grad_above = lax.ppermute(grad, 'slab', DOWN)  6.62 us
    ppermute x1, starting transfers between devices, local(): arrived = lax.ppermute(far.astype(BF16), 'filt', TO_ZHI)  6.47 us
    ppermute x3, starting transfers between devices, gather_inputs(): lax.ppermute(pair, 'filt', to_x(k))  6.42 us
    ppermute x1, starting transfers between devices, gather_inputs(): far = lax.ppermute(once(inputs, w_pieces[5]), 'filt', TO_ZHI)  6.12 us
    ppermute x1, starting transfers between devices, local(): above = lax.ppermute(down, 'slab', DOWN)  5.15 us
  transfers between devices with their start and end apart: 29, of which 9 were waited for; matrix products, arithmetic and copies ran while one was open for 1% of the time, Pallas kernels for 6%

profile of v4, /device:TPU:8, one launch (start us, length us, event | category | flops | bytes accessed | tf_op | source)
XLA Modules:
  0.0 114.2 jit_solution(3589130239526102585)
XLA Ops:
  1.8 2.3 %collective-permute-start.5 = (bf16[64,1792]{1,0:T(8,128)(2,1)S(1)}, bf16[64,1792]{1,0:T(8,128)(2,1)S(1)}, u32[]{:S(2)}, u32[]{:S(2)}) collective-permute-start(bf16[64,1792]{1,0:T(8,128)(2,1)S(1)} %weights_transpose.1.refs_2_), channel_id=1, source_target_pairs={{0,12},{1,13},{2,14},{3,15},{4,0},{5,1},{6,2},{7,3},{8,4},{9,5},{1... | collective-permute-start | bytes 688136 | tf_op jit(solution)/shard_map/ppermute | solution.py:282
  4.1 4.5 %collective-permute-start.2 = (bf16[64,1792]{1,0:T(8,128)(2,1)S(1)}, bf16[64,1792]{1,0:T(8,128)(2,1)S(1)}, u32[]{:S(2)}, u32[]{:S(2)}) collective-permute-start(bf16[64,1792]{1,0:T(8,128)(2,1)S(1)} %weights_transpose.1.refs_2_), channel_id=1, source_target_pairs={{0,3},{1,0},{2,1},{3,2},{4,7},{5,4},{6,5},{7,6},{8,11},{9,8},{10,9... | collective-permute-start | bytes 688136 | tf_op jit(solution)/shard_map/ppermute | solution.py:269
  11.5 3.2 %collective-permute-done.2 = bf16[64,1792]{1,0:T(8,128)(2,1)S(1)} collective-permute-done((bf16[64,1792]{1,0:T(8,128)(2,1)S(1)}, bf16[64,1792]{1,0:T(8,128)(2,1)S(1)}, u32[]{:S(2)}, u32[]{:S(2)}) %collective-permute-start.2) | collective-permute-done | bytes 229408 | tf_op jit(solution)/shard_map/ppermute | solution.py:269
  14.7 12.3 %collective-permute-done.1 = bf16[64,1792]{1,0:T(8,128)(2,1)S(1)} collective-permute-done((bf16[64,1792]{1,0:T(8,128)(2,1)S(1)}, bf16[64,1792]{1,0:T(8,128)(2,1)S(1)}, u32[]{:S(2)}, u32[]{:S(2)}) %collective-permute-start.1) | collective-permute-done | bytes 229408 | tf_op jit(solution)/shard_map/ppermute | solution.py:269
  29.2 6.1 %collective-permute-start.7 = (bf16[64,1024]{1,0:T(8,128)(2,1)S(1)}, bf16[64,1024]{1,0:T(8,128)(2,1)S(1)}, u32[]{:S(2)}, u32[]{:S(2)}) collective-permute-start(bf16[64,1024]{1,0:T(8,128)(2,1)S(1)} %bitcast.12), channel_id=1, source_target_pairs={{0,128},{16,144},{32,160},{48,176},{64,192},{80,208},{96,224},{112... | collective-permute-start | bytes 393224 | tf_op jit(solution)/shard_map/ppermute | solution.py:289
  35.3 4.0 %collective-permute-done.7 = bf16[64,1024]{1,0:T(8,128)(2,1)S(1)} collective-permute-done((bf16[64,1024]{1,0:T(8,128)(2,1)S(1)}, bf16[64,1024]{1,0:T(8,128)(2,1)S(1)}, u32[]{:S(2)}, u32[]{:S(2)}) %collective-permute-start.7) | collective-permute-done | bytes 131104 | tf_op jit(solution)/shard_map/ppermute | solution.py:289
  39.3 3.1 %collective-permute-start.9 = (bf16[128,1024]{1,0:T(8,128)(2,1)S(1)}, bf16[128,1024]{1,0:T(8,128)(2,1)S(1)}, u32[]{:S(2)}, u32[]{:S(2)}) collective-permute-start(bf16[128,1024]{1,0:T(8,128)(2,1)S(1)} %pad_maximum_fusion.1), channel_id=1, source_target_pairs={{0,64},{16,80},{32,96},{48,112},{64,0},{80,16},{96,32},{112,48},{1... | collective-permute-start | bytes 786440 | tf_op jit(solution)/shard_map/ppermute | solution.py:292
  43.0 2.7 %collective-permute-start.10 = (bf16[128,1024]{1,0:T(8,128)(2,1)S(1)}, bf16[128,1024]{1,0:T(8,128)(2,1)S(1)}, u32[]{:S(2)}, u32[]{:S(2)}) collective-permute-start(bf16[128,1024]{1,0:T(8,128)(2,1)S(1)} %pad_maximum_fusion.1), channel_id=1, source_target_pairs={{0,96},{16,112},{32,0},{48,16},{64,32},{80,48},{96,64},{112,80},{1... | collective-permute-start | bytes 786440 | tf_op jit(solution)/shard_map/ppermute | solution.py:292
  45.8 2.9 %collective-permute-start.15 = (bf16[96,1792]{1,0:T(8,128)(2,1)S(1)}, bf16[96,1792]{1,0:T(8,128)(2,1)S(1)}, u32[]{:S(2)}, u32[]{:S(2)}) collective-permute-start(bf16[96,1792]{1,0:T(8,128)(2,1)S(1)} %slice.91), channel_id=1, source_target_pairs={{0,12},{1,13},{2,14},{3,15},{4,0},{5,1},{6,2},{7,3},{8,4},{9,5},{1... | collective-permute-start | bytes 1032200 | tf_op jit(solution)/shard_map/ppermute | solution.py:284
  48.8 2.1 %collective-permute-done.8 = bf16[128,1024]{1,0:T(8,128)(2,1)S(1)} collective-permute-done((bf16[128,1024]{1,0:T(8,128)(2,1)S(1)}, bf16[128,1024]{1,0:T(8,128)(2,1)S(1)}, u32[]{:S(2)}, u32[]{:S(2)}) %collective-permute-start.8) | collective-permute-done | bytes 262176 | tf_op jit(solution)/shard_map/ppermute | solution.py:292
  51.3 2.2 %collective-permute-done.15.refs_1_.refs_10_ = bf16[96,1792]{1,0:T(8,128)(2,1)S(1)} collective-permute-done((bf16[96,1792]{1,0:T(8,128)(2,1)S(1)}, bf16[96,1792]{1,0:T(8,128)(2,1)S(1)}, u32[]{:S(2)}, u32[]{:S(2)}) %collective-permute-start.15) | collective-permute-done | bytes 344096 | tf_op jit(solution)/shard_map/ppermute | solution.py:284
  53.5 3.5 %collective-permute-done.13.refs_0_.refs_9_ = bf16[96,1792]{1,0:T(8,128)(2,1)S(1)} collective-permute-done((bf16[96,1792]{1,0:T(8,128)(2,1)S(1)}, bf16[96,1792]{1,0:T(8,128)(2,1)S(1)}, u32[]{:S(2)}, u32[]{:S(2)}) %collective-permute-start.13) | collective-permute-done | bytes 344096 | tf_op jit(solution)/shard_map/ppermute | solution.py:283
  57.0 5.1 %forward_beside.1 = (bf16[1024,640]{1,0:T(8,128)(2,1)S(1)}, bf16[1024,1152]{1,0:T(8,128)(2,1)}, bf16[64,1024]{1,0:T(8,128)(2,1)S(1)}, bf16[64,1024]{1,0:T(8,128)(2,1)S(1)}) custom-call(bf16[512,1024]{1,0:T(8,128)(2,1)S(1)} %constant_dynamic-update-slice_fusion.refs_0_.first_ref, bf16[512,1024]{1,0:T(8,128)(2,1)S(1)} %collective-permute-done.11.refs_1_.second_ref, ...), custom_call_target="tpu_custom_call" | custom-call | flops 2415919104 | bytes 1048576 | tf_op jit(solution)/shard_map/forward_beside/pallas_call | solution.py:252
  62.2 3.4 %collective-permute-start.16 = (bf16[64,1024]{1,0:T(8,128)(2,1)S(1)}, bf16[64,1024]{1,0:T(8,128)(2,1)S(1)}, u32[]{:S(2)}, u32[]{:S(2)}) collective-permute-start(bf16[64,1024]{1,0:T(8,128)(2,1)S(1)} %get-tuple-element.15), channel_id=1, source_target_pairs={{0,1},{1,2},{2,3},{3,4},{4,5},{5,6},{6,7},{7,8},{8,9},{9,10},{10,1... | collective-permute-start | bytes 393224 | tf_op jit(solution)/shard_map/ppermute | solution.py:338
  65.6 5.1 %collective-permute-start.17 = (bf16[64,1024]{1,0:T(8,128)(2,1)S(1)}, bf16[64,1024]{1,0:T(8,128)(2,1)S(1)}, u32[]{:S(2)}, u32[]{:S(2)}) collective-permute-start(bf16[64,1024]{1,0:T(8,128)(2,1)S(1)} %get-tuple-element.16), channel_id=1, source_target_pairs={{1,0},{2,1},{3,2},{4,3},{5,4},{6,5},{7,6},{8,7},{9,8},{10,9},{11,1... | collective-permute-start | bytes 393224 | tf_op jit(solution)/shard_map/ppermute | solution.py:339
  72.1 3.1 %forward_same.1.own_ref = f32[64,1024]{1,0:T(8,128)S(1)} custom-call(bf16[512,1024]{1,0:T(8,128)(2,1)S(1)} %constant_dynamic-update-slice_fusion.refs_0_.first_ref, bf16[512,1024]{1,0:T(8,128)(2,1)S(1)} %copy-done.4, bf16[1024,640]{1,0:T(8,128)(2,1)S(1)} %get-tuple-element.14.same_ref.w_ref), custom_call_target="tpu_custom_call" | custom-call | flops 1342177280 | bytes 1048576 | tf_op jit(solution)/shard_map/forward_same/pallas_call | solution.py:252
  77.9 6.6 %collective-permute-start.18 = (bf16[64,1024]{1,0:T(8,128)(2,1)S(1)}, bf16[64,1024]{1,0:T(8,128)(2,1)S(1)}, u32[]{:S(2)}, u32[]{:S(2)}) collective-permute-start(bf16[64,1024]{1,0:T(8,128)(2,1)S(1)} %get-tuple-element.18.grad_ref), channel_id=1, source_target_pairs={{1,0},{2,1},{3,2},{4,3},{5,4},{6,5},{7,6},{8,7},{9,8},{10,9},{11,1... | collective-permute-start | bytes 393224 | tf_op jit(solution)/shard_map/ppermute | solution.py:357
  84.5 2.5 %backward_same.1.same_ref = f32[1024,1024]{1,0:T(8,128)S(1)} custom-call(bf16[64,1024]{1,0:T(8,128)(2,1)S(1)} %get-tuple-element.18.grad_ref, bf16[1024,640]{1,0:T(8,128)(2,1)S(1)} %get-tuple-element.14.same_ref.w_ref), custom_call_target="tpu_custom_call" | custom-call | flops 1342177280 | bytes 1048576 | tf_op jit(solution)/shard_map/backward_same/pallas_call | solution.py:252
  87.1 3.0 %backward_far.1 = (bf16[512,1024]{1,0:T(8,128)(2,1)S(1)}, bf16[1152,1024]{1,0:T(8,128)(2,1)S(1)}) custom-call(bf16[64,1024]{1,0:T(8,128)(2,1)S(1)} %collective-permute-done.18.above_ref, bf16[64,1024]{1,0:T(8,128)(2,1)S(1)} %collective-permute-done.19.below_ref, f32[1024,1024]{1,0:T(8,128)S(1)} %backward_same.1.same_ref, bf16[1024,1152]{1,0:T(8,128)(2,1)S(1)} %copy-done), custom_call_target="tpu_custom_call" | custom-call | flops 1207959552 | bytes 1048576 | tf_op jit(solution)/shard_map/backward_far/pallas_call | solution.py:252
  93.6 2.3 %collective-permute-start.27 = (bf16[64,1024]{1,0:T(8,128)(2,1)S(1)}, bf16[64,1024]{1,0:T(8,128)(2,1)S(1)}, u32[]{:S(2)}, u32[]{:S(2)}) collective-permute-start(bf16[64,1024]{1,0:T(8,128)(2,1)S(1)} %get-tuple-element.26), channel_id=1, source_target_pairs={{0,96},{16,112},{32,0},{48,16},{64,32},{80,48},{96,64},{112,80},{1... | collective-permute-start | bytes 393224 | tf_op jit(solution)/shard_map/ppermute | solution.py:304
  99.7 2.0 %collective-permute-start.22 = (bf16[64,1024]{1,0:T(8,128)(2,1)S(1)}, bf16[64,1024]{1,0:T(8,128)(2,1)S(1)}, u32[]{:S(2)}, u32[]{:S(2)}) collective-permute-start(bf16[64,1024]{1,0:T(8,128)(2,1)S(1)} %get-tuple-element.24), channel_id=1, source_target_pairs={{0,64},{16,80},{32,96},{48,112},{64,0},{80,16},{96,32},{112,48},{1... | collective-permute-start | bytes 393224 | tf_op jit(solution)/shard_map/ppermute | solution.py:304
  101.9 1.9 %collective-permute-done.26 = bf16[64,1024]{1,0:T(8,128)(2,1)S(1)} collective-permute-done((bf16[64,1024]{1,0:T(8,128)(2,1)S(1)}, bf16[64,1024]{1,0:T(8,128)(2,1)S(1)}, u32[]{:S(2)}, u32[]{:S(2)}) %collective-permute-start.26) | collective-permute-done | bytes 131104 | tf_op jit(solution)/shard_map/ppermute | solution.py:304
  103.9 6.5 %collective-permute-start.28 = (bf16[64,1024]{1,0:T(8,128)(2,1)S(1)}, bf16[64,1024]{1,0:T(8,128)(2,1)S(1)}, u32[]{:S(2)}, u32[]{:S(2)}) collective-permute-start(bf16[64,1024]{1,0:T(8,128)(2,1)S(1)} %add_convert_fusion.1), channel_id=1, source_target_pairs={{0,128},{16,144},{32,160},{48,176},{64,192},{80,208},{96,224},{112... | collective-permute-start | bytes 393224 | tf_op jit(solution)/shard_map/ppermute | solution.py:383
  110.4 3.1 %collective-permute-done.28 = bf16[64,1024]{1,0:T(8,128)(2,1)S(1)} collective-permute-done((bf16[64,1024]{1,0:T(8,128)(2,1)S(1)}, bf16[64,1024]{1,0:T(8,128)(2,1)S(1)}, u32[]{:S(2)}, u32[]{:S(2)}) %collective-permute-start.28) | collective-permute-done | bytes 131104 | tf_op jit(solution)/shard_map/ppermute | solution.py:383
  (74 shorter events, 19.8 us)
Async XLA Ops:
  1.8 7.4 %collective-permute-start.5 = (bf16[64,1792]{1,0:T(8,128)(2,1)S(1)}, bf16[64,1792]{1,0:T(8,128)(2,1)S(1)}, u32[]{:S(2)}, u32[]{:S(2)}) collective-permute-start(bf16[64,1792]{1,0:T(8,128)(2,1)S(1)} %weights_transpose.1.refs_2_), channel_id=1, source_target_pairs={{0,12},{1,13},{2,14},{3,15},{4,0},{5,1},{6,2},{7,3},{8,4},{9,5},{1... | collective-permute-start | bytes 688136 | tf_op jit(solution)/shard_map/ppermute | solution.py:282
  4.1 10.6 %collective-permute-start.2 = (bf16[64,1792]{1,0:T(8,128)(2,1)S(1)}, bf16[64,1792]{1,0:T(8,128)(2,1)S(1)}, u32[]{:S(2)}, u32[]{:S(2)}) collective-permute-start(bf16[64,1792]{1,0:T(8,128)(2,1)S(1)} %weights_transpose.1.refs_2_), channel_id=1, source_target_pairs={{0,3},{1,0},{2,1},{3,2},{4,7},{5,4},{6,5},{7,6},{8,11},{9,8},{10,9... | collective-permute-start | bytes 688136 | tf_op jit(solution)/shard_map/ppermute | solution.py:269
  8.6 18.4 %collective-permute-start.1 = (bf16[64,1792]{1,0:T(8,128)(2,1)S(1)}, bf16[64,1792]{1,0:T(8,128)(2,1)S(1)}, u32[]{:S(2)}, u32[]{:S(2)}) collective-permute-start(bf16[64,1792]{1,0:T(8,128)(2,1)S(1)} %weights_transpose.1.refs_2_), channel_id=1, source_target_pairs={{0,2},{1,3},{2,0},{3,1},{4,6},{5,7},{6,4},{7,5},{8,10},{9,11},{10,... | collective-permute-start | bytes 688136 | tf_op jit(solution)/shard_map/ppermute | solution.py:269
  8.6 18.4 %collective-permute-start = (bf16[64,1792]{1,0:T(8,128)(2,1)S(1)}, bf16[64,1792]{1,0:T(8,128)(2,1)S(1)}, u32[]{:S(2)}, u32[]{:S(2)}) collective-permute-start(bf16[64,1792]{1,0:T(8,128)(2,1)S(1)} %weights_transpose.1.refs_2_), channel_id=1, source_target_pairs={{0,1},{1,2},{2,3},{3,0},{4,5},{5,6},{6,7},{7,4},{8,9},{9,10},{10,1... | collective-permute-start | bytes 688136 | tf_op jit(solution)/shard_map/ppermute | solution.py:269
  9.3 17.8 %collective-permute-start.6 = (bf16[32,1792]{1,0:T(8,128)(2,1)S(1)}, bf16[32,1792]{1,0:T(8,128)(2,1)S(1)}, u32[]{:S(2)}, u32[]{:S(2)}) collective-permute-start(bf16[32,1792]{1,0:T(8,128)(2,1)S(1)} %slice.89), channel_id=1, source_target_pairs={{0,12},{1,13},{2,14},{3,15},{4,0},{5,1},{6,2},{7,3},{8,4},{9,5},{1... | collective-permute-start | bytes 344072 | tf_op jit(solution)/shard_map/ppermute | solution.py:284
  10.8 16.3 %collective-permute-start.4 = (bf16[32,1792]{1,0:T(8,128)(2,1)S(1)}, bf16[32,1792]{1,0:T(8,128)(2,1)S(1)}, u32[]{:S(2)}, u32[]{:S(2)}) collective-permute-start(bf16[32,1792]{1,0:T(8,128)(2,1)S(1)} %slice.88), channel_id=1, source_target_pairs={{0,4},{1,5},{2,6},{3,7},{4,8},{5,9},{6,10},{7,11},{8,12},{9,13},{1... | collective-permute-start | bytes 344072 | tf_op jit(solution)/shard_map/ppermute | solution.py:283
  27.1 18.7 %collective-permute-start.14 = (bf16[192,1792]{1,0:T(8,128)(2,1)S(1)}, bf16[192,1792]{1,0:T(8,128)(2,1)S(1)}, u32[]{:S(2)}, u32[]{:S(2)}) collective-permute-start(bf16[192,1792]{1,0:T(8,128)(2,1)S(1)} %pad_maximum_fusion.refs_7_), channel_id=1, source_target_pairs={{0,12},{1,13},{2,14},{3,15},{4,0},{5,1},{6,2},{7,3},{8,4},{9,5},{1... | collective-permute-start | bytes 2064392 | tf_op jit(solution)/shard_map/ppermute | solution.py:282
  28.9 19.8 %collective-permute-start.12 = (bf16[192,1792]{1,0:T(8,128)(2,1)S(1)}, bf16[192,1792]{1,0:T(8,128)(2,1)S(1)}, u32[]{:S(2)}, u32[]{:S(2)}) collective-permute-start(bf16[192,1792]{1,0:T(8,128)(2,1)S(1)} %pad_maximum_fusion.refs_7_), channel_id=1, source_target_pairs={{0,4},{1,5},{2,6},{3,7},{4,8},{5,9},{6,10},{7,11},{8,12},{9,13},{1... | collective-permute-start | bytes 2064392 | tf_op jit(solution)/shard_map/ppermute | solution.py:281
  29.2 10.1 %collective-permute-start.7 = (bf16[64,1024]{1,0:T(8,128)(2,1)S(1)}, bf16[64,1024]{1,0:T(8,128)(2,1)S(1)}, u32[]{:S(2)}, u32[]{:S(2)}) collective-permute-start(bf16[64,1024]{1,0:T(8,128)(2,1)S(1)} %bitcast.12), channel_id=1, source_target_pairs={{0,128},{16,144},{32,160},{48,176},{64,192},{80,208},{96,224},{112... | collective-permute-start | bytes 393224 | tf_op jit(solution)/shard_map/ppermute | solution.py:289
  39.3 11.6 %collective-permute-start.9 = (bf16[128,1024]{1,0:T(8,128)(2,1)S(1)}, bf16[128,1024]{1,0:T(8,128)(2,1)S(1)}, u32[]{:S(2)}, u32[]{:S(2)}) collective-permute-start(bf16[128,1024]{1,0:T(8,128)(2,1)S(1)} %pad_maximum_fusion.1), channel_id=1, source_target_pairs={{0,64},{16,80},{32,96},{48,112},{64,0},{80,16},{96,32},{112,48},{1... | collective-permute-start | bytes 786440 | tf_op jit(solution)/shard_map/ppermute | solution.py:292
  42.4 8.5 %collective-permute-start.8 = (bf16[128,1024]{1,0:T(8,128)(2,1)S(1)}, bf16[128,1024]{1,0:T(8,128)(2,1)S(1)}, u32[]{:S(2)}, u32[]{:S(2)}) collective-permute-start(bf16[128,1024]{1,0:T(8,128)(2,1)S(1)} %pad_maximum_fusion.1), channel_id=1, source_target_pairs={{0,32},{16,48},{32,64},{48,80},{64,96},{80,112},{96,0},{112,16},{1... | collective-permute-start | bytes 786440 | tf_op jit(solution)/shard_map/ppermute | solution.py:292
  43.0 8.0 %collective-permute-start.10 = (bf16[128,1024]{1,0:T(8,128)(2,1)S(1)}, bf16[128,1024]{1,0:T(8,128)(2,1)S(1)}, u32[]{:S(2)}, u32[]{:S(2)}) collective-permute-start(bf16[128,1024]{1,0:T(8,128)(2,1)S(1)} %pad_maximum_fusion.1), channel_id=1, source_target_pairs={{0,96},{16,112},{32,0},{48,16},{64,32},{80,48},{96,64},{112,80},{1... | collective-permute-start | bytes 786440 | tf_op jit(solution)/shard_map/ppermute | solution.py:292
  45.8 7.7 %collective-permute-start.15 = (bf16[96,1792]{1,0:T(8,128)(2,1)S(1)}, bf16[96,1792]{1,0:T(8,128)(2,1)S(1)}, u32[]{:S(2)}, u32[]{:S(2)}) collective-permute-start(bf16[96,1792]{1,0:T(8,128)(2,1)S(1)} %slice.91), channel_id=1, source_target_pairs={{0,12},{1,13},{2,14},{3,15},{4,0},{5,1},{6,2},{7,3},{8,4},{9,5},{1... | collective-permute-start | bytes 1032200 | tf_op jit(solution)/shard_map/ppermute | solution.py:284
  48.7 8.3 %collective-permute-start.13 = (bf16[96,1792]{1,0:T(8,128)(2,1)S(1)}, bf16[96,1792]{1,0:T(8,128)(2,1)S(1)}, u32[]{:S(2)}, u32[]{:S(2)}) collective-permute-start(bf16[96,1792]{1,0:T(8,128)(2,1)S(1)} %slice.90), channel_id=1, source_target_pairs={{0,4},{1,5},{2,6},{3,7},{4,8},{5,9},{6,10},{7,11},{8,12},{9,13},{1... | collective-permute-start | bytes 1032200 | tf_op jit(solution)/shard_map/ppermute | solution.py:283
  62.2 13.0 %collective-permute-start.16 = (bf16[64,1024]{1,0:T(8,128)(2,1)S(1)}, bf16[64,1024]{1,0:T(8,128)(2,1)S(1)}, u32[]{:S(2)}, u32[]{:S(2)}) collective-permute-start(bf16[64,1024]{1,0:T(8,128)(2,1)S(1)} %get-tuple-element.15), channel_id=1, source_target_pairs={{0,1},{1,2},{2,3},{3,4},{4,5},{5,6},{6,7},{7,8},{8,9},{9,10},{10,1... | collective-permute-start | bytes 393224 | tf_op jit(solution)/shard_map/ppermute | solution.py:338
  65.6 9.6 %collective-permute-start.17 = (bf16[64,1024]{1,0:T(8,128)(2,1)S(1)}, bf16[64,1024]{1,0:T(8,128)(2,1)S(1)}, u32[]{:S(2)}, u32[]{:S(2)}) collective-permute-start(bf16[64,1024]{1,0:T(8,128)(2,1)S(1)} %get-tuple-element.16), channel_id=1, source_target_pairs={{1,0},{2,1},{3,2},{4,3},{5,4},{6,5},{7,6},{8,7},{9,8},{10,9},{11,1... | collective-permute-start | bytes 393224 | tf_op jit(solution)/shard_map/ppermute | solution.py:339
  76.0 11.1 %collective-permute-start.19 = (bf16[64,1024]{1,0:T(8,128)(2,1)S(1)}, bf16[64,1024]{1,0:T(8,128)(2,1)S(1)}, u32[]{:S(2)}, u32[]{:S(2)}) collective-permute-start(bf16[64,1024]{1,0:T(8,128)(2,1)S(1)} %get-tuple-element.18.grad_ref), channel_id=1, source_target_pairs={{0,1},{1,2},{2,3},{3,4},{4,5},{5,6},{6,7},{7,8},{8,9},{9,10},{10,1... | collective-permute-start | bytes 393224 | tf_op jit(solution)/shard_map/ppermute | solution.py:356
  77.9 9.2 %collective-permute-start.18 = (bf16[64,1024]{1,0:T(8,128)(2,1)S(1)}, bf16[64,1024]{1,0:T(8,128)(2,1)S(1)}, u32[]{:S(2)}, u32[]{:S(2)}) collective-permute-start(bf16[64,1024]{1,0:T(8,128)(2,1)S(1)} %get-tuple-element.18.grad_ref), channel_id=1, source_target_pairs={{1,0},{2,1},{3,2},{4,3},{5,4},{6,5},{7,6},{8,7},{9,8},{10,9},{11,1... | collective-permute-start | bytes 393224 | tf_op jit(solution)/shard_map/ppermute | solution.py:357
  93.6 8.3 %collective-permute-start.27 = (bf16[64,1024]{1,0:T(8,128)(2,1)S(1)}, bf16[64,1024]{1,0:T(8,128)(2,1)S(1)}, u32[]{:S(2)}, u32[]{:S(2)}) collective-permute-start(bf16[64,1024]{1,0:T(8,128)(2,1)S(1)} %get-tuple-element.26), channel_id=1, source_target_pairs={{0,96},{16,112},{32,0},{48,16},{64,32},{80,48},{96,64},{112,80},{1... | collective-permute-start | bytes 393224 | tf_op jit(solution)/shard_map/ppermute | solution.py:304
  95.9 8.0 %collective-permute-start.26 = (bf16[64,1024]{1,0:T(8,128)(2,1)S(1)}, bf16[64,1024]{1,0:T(8,128)(2,1)S(1)}, u32[]{:S(2)}, u32[]{:S(2)}) collective-permute-start(bf16[64,1024]{1,0:T(8,128)(2,1)S(1)} %get-tuple-element.27), channel_id=1, source_target_pairs={{0,64},{16,80},{32,96},{48,112},{64,0},{80,16},{96,32},{112,48},{1... | collective-permute-start | bytes 393224 | tf_op jit(solution)/shard_map/ppermute | solution.py:304
  96.4 14.0 %collective-permute-start.21 = (bf16[64,1024]{1,0:T(8,128)(2,1)S(1)}, bf16[64,1024]{1,0:T(8,128)(2,1)S(1)}, u32[]{:S(2)}, u32[]{:S(2)}) collective-permute-start(bf16[64,1024]{1,0:T(8,128)(2,1)S(1)} %get-tuple-element.22), channel_id=1, source_target_pairs={{0,32},{16,48},{32,64},{48,80},{64,96},{80,112},{96,0},{112,16},{1... | collective-permute-start | bytes 393224 | tf_op jit(solution)/shard_map/ppermute | solution.py:304
  97.8 12.6 %collective-permute-start.23 = (bf16[64,1024]{1,0:T(8,128)(2,1)S(1)}, bf16[64,1024]{1,0:T(8,128)(2,1)S(1)}, u32[]{:S(2)}, u32[]{:S(2)}) collective-permute-start(bf16[64,1024]{1,0:T(8,128)(2,1)S(1)} %get-tuple-element.23), channel_id=1, source_target_pairs={{0,96},{16,112},{32,0},{48,16},{64,32},{80,48},{96,64},{112,80},{1... | collective-permute-start | bytes 393224 | tf_op jit(solution)/shard_map/ppermute | solution.py:304
  99.7 10.7 %collective-permute-start.22 = (bf16[64,1024]{1,0:T(8,128)(2,1)S(1)}, bf16[64,1024]{1,0:T(8,128)(2,1)S(1)}, u32[]{:S(2)}, u32[]{:S(2)}) collective-permute-start(bf16[64,1024]{1,0:T(8,128)(2,1)S(1)} %get-tuple-element.24), channel_id=1, source_target_pairs={{0,64},{16,80},{32,96},{48,112},{64,0},{80,16},{96,32},{112,48},{1... | collective-permute-start | bytes 393224 | tf_op jit(solution)/shard_map/ppermute | solution.py:304
  103.9 9.5 %collective-permute-start.28 = (bf16[64,1024]{1,0:T(8,128)(2,1)S(1)}, bf16[64,1024]{1,0:T(8,128)(2,1)S(1)}, u32[]{:S(2)}, u32[]{:S(2)}) collective-permute-start(bf16[64,1024]{1,0:T(8,128)(2,1)S(1)} %add_convert_fusion.1), channel_id=1, source_target_pairs={{0,128},{16,144},{32,160},{48,176},{64,192},{80,208},{96,224},{112... | collective-permute-start | bytes 393224 | tf_op jit(solution)/shard_map/ppermute | solution.py:383
  (12 other events, 80.7 us)

commit v5 on v4

--- a/solution.py
+++ b/solution.py
@@ -86,16 +86,18 @@
     half = BLOCK // 2
     for step_y in range(YN):
         for step_z in range(ZN):
-            group, index = (0, 0) if step_z == 0 else (5, step_z - 1)
             block = ((y + YN - step_y) % YN) * ZN + (z + ZN - step_z) % ZN
             for part in range(2):
-                start = index * BLOCK + part * half
-                if step_y == 2:
-                    middle = half if step_z == 0 else 3 * half
-                    ref = pieces[group + (2 if start < middle else 3)]
-                    start %= middle
+                start = part * half
+                if step_z == 0:
+                    ref = pieces[step_y]
                 else:
-                    ref = pieces[group + {0: 0, 1: 1, 3: 4}[step_y]]
+                    start += (step_z - 1) * BLOCK
+                    if step_y == 2:
+                        ref = pieces[YN + (2 if start < 3 * half else 3)]
+                        start %= 3 * half
+                    else:
+                        ref = pieces[YN + {0: 0, 1: 1, 3: 4}[step_y]]
                 rows = pl.ds(pl.multiple_of(block * BLOCK + part * half, half), half)
                 same_ref[rows, :] = ref[start : start + half, :SAME]
                 beside_ref[rows, :] = ref[start : start + half, SAME:]
@@ -147,8 +149,8 @@
 
 
 def forward_beside_kernel(*refs):
-    x_pieces, w_pieces = refs[:2], refs[2:12]
-    same_ref, beside_ref, up_ref, down_ref, x_scr, w_scr, y_scr, sem = refs[13:]
+    x_pieces, w_pieces = refs[:2], refs[2:11]
+    same_ref, beside_ref, up_ref, down_ref, x_scr, w_scr, y_scr, sem = refs[12:]
     assemble_inputs(x_pieces, x_scr)
     assemble_weights(w_pieces, same_ref, w_scr)
     keep = pltpu.make_async_copy(w_scr, beside_ref, sem)
@@ -267,9 +269,9 @@
         transpose_kernel, "weights_transpose", (shape(BLOCK, COLS),), [], 0, [taps_first]
     )
     beside = [lax.ppermute(own, "slab", to_z(k)) for k in range(1, ZN)]
-    pieces = along_y(own)
+    pieces = [own] + [lax.ppermute(own, "slab", to_y(k)) for k in range(1, YN)]
     line = jnp.concatenate(beside, axis=0)
-    return pieces + along_y(once(line, pieces[2], pieces[3]))
+    return pieces + along_y(once(line, pieces[1], pieces[3]))
 
 
 def once(value, *others):
@@ -286,7 +288,7 @@
 
 
 def gather_inputs(inputs, w_pieces):
-    far = lax.ppermute(once(inputs, w_pieces[5]), "filt", TO_ZHI)
+    far = lax.ppermute(once(inputs, w_pieces[4], w_pieces[2]), "filt", TO_ZHI)
     pair = jnp.concatenate([inputs, far], axis=0)
     row = jnp.concatenate(
         [pair] + [lax.ppermute(pair, "filt", to_x(k)) for k in range(1, XN)], axis=0
@@ -312,7 +314,7 @@
     w_pieces = gather_weights(weights)
     x_pieces = gather_inputs(inputs.reshape(BLOCK, CELLS), w_pieces)
     (ready,) = call(
-        ready_kernel, "weights_ready", (shape(8, 128),), [], 7168, w_pieces[7:9], in_any=range(2)
+        ready_kernel, "weights_ready", (shape(8, 128),), [], 7168, w_pieces[6:8], in_any=range(2)
     )
     same_taps, beside_taps, up, down = call(
         forward_beside_kernel,
@@ -331,7 +333,7 @@
         ],
         BESIDE,
         x_pieces + w_pieces + [ready],
-        in_any=(12,),
+        in_any=(11,),
         out_any=(1,),
         limit=46,
     )

time: 116 us -> 114 us (0.983)
  waiting for transfers between devices: 32.7 us -> 31.1 us
    ppermute x1 -> x4, starting transfers between devices: 6.12 us -> 11.3 us  [the longest x1 6.11 us: gather_inputs(): far = lax.ppermute(once(inputs, w_pieces[4], w_pieces[2]), 'filt', TO_ZHI)]
    ppermute x2 -> x1, starting transfers between devices: 4.06 us -> 0.53 us  [along_y(): after = lax.ppermute(line, 'slab', to_y(-1))]
    ppermute x2 -> x1, starting transfers between devices: 4.4 us -> 1.89 us  [along_y(): second = lax.ppermute(after[half:], 'slab', to_y(-1))]
    ppermute x3, waiting for transfers between devices: 15.5 us -> 13.1 us  [gather_weights(): beside = [lax.ppermute(own, 'slab', to_z(k)) for k in range(1, ZN)]]
    ppermute x2 -> x1, starting transfers between devices: 0.31 us -> 1.58 us  [along_y(): before = lax.ppermute(line, 'slab', to_y(1))]
    ppermute x2 -> x1, waiting for transfers between devices: 3.55 us -> 2.76 us  [along_y(): first = lax.ppermute(before[:half], 'slab', to_y(1))]
    ppermute x1 -> x4, waiting for transfers between devices: 4.01 us -> 4.35 us  [the longest x1 4.35 us: gather_inputs(): far = lax.ppermute(once(inputs, w_pieces[4], w_pieces[2]), 'filt', TO_ZHI)]
  transfers between devices with their start and end apart: 29 -> 28, of which waited for: 9 -> 9; matrix products, arithmetic and copies ran while one was open for 1% -> 1% of each run, Pallas kernels for 6% -> 6%
where the time goes in v5:
time: 114 us; the launch traced here: 113 us
  starting transfers between devices  60.7 us (53%)
  waiting for transfers between devices  31.1 us (27%)
  Pallas kernels  16.2 us (14%)
  local copies, waits for them, and re-layouts  2.56 us (2%)
  other arithmetic  1.18 us (1%)
    pallas_call x8, Pallas kernels, call(): pl.pallas_call(kernel, out_shape=outs, in_specs=[ANY if at in in_any else...  16.2 us
    ppermute x3, waiting for transfers between devices, gather_weights(): beside = [lax.ppermute(own, 'slab', to_z(k)) for k in range(1, ZN)]  13.1 us
    ppermute x6, starting transfers between devices, sum_over_row(): arrived = [lax.ppermute(sums[k], 'filt', to_x(k)) for k in range(1, XN)]  8.95 us
    ppermute x3, starting transfers between devices, gather_inputs(): lax.ppermute(pair, 'filt', to_x(k))  6.42 us
    ppermute x1, starting transfers between devices, local(): arrived = lax.ppermute(far.astype(BF16), 'filt', TO_ZHI)  6.32 us
    ppermute x1, starting transfers between devices, local(): grad_above = lax.ppermute(grad, 'slab', DOWN)  6.23 us
    ppermute x1, starting transfers between devices, gather_inputs(): far = lax.ppermute(once(inputs, w_pieces[4], w_pieces[2]), 'filt', TO_ZHI)  6.11 us
    ppermute x3, starting transfers between devices, gather_weights(): beside = [lax.ppermute(own, 'slab', to_z(k)) for k in range(1, ZN)]  5.37 us
  transfers between devices with their start and end apart: 28, of which 9 were waited for; matrix products, arithmetic and copies ran while one was open for 1% of the time, Pallas kernels for 6%

profile of v5, /device:TPU:8, one launch (start us, length us, event | category | flops | bytes accessed | tf_op | source)
XLA Modules:
  0.0 112.7 jit_solution(14410129876364459186)
XLA Ops:
  1.8 4.7 %collective-permute-start.2 = (bf16[64,1792]{1,0:T(8,128)(2,1)S(1)}, bf16[64,1792]{1,0:T(8,128)(2,1)S(1)}, u32[]{:S(2)}, u32[]{:S(2)}) collective-permute-start(bf16[64,1792]{1,0:T(8,128)(2,1)S(1)} %weights_transpose.1.refs_2_), channel_id=1, source_target_pairs={{0,3},{1,0},{2,1},{3,2},{4,7},{5,4},{6,5},{7,6},{8,11},{9,8},{10,9... | collective-permute-start | bytes 688136 | tf_op jit(solution)/shard_map/ppermute | solution.py:271
  7.2 2.3 %collective-permute-start.5 = (bf16[64,1792]{1,0:T(8,128)(2,1)S(1)}, bf16[64,1792]{1,0:T(8,128)(2,1)S(1)}, u32[]{:S(2)}, u32[]{:S(2)}) collective-permute-start(bf16[64,1792]{1,0:T(8,128)(2,1)S(1)} %weights_transpose.1.refs_2_), channel_id=1, source_target_pairs={{0,8},{1,9},{2,10},{3,11},{4,12},{5,13},{6,14},{7,15},{8,0},{9,1},... | collective-permute-start | bytes 688136 | tf_op jit(solution)/shard_map/ppermute | solution.py:272
  10.9 1.7 %collective-permute-done.2 = bf16[64,1792]{1,0:T(8,128)(2,1)S(1)} collective-permute-done((bf16[64,1792]{1,0:T(8,128)(2,1)S(1)}, bf16[64,1792]{1,0:T(8,128)(2,1)S(1)}, u32[]{:S(2)}, u32[]{:S(2)}) %collective-permute-start.2) | collective-permute-done | bytes 229408 | tf_op jit(solution)/shard_map/ppermute | solution.py:271
  14.2 11.4 %collective-permute-done.1 = bf16[64,1792]{1,0:T(8,128)(2,1)S(1)} collective-permute-done((bf16[64,1792]{1,0:T(8,128)(2,1)S(1)}, bf16[64,1792]{1,0:T(8,128)(2,1)S(1)}, u32[]{:S(2)}, u32[]{:S(2)}) %collective-permute-start.1) | collective-permute-done | bytes 229408 | tf_op jit(solution)/shard_map/ppermute | solution.py:271
  27.7 6.1 %collective-permute-start.6 = (bf16[64,1024]{1,0:T(8,128)(2,1)S(1)}, bf16[64,1024]{1,0:T(8,128)(2,1)S(1)}, u32[]{:S(2)}, u32[]{:S(2)}) collective-permute-start(bf16[64,1024]{1,0:T(8,128)(2,1)S(1)} %bitcast.12), channel_id=1, source_target_pairs={{0,128},{16,144},{32,160},{48,176},{64,192},{80,208},{96,224},{112... | collective-permute-start | bytes 393224 | tf_op jit(solution)/shard_map/ppermute | solution.py:291
  33.8 4.3 %collective-permute-done.6 = bf16[64,1024]{1,0:T(8,128)(2,1)S(1)} collective-permute-done((bf16[64,1024]{1,0:T(8,128)(2,1)S(1)}, bf16[64,1024]{1,0:T(8,128)(2,1)S(1)}, u32[]{:S(2)}, u32[]{:S(2)}) %collective-permute-start.6) | collective-permute-done | bytes 131104 | tf_op jit(solution)/shard_map/ppermute | solution.py:291
  38.2 3.1 %collective-permute-start.8 = (bf16[128,1024]{1,0:T(8,128)(2,1)S(1)}, bf16[128,1024]{1,0:T(8,128)(2,1)S(1)}, u32[]{:S(2)}, u32[]{:S(2)}) collective-permute-start(bf16[128,1024]{1,0:T(8,128)(2,1)S(1)} %pad_maximum_fusion.1), channel_id=1, source_target_pairs={{0,64},{16,80},{32,96},{48,112},{64,0},{80,16},{96,32},{112,48},{1... | collective-permute-start | bytes 786440 | tf_op jit(solution)/shard_map/ppermute | solution.py:294
  41.9 2.7 %collective-permute-start.9 = (bf16[128,1024]{1,0:T(8,128)(2,1)S(1)}, bf16[128,1024]{1,0:T(8,128)(2,1)S(1)}, u32[]{:S(2)}, u32[]{:S(2)}) collective-permute-start(bf16[128,1024]{1,0:T(8,128)(2,1)S(1)} %pad_maximum_fusion.1), channel_id=1, source_target_pairs={{0,96},{16,112},{32,0},{48,16},{64,32},{80,48},{96,64},{112,80},{1... | collective-permute-start | bytes 786440 | tf_op jit(solution)/shard_map/ppermute | solution.py:294
  44.7 1.9 %collective-permute-start.14 = (bf16[96,1792]{1,0:T(8,128)(2,1)S(1)}, bf16[96,1792]{1,0:T(8,128)(2,1)S(1)}, u32[]{:S(2)}, u32[]{:S(2)}) collective-permute-start(bf16[96,1792]{1,0:T(8,128)(2,1)S(1)} %slice.81), channel_id=1, source_target_pairs={{0,12},{1,13},{2,14},{3,15},{4,0},{5,1},{6,2},{7,3},{8,4},{9,5},{1... | collective-permute-start | bytes 1032200 | tf_op jit(solution)/shard_map/ppermute | solution.py:286
  46.9 2.9 %collective-permute-done.7 = bf16[128,1024]{1,0:T(8,128)(2,1)S(1)} collective-permute-done((bf16[128,1024]{1,0:T(8,128)(2,1)S(1)}, bf16[128,1024]{1,0:T(8,128)(2,1)S(1)}, u32[]{:S(2)}, u32[]{:S(2)}) %collective-permute-start.7) | collective-permute-done | bytes 262176 | tf_op jit(solution)/shard_map/ppermute | solution.py:294
  50.2 1.8 %collective-permute-done.14.refs_1_.refs_9_ = bf16[96,1792]{1,0:T(8,128)(2,1)S(1)} collective-permute-done((bf16[96,1792]{1,0:T(8,128)(2,1)S(1)}, bf16[96,1792]{1,0:T(8,128)(2,1)S(1)}, u32[]{:S(2)}, u32[]{:S(2)}) %collective-permute-start.14) | collective-permute-done | bytes 344096 | tf_op jit(solution)/shard_map/ppermute | solution.py:286
  52.0 2.8 %collective-permute-done.12.refs_0_.refs_8_ = bf16[96,1792]{1,0:T(8,128)(2,1)S(1)} collective-permute-done((bf16[96,1792]{1,0:T(8,128)(2,1)S(1)}, bf16[96,1792]{1,0:T(8,128)(2,1)S(1)}, u32[]{:S(2)}, u32[]{:S(2)}) %collective-permute-start.12) | collective-permute-done | bytes 344096 | tf_op jit(solution)/shard_map/ppermute | solution.py:285
  54.8 5.1 %forward_beside.1 = (bf16[1024,640]{1,0:T(8,128)(2,1)S(1)}, bf16[1024,1152]{1,0:T(8,128)(2,1)}, bf16[64,1024]{1,0:T(8,128)(2,1)S(1)}, bf16[64,1024]{1,0:T(8,128)(2,1)S(1)}) custom-call(bf16[512,1024]{1,0:T(8,128)(2,1)S(1)} %constant_dynamic-update-slice_fusion.refs_0_.first_ref, bf16[512,1024]{1,0:T(8,128)(2,1)S(1)} %collective-permute-done.10.refs_1_.second_ref, ...), custom_call_target="tpu_custom_call" | custom-call | flops 2415919104 | bytes 1048576 | tf_op jit(solution)/shard_map/forward_beside/pallas_call | solution.py:254
  59.9 3.2 %collective-permute-start.15 = (bf16[64,1024]{1,0:T(8,128)(2,1)S(1)}, bf16[64,1024]{1,0:T(8,128)(2,1)S(1)}, u32[]{:S(2)}, u32[]{:S(2)}) collective-permute-start(bf16[64,1024]{1,0:T(8,128)(2,1)S(1)} %get-tuple-element.15), channel_id=1, source_target_pairs={{0,1},{1,2},{2,3},{3,4},{4,5},{5,6},{6,7},{7,8},{8,9},{9,10},{10,1... | collective-permute-start | bytes 393224 | tf_op jit(solution)/shard_map/ppermute | solution.py:340
  63.1 5.4 %collective-permute-start.16 = (bf16[64,1024]{1,0:T(8,128)(2,1)S(1)}, bf16[64,1024]{1,0:T(8,128)(2,1)S(1)}, u32[]{:S(2)}, u32[]{:S(2)}) collective-permute-start(bf16[64,1024]{1,0:T(8,128)(2,1)S(1)} %get-tuple-element.16), channel_id=1, source_target_pairs={{1,0},{2,1},{3,2},{4,3},{5,4},{6,5},{7,6},{8,7},{9,8},{10,9},{11,1... | collective-permute-start | bytes 393224 | tf_op jit(solution)/shard_map/ppermute | solution.py:341
  69.8 3.1 %forward_same.1.own_ref = f32[64,1024]{1,0:T(8,128)S(1)} custom-call(bf16[512,1024]{1,0:T(8,128)(2,1)S(1)} %constant_dynamic-update-slice_fusion.refs_0_.first_ref, bf16[512,1024]{1,0:T(8,128)(2,1)S(1)} %copy-done.4, bf16[1024,640]{1,0:T(8,128)(2,1)S(1)} %get-tuple-element.14.same_ref.w_ref), custom_call_target="tpu_custom_call" | custom-call | flops 1342177280 | bytes 1048576 | tf_op jit(solution)/shard_map/forward_same/pallas_call | solution.py:254
  73.7 2.3 %collective-permute-start.18 = (bf16[64,1024]{1,0:T(8,128)(2,1)S(1)}, bf16[64,1024]{1,0:T(8,128)(2,1)S(1)}, u32[]{:S(2)}, u32[]{:S(2)}) collective-permute-start(bf16[64,1024]{1,0:T(8,128)(2,1)S(1)} %get-tuple-element.18.grad_ref), channel_id=1, source_target_pairs={{0,1},{1,2},{2,3},{3,4},{4,5},{5,6},{6,7},{7,8},{8,9},{9,10},{10,1... | collective-permute-start | bytes 393224 | tf_op jit(solution)/shard_map/ppermute | solution.py:358
  76.0 6.2 %collective-permute-start.17 = (bf16[64,1024]{1,0:T(8,128)(2,1)S(1)}, bf16[64,1024]{1,0:T(8,128)(2,1)S(1)}, u32[]{:S(2)}, u32[]{:S(2)}) collective-permute-start(bf16[64,1024]{1,0:T(8,128)(2,1)S(1)} %get-tuple-element.18.grad_ref), channel_id=1, source_target_pairs={{1,0},{2,1},{3,2},{4,3},{5,4},{6,5},{7,6},{8,7},{9,8},{10,9},{11,1... | collective-permute-start | bytes 393224 | tf_op jit(solution)/shard_map/ppermute | solution.py:359
  82.3 2.5 %backward_same.1.same_ref = f32[1024,1024]{1,0:T(8,128)S(1)} custom-call(bf16[64,1024]{1,0:T(8,128)(2,1)S(1)} %get-tuple-element.18.grad_ref, bf16[1024,640]{1,0:T(8,128)(2,1)S(1)} %get-tuple-element.14.same_ref.w_ref), custom_call_target="tpu_custom_call" | custom-call | flops 1342177280 | bytes 1048576 | tf_op jit(solution)/shard_map/backward_same/pallas_call | solution.py:254
  85.0 3.0 %backward_far.1 = (bf16[512,1024]{1,0:T(8,128)(2,1)S(1)}, bf16[1152,1024]{1,0:T(8,128)(2,1)S(1)}) custom-call(bf16[64,1024]{1,0:T(8,128)(2,1)S(1)} %collective-permute-done.17.above_ref, bf16[64,1024]{1,0:T(8,128)(2,1)S(1)} %collective-permute-done.18.below_ref, f32[1024,1024]{1,0:T(8,128)S(1)} %backward_same.1.same_ref, bf16[1024,1152]{1,0:T(8,128)(2,1)S(1)} %copy-done), custom_call_target="tpu_custom_call" | custom-call | flops 1207959552 | bytes 1048576 | tf_op jit(solution)/shard_map/backward_far/pallas_call | solution.py:254
  96.3 1.9 %collective-permute-start.22 = (bf16[64,1024]{1,0:T(8,128)(2,1)S(1)}, bf16[64,1024]{1,0:T(8,128)(2,1)S(1)}, u32[]{:S(2)}, u32[]{:S(2)}) collective-permute-start(bf16[64,1024]{1,0:T(8,128)(2,1)S(1)} %get-tuple-element.23), channel_id=1, source_target_pairs={{0,96},{16,112},{32,0},{48,16},{64,32},{80,48},{96,64},{112,80},{1... | collective-permute-start | bytes 393224 | tf_op jit(solution)/shard_map/ppermute | solution.py:306
  99.5 2.2 %collective-permute-done.25 = bf16[64,1024]{1,0:T(8,128)(2,1)S(1)} collective-permute-done((bf16[64,1024]{1,0:T(8,128)(2,1)S(1)}, bf16[64,1024]{1,0:T(8,128)(2,1)S(1)}, u32[]{:S(2)}, u32[]{:S(2)}) %collective-permute-start.25) | collective-permute-done | bytes 131104 | tf_op jit(solution)/shard_map/ppermute | solution.py:306
  101.8 6.3 %collective-permute-start.27 = (bf16[64,1024]{1,0:T(8,128)(2,1)S(1)}, bf16[64,1024]{1,0:T(8,128)(2,1)S(1)}, u32[]{:S(2)}, u32[]{:S(2)}) collective-permute-start(bf16[64,1024]{1,0:T(8,128)(2,1)S(1)} %add_convert_fusion.1), channel_id=1, source_target_pairs={{0,128},{16,144},{32,160},{48,176},{64,192},{80,208},{96,224},{112... | collective-permute-start | bytes 393224 | tf_op jit(solution)/shard_map/ppermute | solution.py:385
  108.2 3.7 %collective-permute-done.27 = bf16[64,1024]{1,0:T(8,128)(2,1)S(1)} collective-permute-done((bf16[64,1024]{1,0:T(8,128)(2,1)S(1)}, bf16[64,1024]{1,0:T(8,128)(2,1)S(1)}, u32[]{:S(2)}, u32[]{:S(2)}) %collective-permute-start.27) | collective-permute-done | bytes 131104 | tf_op jit(solution)/shard_map/ppermute | solution.py:385
  (70 shorter events, 21.1 us)
Async XLA Ops:
  1.8 10.8 %collective-permute-start.2 = (bf16[64,1792]{1,0:T(8,128)(2,1)S(1)}, bf16[64,1792]{1,0:T(8,128)(2,1)S(1)}, u32[]{:S(2)}, u32[]{:S(2)}) collective-permute-start(bf16[64,1792]{1,0:T(8,128)(2,1)S(1)} %weights_transpose.1.refs_2_), channel_id=1, source_target_pairs={{0,3},{1,0},{2,1},{3,2},{4,7},{5,4},{6,5},{7,6},{8,11},{9,8},{10,9... | collective-permute-start | bytes 688136 | tf_op jit(solution)/shard_map/ppermute | solution.py:271
  6.5 19.0 %collective-permute-start.1 = (bf16[64,1792]{1,0:T(8,128)(2,1)S(1)}, bf16[64,1792]{1,0:T(8,128)(2,1)S(1)}, u32[]{:S(2)}, u32[]{:S(2)}) collective-permute-start(bf16[64,1792]{1,0:T(8,128)(2,1)S(1)} %weights_transpose.1.refs_2_), channel_id=1, source_target_pairs={{0,2},{1,3},{2,0},{3,1},{4,6},{5,7},{6,4},{7,5},{8,10},{9,11},{10,... | collective-permute-start | bytes 688136 | tf_op jit(solution)/shard_map/ppermute | solution.py:271
  6.5 19.0 %collective-permute-start = (bf16[64,1792]{1,0:T(8,128)(2,1)S(1)}, bf16[64,1792]{1,0:T(8,128)(2,1)S(1)}, u32[]{:S(2)}, u32[]{:S(2)}) collective-permute-start(bf16[64,1792]{1,0:T(8,128)(2,1)S(1)} %weights_transpose.1.refs_2_), channel_id=1, source_target_pairs={{0,1},{1,2},{2,3},{3,0},{4,5},{5,6},{6,7},{7,4},{8,9},{9,10},{10,1... | collective-permute-start | bytes 688136 | tf_op jit(solution)/shard_map/ppermute | solution.py:271
  7.2 20.5 %collective-permute-start.5 = (bf16[64,1792]{1,0:T(8,128)(2,1)S(1)}, bf16[64,1792]{1,0:T(8,128)(2,1)S(1)}, u32[]{:S(2)}, u32[]{:S(2)}) collective-permute-start(bf16[64,1792]{1,0:T(8,128)(2,1)S(1)} %weights_transpose.1.refs_2_), channel_id=1, source_target_pairs={{0,8},{1,9},{2,10},{3,11},{4,12},{5,13},{6,14},{7,15},{8,0},{9,1},... | collective-permute-start | bytes 688136 | tf_op jit(solution)/shard_map/ppermute | solution.py:272
  9.5 16.1 %collective-permute-start.4 = (bf16[64,1792]{1,0:T(8,128)(2,1)S(1)}, bf16[64,1792]{1,0:T(8,128)(2,1)S(1)}, u32[]{:S(2)}, u32[]{:S(2)}) collective-permute-start(bf16[64,1792]{1,0:T(8,128)(2,1)S(1)} %weights_transpose.1.refs_2_), channel_id=1, source_target_pairs={{0,12},{1,13},{2,14},{3,15},{4,0},{5,1},{6,2},{7,3},{8,4},{9,5},{1... | collective-permute-start | bytes 688136 | tf_op jit(solution)/shard_map/ppermute | solution.py:272
  12.6 13.0 %collective-permute-start.3 = (bf16[64,1792]{1,0:T(8,128)(2,1)S(1)}, bf16[64,1792]{1,0:T(8,128)(2,1)S(1)}, u32[]{:S(2)}, u32[]{:S(2)}) collective-permute-start(bf16[64,1792]{1,0:T(8,128)(2,1)S(1)} %weights_transpose.1.refs_2_), channel_id=1, source_target_pairs={{0,4},{1,5},{2,6},{3,7},{4,8},{5,9},{6,10},{7,11},{8,12},{9,13},{1... | collective-permute-start | bytes 688136 | tf_op jit(solution)/shard_map/ppermute | solution.py:272
  25.6 19.0 %collective-permute-start.13 = (bf16[192,1792]{1,0:T(8,128)(2,1)S(1)}, bf16[192,1792]{1,0:T(8,128)(2,1)S(1)}, u32[]{:S(2)}, u32[]{:S(2)}) collective-permute-start(bf16[192,1792]{1,0:T(8,128)(2,1)S(1)} %pad_maximum_fusion.refs_6_), channel_id=1, source_target_pairs={{0,12},{1,13},{2,14},{3,15},{4,0},{5,1},{6,2},{7,3},{8,4},{9,5},{1... | collective-permute-start | bytes 2064392 | tf_op jit(solution)/shard_map/ppermute | solution.py:284
  26.1 20.4 %collective-permute-start.11 = (bf16[192,1792]{1,0:T(8,128)(2,1)S(1)}, bf16[192,1792]{1,0:T(8,128)(2,1)S(1)}, u32[]{:S(2)}, u32[]{:S(2)}) collective-permute-start(bf16[192,1792]{1,0:T(8,128)(2,1)S(1)} %pad_maximum_fusion.refs_6_), channel_id=1, source_target_pairs={{0,4},{1,5},{2,6},{3,7},{4,8},{5,9},{6,10},{7,11},{8,12},{9,13},{1... | collective-permute-start | bytes 2064392 | tf_op jit(solution)/shard_map/ppermute | solution.py:283
  27.7 10.5 %collective-permute-start.6 = (bf16[64,1024]{1,0:T(8,128)(2,1)S(1)}, bf16[64,1024]{1,0:T(8,128)(2,1)S(1)}, u32[]{:S(2)}, u32[]{:S(2)}) collective-permute-start(bf16[64,1024]{1,0:T(8,128)(2,1)S(1)} %bitcast.12), channel_id=1, source_target_pairs={{0,128},{16,144},{32,160},{48,176},{64,192},{80,208},{96,224},{112... | collective-permute-start | bytes 393224 | tf_op jit(solution)/shard_map/ppermute | solution.py:291
  38.2 11.6 %collective-permute-start.8 = (bf16[128,1024]{1,0:T(8,128)(2,1)S(1)}, bf16[128,1024]{1,0:T(8,128)(2,1)S(1)}, u32[]{:S(2)}, u32[]{:S(2)}) collective-permute-start(bf16[128,1024]{1,0:T(8,128)(2,1)S(1)} %pad_maximum_fusion.1), channel_id=1, source_target_pairs={{0,64},{16,80},{32,96},{48,112},{64,0},{80,16},{96,32},{112,48},{1... | collective-permute-start | bytes 786440 | tf_op jit(solution)/shard_map/ppermute | solution.py:294
  41.3 8.5 %collective-permute-start.7 = (bf16[128,1024]{1,0:T(8,128)(2,1)S(1)}, bf16[128,1024]{1,0:T(8,128)(2,1)S(1)}, u32[]{:S(2)}, u32[]{:S(2)}) collective-permute-start(bf16[128,1024]{1,0:T(8,128)(2,1)S(1)} %pad_maximum_fusion.1), channel_id=1, source_target_pairs={{0,32},{16,48},{32,64},{48,80},{64,96},{80,112},{96,0},{112,16},{1... | collective-permute-start | bytes 786440 | tf_op jit(solution)/shard_map/ppermute | solution.py:294
  41.9 8.0 %collective-permute-start.9 = (bf16[128,1024]{1,0:T(8,128)(2,1)S(1)}, bf16[128,1024]{1,0:T(8,128)(2,1)S(1)}, u32[]{:S(2)}, u32[]{:S(2)}) collective-permute-start(bf16[128,1024]{1,0:T(8,128)(2,1)S(1)} %pad_maximum_fusion.1), channel_id=1, source_target_pairs={{0,96},{16,112},{32,0},{48,16},{64,32},{80,48},{96,64},{112,80},{1... | collective-permute-start | bytes 786440 | tf_op jit(solution)/shard_map/ppermute | solution.py:294
  46.6 8.2 %collective-permute-start.12 = (bf16[96,1792]{1,0:T(8,128)(2,1)S(1)}, bf16[96,1792]{1,0:T(8,128)(2,1)S(1)}, u32[]{:S(2)}, u32[]{:S(2)}) collective-permute-start(bf16[96,1792]{1,0:T(8,128)(2,1)S(1)} %slice.80), channel_id=1, source_target_pairs={{0,4},{1,5},{2,6},{3,7},{4,8},{5,9},{6,10},{7,11},{8,12},{9,13},{1... | collective-permute-start | bytes 1032200 | tf_op jit(solution)/shard_map/ppermute | solution.py:285
  59.9 13.0 %collective-permute-start.15 = (bf16[64,1024]{1,0:T(8,128)(2,1)S(1)}, bf16[64,1024]{1,0:T(8,128)(2,1)S(1)}, u32[]{:S(2)}, u32[]{:S(2)}) collective-permute-start(bf16[64,1024]{1,0:T(8,128)(2,1)S(1)} %get-tuple-element.15), channel_id=1, source_target_pairs={{0,1},{1,2},{2,3},{3,4},{4,5},{5,6},{6,7},{7,8},{8,9},{9,10},{10,1... | collective-permute-start | bytes 393224 | tf_op jit(solution)/shard_map/ppermute | solution.py:340
  63.1 9.8 %collective-permute-start.16 = (bf16[64,1024]{1,0:T(8,128)(2,1)S(1)}, bf16[64,1024]{1,0:T(8,128)(2,1)S(1)}, u32[]{:S(2)}, u32[]{:S(2)}) collective-permute-start(bf16[64,1024]{1,0:T(8,128)(2,1)S(1)} %get-tuple-element.16), channel_id=1, source_target_pairs={{1,0},{2,1},{3,2},{4,3},{5,4},{6,5},{7,6},{8,7},{9,8},{10,9},{11,1... | collective-permute-start | bytes 393224 | tf_op jit(solution)/shard_map/ppermute | solution.py:341
  73.7 11.1 %collective-permute-start.18 = (bf16[64,1024]{1,0:T(8,128)(2,1)S(1)}, bf16[64,1024]{1,0:T(8,128)(2,1)S(1)}, u32[]{:S(2)}, u32[]{:S(2)}) collective-permute-start(bf16[64,1024]{1,0:T(8,128)(2,1)S(1)} %get-tuple-element.18.grad_ref), channel_id=1, source_target_pairs={{0,1},{1,2},{2,3},{3,4},{4,5},{5,6},{6,7},{7,8},{8,9},{9,10},{10,1... | collective-permute-start | bytes 393224 | tf_op jit(solution)/shard_map/ppermute | solution.py:358
  76.0 8.9 %collective-permute-start.17 = (bf16[64,1024]{1,0:T(8,128)(2,1)S(1)}, bf16[64,1024]{1,0:T(8,128)(2,1)S(1)}, u32[]{:S(2)}, u32[]{:S(2)}) collective-permute-start(bf16[64,1024]{1,0:T(8,128)(2,1)S(1)} %get-tuple-element.18.grad_ref), channel_id=1, source_target_pairs={{1,0},{2,1},{3,2},{4,3},{5,4},{6,5},{7,6},{8,7},{9,8},{10,9},{11,1... | collective-permute-start | bytes 393224 | tf_op jit(solution)/shard_map/ppermute | solution.py:359
  90.4 7.7 %collective-permute-start.24 = (bf16[64,1024]{1,0:T(8,128)(2,1)S(1)}, bf16[64,1024]{1,0:T(8,128)(2,1)S(1)}, u32[]{:S(2)}, u32[]{:S(2)}) collective-permute-start(bf16[64,1024]{1,0:T(8,128)(2,1)S(1)} %get-tuple-element.25), channel_id=1, source_target_pairs={{0,32},{16,48},{32,64},{48,80},{64,96},{80,112},{96,0},{112,16},{1... | collective-permute-start | bytes 393224 | tf_op jit(solution)/shard_map/ppermute | solution.py:306
  92.1 7.5 %collective-permute-start.26 = (bf16[64,1024]{1,0:T(8,128)(2,1)S(1)}, bf16[64,1024]{1,0:T(8,128)(2,1)S(1)}, u32[]{:S(2)}, u32[]{:S(2)}) collective-permute-start(bf16[64,1024]{1,0:T(8,128)(2,1)S(1)} %get-tuple-element.26), channel_id=1, source_target_pairs={{0,96},{16,112},{32,0},{48,16},{64,32},{80,48},{96,64},{112,80},{1... | collective-permute-start | bytes 393224 | tf_op jit(solution)/shard_map/ppermute | solution.py:306
  93.7 8.0 %collective-permute-start.25 = (bf16[64,1024]{1,0:T(8,128)(2,1)S(1)}, bf16[64,1024]{1,0:T(8,128)(2,1)S(1)}, u32[]{:S(2)}, u32[]{:S(2)}) collective-permute-start(bf16[64,1024]{1,0:T(8,128)(2,1)S(1)} %get-tuple-element.27), channel_id=1, source_target_pairs={{0,64},{16,80},{32,96},{48,112},{64,0},{80,16},{96,32},{112,48},{1... | collective-permute-start | bytes 393224 | tf_op jit(solution)/shard_map/ppermute | solution.py:306
  94.8 13.3 %collective-permute-start.20 = (bf16[64,1024]{1,0:T(8,128)(2,1)S(1)}, bf16[64,1024]{1,0:T(8,128)(2,1)S(1)}, u32[]{:S(2)}, u32[]{:S(2)}) collective-permute-start(bf16[64,1024]{1,0:T(8,128)(2,1)S(1)} %get-tuple-element.22), channel_id=1, source_target_pairs={{0,32},{16,48},{32,64},{48,80},{64,96},{80,112},{96,0},{112,16},{1... | collective-permute-start | bytes 393224 | tf_op jit(solution)/shard_map/ppermute | solution.py:306
  96.3 11.9 %collective-permute-start.22 = (bf16[64,1024]{1,0:T(8,128)(2,1)S(1)}, bf16[64,1024]{1,0:T(8,128)(2,1)S(1)}, u32[]{:S(2)}, u32[]{:S(2)}) collective-permute-start(bf16[64,1024]{1,0:T(8,128)(2,1)S(1)} %get-tuple-element.23), channel_id=1, source_target_pairs={{0,96},{16,112},{32,0},{48,16},{64,32},{80,48},{96,64},{112,80},{1... | collective-permute-start | bytes 393224 | tf_op jit(solution)/shard_map/ppermute | solution.py:306
  98.1 10.0 %collective-permute-start.21 = (bf16[64,1024]{1,0:T(8,128)(2,1)S(1)}, bf16[64,1024]{1,0:T(8,128)(2,1)S(1)}, u32[]{:S(2)}, u32[]{:S(2)}) collective-permute-start(bf16[64,1024]{1,0:T(8,128)(2,1)S(1)} %get-tuple-element.24), channel_id=1, source_target_pairs={{0,64},{16,80},{32,96},{48,112},{64,0},{80,16},{96,32},{112,48},{1... | collective-permute-start | bytes 393224 | tf_op jit(solution)/shard_map/ppermute | solution.py:306
  101.8 10.1 %collective-permute-start.27 = (bf16[64,1024]{1,0:T(8,128)(2,1)S(1)}, bf16[64,1024]{1,0:T(8,128)(2,1)S(1)}, u32[]{:S(2)}, u32[]{:S(2)}) collective-permute-start(bf16[64,1024]{1,0:T(8,128)(2,1)S(1)} %add_convert_fusion.1), channel_id=1, source_target_pairs={{0,128},{16,144},{32,160},{48,176},{64,192},{80,208},{96,224},{112... | collective-permute-start | bytes 393224 | tf_op jit(solution)/shard_map/ppermute | solution.py:385
  (11 other events, 72.3 us)
